TPU v7x, 32 devices: a whole 2x2x4 slice. The times are simulated.
32 devices in a mesh: node: 16 (over z, y, x), state: 2 (over core).
Axes of the slice: x: 2, y: 2, z: 4, core: 2. Of those that a mesh axis runs over, the one named last changes fastest.
Arguments:
- wavefunctions: float32 [16384, 8192], P('node', 'state'), may hold values from -0.53033006 to 0.53033006
- h_wavefunctions: float32 [16384, 8192], P('node', 'state'), may hold values from -0.53033006 to 0.53033006
- block_ids: int32 [4], replicated, may hold values from 0 to 63, as said below
Outputs:
- correlation: float32 [8192, 512], P(('state', 'node'))
- projected: float32 [8192, 512], P(('state', 'node'))
Inputs may be any that keep to these rules, and one draw needn't show every extreme that they name: `block_ids`: the 4 block numbers are distinct, and among them are always the first and the last block.
All inputs are finite; a program needn't handle non-finite values.
Results may differ from a plain program's by a relative error of at most 0.0001.
Values sent between devices are 32-bit elements; how exact they have to be, the bound alone decides.
No kernel may reach another device: no remote copies, remote signals or barrier semaphores. Data moves between devices by JAX's collectives and lax.ppermute only.
A program may use at most 192 MiB of HBM per device.

v0:
```python
import jax
import jax.numpy as jnp
from jax import lax
from jax.sharding import PartitionSpec as P

BLOCK = 128
NBLK = 4


def from_root(value, axis, source):
    kept = jnp.where(lax.axis_index(axis) == source, value, 0).astype(value.dtype)
    return lax.psum(kept, axis)


def body(wavefunctions, h_wavefunctions, block_ids):
    local_states = wavefunctions.shape[1]
    node_count = lax.axis_size("node")
    share_rows = local_states // node_count
    correlation_cols = []
    energy_cols = []
    for step in range(NBLK):
        first = block_ids[step] * BLOCK
        owner = first // local_states
        offset = first - owner * local_states
        psi_block = lax.dynamic_slice_in_dim(wavefunctions, offset, BLOCK, 1)
        hpsi_block = lax.dynamic_slice_in_dim(h_wavefunctions, offset, BLOCK, 1)
        psi_block, hpsi_block = (
            from_root(psi_block, "state", owner),
            from_root(hpsi_block, "state", owner),
        )
        correlation_full = jnp.dot(
            wavefunctions.T,
            psi_block,
            preferred_element_type=jnp.float32,
            precision=lax.Precision.HIGHEST,
        )
        energy_full = jnp.dot(
            wavefunctions.T,
            hpsi_block,
            preferred_element_type=jnp.float32,
            precision=lax.Precision.HIGHEST,
        )
        correlation_full, energy_full = lax.psum((correlation_full, energy_full), "node")
        row_start = lax.axis_index("node") * share_rows
        correlation_mine = lax.dynamic_slice_in_dim(correlation_full, row_start, share_rows, 0)
        energy_mine = lax.dynamic_slice_in_dim(energy_full, row_start, share_rows, 0)
        correlation_cols.append(correlation_mine)
        energy_cols.append(energy_mine)
    return (jnp.concatenate(correlation_cols, axis=1), jnp.concatenate(energy_cols, axis=1))


def solution(mesh):
    placed = (P("node", "state"), P("node", "state"), P())
    return jax.shard_map(
        body,
        mesh=mesh,
        in_specs=placed,
        out_specs=(P(("state", "node"), None), P(("state", "node"), None)),
        check_vma=False,
    )
```

profile of v0, /device:TPU:0, one launch (start us, length us, event | category | flops | bytes accessed | tf_op | source)
XLA Modules:
  0.0 619.8 jit_solution(17973891120407697768)
XLA Ops:
  7.2 0.0 all-reduce.7.cloned.1.call-start
  7.2 1.5 fusion
  11.3 4.3 dynamic-slice_select_fusion.3
  15.6 0.0 all-reduce.7.cloned.1.call-update
  15.6 0.0 all-reduce.5.cloned.1.call-start
  15.7 32.0 %all-reduce.7.cloned.1.call-done = (f32[1024,128]{1,0:T(8,128)}, f32[1024,128]{1,0:T(8,128)}, f32[1024,128]{1,0:T(8,128)}, f32[1024,128]{1,0:T(8,128)}, f32[1024...) async-done(((f32[1024,128]{1,0:T(8,128)}, f32[1024,128]{1,0:T(8,128)}, f32[1024,128]{1,0:T(8,128)}, f32[1024,128]{1,0:T(8,128)}, ...) | async-done | bytes 4194320 | tf_op jit(solution)/shard_map/psum | solution.py:12
  47.7 14.1 %convolution_bitcast_fusion.4 = f32[4096,128]{0,1:T(8,128)} fusion(f32[1024,128]{1,0:T(8,128)} %get-tuple-element.12, f32[1024,4096]{1,0:T(8,128)} %param.3), kind=kOutput, calls=%fused_computation.4 | convolution fusion | flops 6442450944 | bytes 19398656 | tf_op jit(solution)/shard_map/dot_general | solution.py:31
  61.8 0.0 copy-done
  61.8 0.0 copy-done.7
  61.8 0.0 copy-start.6
  61.8 10.1 %convolution_bitcast_fusion.5 = f32[4096,128]{0,1:T(8,128)} fusion(f32[1024,128]{1,0:T(8,128)S(1)} %copy-done.7, f32[1024,4096]{1,0:T(8,128)S(1)} %copy-done), kind=kOutput, calls=%fused_computation.5 | convolution fusion | flops 6442450944 | bytes 19398656 | tf_op jit(solution)/shard_map/dot_general | solution.py:31
  72.0 0.0 copy-done.6
  72.0 10.3 %convolution_bitcast_fusion.6 = f32[4096,128]{0,1:T(8,128)} fusion(f32[1024,128]{1,0:T(8,128)S(1)} %copy-done.6, f32[1024,4096]{1,0:T(8,128)S(1)} %copy-done), kind=kOutput, calls=%fused_computation.6 | convolution fusion | flops 6442450944 | bytes 19398656 | tf_op jit(solution)/shard_map/dot_general | solution.py:31
  82.3 0.0 copy-done.5
  82.3 10.4 %convolution_bitcast_fusion.7 = f32[4096,128]{0,1:T(8,128)} fusion(f32[1024,128]{1,0:T(8,128)S(1)} %copy-done.5, f32[1024,4096]{1,0:T(8,128)S(1)} %copy-done), kind=kOutput, calls=%fused_computation.7 | convolution fusion | flops 6442450944 | bytes 19398656 | tf_op jit(solution)/shard_map/dot_general | solution.py:31
  92.7 0.0 copy-done.4
  92.7 10.2 %convolution_bitcast_fusion = f32[4096,128]{0,1:T(8,128)} fusion(f32[1024,128]{1,0:T(8,128)S(1)} %copy-done.4, f32[1024,4096]{1,0:T(8,128)S(1)} %copy-done), kind=kOutput, calls=%fused_computation | convolution fusion | flops 6442450944 | bytes 19398656 | tf_op jit(solution)/shard_map/dot_general | solution.py:37
  102.9 10.6 %convolution_bitcast_fusion.1 = f32[4096,128]{0,1:T(8,128)} fusion(f32[1024,128]{1,0:T(8,128)S(1)} %copy-done.3, f32[1024,4096]{1,0:T(8,128)S(1)} %copy-done), kind=kOutput, calls=%fused_computation.1 | convolution fusion | flops 6442450944 | bytes 19398656 | tf_op jit(solution)/shard_map/dot_general | solution.py:37
  113.5 10.3 %convolution_bitcast_fusion.2 = f32[4096,128]{0,1:T(8,128)} fusion(f32[1024,128]{1,0:T(8,128)S(1)} %copy-done.2, f32[1024,4096]{1,0:T(8,128)S(1)} %copy-done), kind=kOutput, calls=%fused_computation.2 | convolution fusion | flops 6442450944 | bytes 19398656 | tf_op jit(solution)/shard_map/dot_general | solution.py:37
  123.9 10.1 %convolution_bitcast_fusion.3 = f32[4096,128]{0,1:T(8,128)} fusion(f32[1024,128]{1,0:T(8,128)S(1)} %copy-done.1, f32[1024,4096]{1,0:T(8,128)S(1)} %copy-done), kind=kOutput, calls=%fused_computation.3 | convolution fusion | flops 6442450944 | bytes 19398656 | tf_op jit(solution)/shard_map/dot_general | solution.py:37
  134.0 0.0 all-reduce.5.cloned.1.call-update
  134.0 469.3 %all-reduce.5.cloned.1.call-done = (f32[4096,128]{0,1:T(8,128)}, f32[4096,128]{0,1:T(8,128)}, f32[4096,128]{0,1:T(8,128)}, f32[4096,128]{0,1:T(8,128)}, f32[4096...) async-done(((f32[4096,128]{0,1:T(8,128)}, f32[4096,128]{0,1:T(8,128)}, f32[4096,128]{0,1:T(8,128)}, f32[4096,128]{0,1:T(8,128)}, ...) | async-done | bytes 16777232 | tf_op jit(solution)/shard_map/psum | solution.py:43
  603.3 0.9 constant_dynamic-slice_fusion.4
  604.2 0.9 constant_dynamic-slice_fusion.5
  605.1 0.9 constant_dynamic-slice_fusion.6
  606.1 0.9 constant_dynamic-slice_fusion.7
  607.0 1.0 copy.5
  608.0 0.9 constant_dynamic-slice_fusion
  608.9 0.9 constant_dynamic-slice_fusion.1
  609.9 0.9 constant_dynamic-slice_fusion.2
  610.8 0.9 constant_dynamic-slice_fusion.3
  611.8 1.0 copy.6
  (12 shorter events, 0.1 us)
Async XLA Ops:
  7.2 40.5 %all-reduce.7.cloned.1.call-start = ((), (), s32[]{:S(2)}) async-start(), calls=%async_computation.1 | async-start | bytes 8388608 | tf_op jit(solution)/shard_map/psum | solution.py:12
  15.6 587.7 %all-reduce.5.cloned.1.call-start = ((), (), s32[]{:S(2)}) async-start(), calls=%async_computation | async-start | bytes 33554432 | tf_op jit(solution)/shard_map/psum | solution.py:43
  47.7 14.1 %copy-start = (f32[1024,4096]{1,0:T(8,128)S(1)}, f32[1024,4096]{1,0:T(8,128)}, u32[]{:S(2)}) copy-start(f32[1024,4096]{1,0:T(8,128)} %param.3) | copy-start | bytes 50331652
  47.7 14.1 %copy-start.7 = (f32[1024,128]{1,0:T(8,128)S(1)}, f32[1024,128]{1,0:T(8,128)}, u32[]{:S(2)}) copy-start(f32[1024,128]{1,0:T(8,128)} %get-tuple-element.13) | copy-start | bytes 1572868
  61.8 10.1 %copy-start.6 = (f32[1024,128]{1,0:T(8,128)S(1)}, f32[1024,128]{1,0:T(8,128)}, u32[]{:S(2)}) copy-start(f32[1024,128]{1,0:T(8,128)} %get-tuple-element.14) | copy-start | bytes 1572868
  72.0 10.3 %copy-start.5 = (f32[1024,128]{1,0:T(8,128)S(1)}, f32[1024,128]{1,0:T(8,128)}, u32[]{:S(2)}) copy-start(f32[1024,128]{1,0:T(8,128)} %get-tuple-element.15) | copy-start | bytes 1572868
  82.3 10.4 %copy-start.4 = (f32[1024,128]{1,0:T(8,128)S(1)}, f32[1024,128]{1,0:T(8,128)}, u32[]{:S(2)}) copy-start(f32[1024,128]{1,0:T(8,128)} %get-tuple-element.16) | copy-start | bytes 1572868
  92.7 10.2 %copy-start.3 = (f32[1024,128]{1,0:T(8,128)S(1)}, f32[1024,128]{1,0:T(8,128)}, u32[]{:S(2)}) copy-start(f32[1024,128]{1,0:T(8,128)} %get-tuple-element.17) | copy-start | bytes 1572868
  102.9 10.6 %copy-start.2 = (f32[1024,128]{1,0:T(8,128)S(1)}, f32[1024,128]{1,0:T(8,128)}, u32[]{:S(2)}) copy-start(f32[1024,128]{1,0:T(8,128)} %get-tuple-element.18) | copy-start | bytes 1572868
  113.5 10.3 %copy-start.1 = (f32[1024,128]{1,0:T(8,128)S(1)}, f32[1024,128]{1,0:T(8,128)}, u32[]{:S(2)}) copy-start(f32[1024,128]{1,0:T(8,128)} %get-tuple-element.19) | copy-start | bytes 1572868
Sparse Core Ops, SparseCore 0:
  15.7 31.9 all-reduce.6
  134.1 469.1 all-reduce.4
where the time goes:
time: 624 us; the launch traced here: 620 us
  waiting for transfers between devices  501 us (80%)
  matrix products  86.2 us (14%)
  between operations  17 us (3%)
  local copies, waits for them, and re-layouts  10.8 us (2%)
    psum x1, waiting for transfers between devices, body(): lax.psum((correlation_full, energy_full), 'node')  469 us
    dot_general x4, matrix products, body(): jnp.dot(wavefunctions.T, psi_block, preferred_element_type=jnp.float32, p...  45 us
    dot_general x4, matrix products, body(): jnp.dot(wavefunctions.T, hpsi_block, preferred_element_type=jnp.float32,...  41.2 us
    psum x1, waiting for transfers between devices, from_root(): return lax.psum(kept, axis)  32 us
  transfers between devices with their start and end apart: 2, of which 2 were waited for; matrix products, arithmetic and copies ran while one was open for 0% of the time, Pallas kernels for 0%

commit v1 on v0

v1 whole, which is shorter than its diff:
```python
import functools

import jax
import jax.numpy as jnp
from jax import lax
from jax.experimental import pallas as pl
from jax.experimental.pallas import tpu as pltpu
from jax.sharding import PartitionSpec as P

BLOCK = 128
NBLK = 4
LANES = 128

BITS = {"x": 1, "y": 2, "z": 4, "w": 8}

PARTS = (
    ("xyzw", 88), ("yxzw", 88), ("zxyw", 80),
    ("xyzw", 88), ("yxzw", 88), ("zyxw", 80),
    ("xyzw", 88), ("yxzw", 88), ("zxyw", 80),
    ("xyzw", 88), ("yxzw", 88), ("zyxw", 80),
)


def split(value):
    high = value.astype(jnp.bfloat16)
    low = (value - high.astype(jnp.float32)).astype(jnp.bfloat16)
    return high, low


def dot3(left, right):
    left_high, left_low = left
    right_high, right_low = right
    dot = functools.partial(jnp.dot, preferred_element_type=jnp.float32)
    return dot(left_high, right_high) + (dot(left_high, right_low) + dot(left_low, right_high))


def columns_kernel(places, psi_ref, hpsi_ref, out_ref):
    out_ref[0, :BLOCK, :] = psi_ref[...].T
    out_ref[0, BLOCK:, :] = hpsi_ref[...].T


def block_columns(wavefunctions, h_wavefunctions, places):
    nodes = wavefunctions.shape[0]
    count = places.shape[0]
    source = pl.BlockSpec((nodes, BLOCK), lambda i, places: (0, places[i]))
    return pl.pallas_call(
        columns_kernel,
        grid_spec=pltpu.PrefetchScalarGridSpec(
            num_scalar_prefetch=1,
            grid=(count,),
            in_specs=[source, source],
            out_specs=pl.BlockSpec((1, 2 * BLOCK, nodes), lambda i, places: (i, 0, 0)),
        ),
        out_shape=jax.ShapeDtypeStruct((count, 2 * BLOCK, nodes), jnp.float32),
        compiler_params=pltpu.CompilerParams(vmem_limit_bytes=24 << 20),
        cost_estimate=pl.CostEstimate(
            flops=0, bytes_accessed=count * 4 * BLOCK * nodes * 4, transcendentals=0
        ),
        name="block_columns",
    )(places, wavefunctions, h_wavefunctions)


def partial_kernel(groups, columns_ref, states_ref, out_ref, high_ref, low_ref):
    @pl.when(pl.program_id(0) == 0)
    def _():
        high_ref[...], low_ref[...] = split(columns_ref[...])

    out_ref[0] = dot3((high_ref[...], low_ref[...]), split(states_ref[...]))


def partial_sums(wavefunctions, columns, groups, share_rows):
    nodes = wavefunctions.shape[0]
    width = columns.shape[0]
    count = groups.shape[0]
    return pl.pallas_call(
        partial_kernel,
        grid_spec=pltpu.PrefetchScalarGridSpec(
            num_scalar_prefetch=1,
            grid=(count,),
            in_specs=[
                pl.BlockSpec((width, nodes), lambda i, groups: (0, 0)),
                pl.BlockSpec((nodes, share_rows), lambda i, groups: (0, groups[i])),
            ],
            out_specs=pl.BlockSpec((1, width, share_rows), lambda i, groups: (i, 0, 0)),
            scratch_shapes=[
                pltpu.VMEM((width, nodes), jnp.bfloat16),
                pltpu.VMEM((width, nodes), jnp.bfloat16),
            ],
        ),
        out_shape=jax.ShapeDtypeStruct((count, width, share_rows), jnp.float32),
        compiler_params=pltpu.CompilerParams(vmem_limit_bytes=24 << 20),
        cost_estimate=pl.CostEstimate(
            flops=6 * count * width * share_rows * nodes,
            bytes_accessed=4 * (count * share_rows * (nodes + width) + width * nodes),
            transcendentals=0,
        ),
        name="partial_sums",
    )(groups, columns, wavefunctions)


def place_kernel(slots, sums_ref, correlation_ref, energy_ref):
    correlation_ref[...] = sums_ref[0, :BLOCK, :].T
    energy_ref[...] = sums_ref[0, BLOCK:, :].T


def place_columns(sums, slots, share_rows):
    out = jax.ShapeDtypeStruct((share_rows, NBLK * BLOCK), jnp.float32)
    target = pl.BlockSpec((share_rows, BLOCK), lambda i, slots: (0, slots[i]))
    return pl.pallas_call(
        place_kernel,
        grid_spec=pltpu.PrefetchScalarGridSpec(
            num_scalar_prefetch=1,
            grid=(NBLK,),
            in_specs=[pl.BlockSpec((1, 2 * BLOCK, share_rows), lambda i, slots: (i, 0, 0))],
            out_specs=[target, target],
        ),
        out_shape=[out, out],
        compiler_params=pltpu.CompilerParams(vmem_limit_bytes=24 << 20),
        name="place_columns",
    )(slots, sums)


def swap(value, bit, node_count):
    return lax.ppermute(value, "node", [(i, i ^ bit) for i in range(node_count)])


def halved(wavefunctions, h_wavefunctions, block_ids):
    local_states = wavefunctions.shape[1]
    node_count = lax.axis_size("node")
    share_rows = local_states // node_count
    local_blocks = local_states // BLOCK
    node = lax.axis_index("node")
    state = lax.axis_index("state")

    owned = block_ids // local_blocks == state
    owned_count = jnp.sum(owned.astype(jnp.int32))
    order = jnp.argsort(jnp.logical_not(owned), stable=True).astype(jnp.int32)
    places = (block_ids % local_blocks)[order]
    own = block_columns(wavefunctions, h_wavefunctions, places[: NBLK - 1])
    other = lax.ppermute(own, "state", [(0, 1), (1, 0)])
    first = own[0]
    rest = jnp.concatenate(
        [
            jnp.where(
                i < owned_count,
                own[min(i, NBLK - 2)],
                lax.dynamic_index_in_dim(other, jnp.clip(i - owned_count, 0, NBLK - 2), 0, False),
            )
            for i in range(1, NBLK)
        ]
    )

    sums = []
    start = 0
    for bits, width in PARTS:
        if start < 2 * BLOCK:
            columns = first[start : start + width]
        else:
            columns = rest[start - 2 * BLOCK : start - 2 * BLOCK + width]
        start += width
        values = [BITS[b] for b in bits]
        groups = [
            sum(v for k, v in enumerate(values) if r >> (len(bits) - 1 - k) & 1) for r in range(node_count)
        ]
        half = node_count // 2
        groups = jnp.bitwise_xor(jnp.array(groups, jnp.int32), node)
        sent = partial_sums(wavefunctions, columns, groups[half:], share_rows)
        kept = [partial_sums(wavefunctions, columns, groups[:half], share_rows)]
        for value in values:
            kept.append(swap(sent, value, node_count))
            half = half // 2
            if half:
                sent = sum(k[half : 2 * half] for k in reversed(kept))
        sums.append(sum(k[0] for k in reversed(kept)))
    sums = jnp.concatenate(sums).reshape(NBLK, 2 * BLOCK, share_rows)
    return tuple(place_columns(sums, order, share_rows))


def gathered(wavefunctions, h_wavefunctions, block_ids):
    local_states = wavefunctions.shape[1]
    state = lax.axis_index("state")
    columns = []
    for step in range(NBLK):
        first = block_ids[step] * BLOCK
        owner = first // local_states
        offset = first - owner * local_states
        for array in (wavefunctions, h_wavefunctions):
            block = lax.dynamic_slice_in_dim(array, offset, BLOCK, 1)
            columns.append(jnp.where(state == owner, block, 0))
    columns = columns[::2] + columns[1::2]
    columns = lax.psum(jnp.concatenate(columns, axis=1), "state")
    full = jnp.dot(
        wavefunctions.T, columns, preferred_element_type=jnp.float32, precision=lax.Precision.HIGH
    )
    mine = lax.psum_scatter(full, "node", scatter_dimension=0, tiled=True)
    return mine[:, : NBLK * BLOCK], mine[:, NBLK * BLOCK :]


def solution(mesh):
    node_count, state_count = mesh.shape["node"], mesh.shape["state"]

    def body(wavefunctions, h_wavefunctions, block_ids):
        share_rows = wavefunctions.shape[1] // node_count
        fits = node_count == 16 and state_count == 2 and share_rows % LANES == 0
        return (halved if fits else gathered)(wavefunctions, h_wavefunctions, block_ids)

    placed = (P("node", "state"), P("node", "state"), P())
    return jax.shard_map(
        body,
        mesh=mesh,
        in_specs=placed,
        out_specs=(P(("state", "node"), None), P(("state", "node"), None)),
        check_vma=False,
    )
```

time: 624 us -> 317 us (0.51)
  waiting for transfers between devices: 501 us -> 105 us
  Pallas kernels: 0 us -> 115 us
  matrix products: 86.2 us -> 0 us
  starting transfers between devices: 0.08 us -> 49.8 us
  other arithmetic: 4.33 us -> 17.7 us
  local copies, waits for them, and re-layouts: 10.8 us -> 22.9 us
  between operations: 17 us -> 5.17 us
    psum x2 -> x0, waiting for transfers between devices: 501 us -> none  [the longest x1 469 us: body(): lax.psum((correlation_full, energy_full), 'node')]
    pallas_call x0 -> x26, Pallas kernels: none -> 115 us  [the longest x24 110 us: partial_sums(): pl.pallas_call(partial_kernel, grid_spec=pltpu.PrefetchScalarGridSpec(num...]
    ppermute x0 -> x49, waiting for transfers between devices: none -> 105 us  [the longest x48 105 us: swap(): lax.ppermute(value, 'node', [(i, i ^ bit) for i in range(node_count)])]
    dot_general x8 -> x0, matrix products: 86.2 us -> none  [the longest x4 45 us: body(): jnp.dot(wavefunctions.T, psi_block, preferred_element_type=jnp.float32, p...]
    ppermute x0 -> x49, starting transfers between devices: none -> 49.8 us  [the longest x48 49.3 us: swap(): lax.ppermute(value, 'node', [(i, i ^ bit) for i in range(node_count)])]
    unnamed x18 -> x30, local copies, waits for them, and re-layouts: 2.02 us -> 20.9 us
    add x0 -> x36, other arithmetic: none -> 10.1 us  [halved(): sent = sum((k[half:2 * half] for k in reversed(kept)))]
    dynamic_slice x8 -> x0, local copies, waits for them, and re-layouts: 7.35 us -> none  [the longest x4 3.68 us: body(): lax.dynamic_slice_in_dim(correlation_full, row_start, share_rows, 0)]
  transfers between devices with their start and end apart: 2 -> 49, of which waited for: 2 -> 26; matrix products, arithmetic and copies ran while one was open for 0% -> 5% of each run, Pallas kernels for 0% -> 21%
where the time goes in v1:
time: 317 us; the launch traced here: 316 us
  Pallas kernels  115 us (36%)
  waiting for transfers between devices  105 us (33%)
  starting transfers between devices  49.8 us (16%)
  local copies, waits for them, and re-layouts  22.9 us (7%)
  other arithmetic  17.7 us (6%)
  between operations  5.17 us (2%)
    pallas_call x24, Pallas kernels, partial_sums(): pl.pallas_call(partial_kernel, grid_spec=pltpu.PrefetchScalarGridSpec(num...  110 us
    ppermute x48, waiting for transfers between devices, swap(): lax.ppermute(value, 'node', [(i, i ^ bit) for i in range(node_count)])  105 us
    ppermute x48, starting transfers between devices, swap(): lax.ppermute(value, 'node', [(i, i ^ bit) for i in range(node_count)])  49.3 us
    unnamed x30, local copies, waits for them, and re-layouts  20.9 us
    add x36, other arithmetic, halved(): sent = sum((k[half:2 * half] for k in reversed(kept)))  10.1 us
  transfers between devices with their start and end apart: 49, of which 26 were waited for; matrix products, arithmetic and copies ran while one was open for 5% of the time, Pallas kernels for 21%

profile of v1, /device:TPU:0, one launch (start us, length us, event | category | flops | bytes accessed | tf_op | source)
XLA Modules:
  0.0 315.9 jit_solution(1788732115992335054)
XLA Ops:
  3.3 5.8 %copy-done = f32[1024,4096]{1,0:T(8,128)S(1)} copy-done((f32[1024,4096]{1,0:T(8,128)S(1)}, f32[1024,4096]{1,0:T(8,128)}, u32[]{:S(2)}) %copy-start) | copy-done | bytes 16777240
  14.0 5.8 %copy-done.1 = f32[1024,4096]{1,0:T(8,128)S(1)} copy-done((f32[1024,4096]{1,0:T(8,128)S(1)}, f32[1024,4096]{1,0:T(8,128)}, u32[]{:S(2)}) %copy-start.1) | copy-done | bytes 16777240
  20.8 5.6 %partial_sums.24 = f32[8,88,256]{2,1,0:T(8,128)} custom-call(s32[8]{0:T(128)S(1)} %get-tuple-element.23.groups, f32[88,1024]{1,0:T(8,128)S(1)} %copy-done.3, f32[1024,4096]{1,0:T(8,128)S(1)} %copy-done.1), custom_call_target="tpu_custom_call" | custom-call | flops 1107296256 | bytes 9469952 | tf_op jit(solution)/shard_map/partial_sums/pallas_call | solution.py:75
  29.0 5.5 %partial_sums.28 = f32[8,80,256]{2,1,0:T(8,128)} custom-call(s32[8]{0:T(128)S(1)} %get-tuple-element.19.groups, f32[80,1024]{1,0:T(8,128)S(1)} %slice_bitcast_fusion.11.columns_ref, f32[1024,4096]{1,0:T(8,128)S(1)} %copy-done.1), custom_call_target="tpu_custom_call" | custom-call | flops 1006632960 | bytes 9371648 | tf_op jit(solution)/shard_map/partial_sums/pallas_call | solution.py:75
  36.1 5.6 %partial_sums.26 = f32[8,88,256]{2,1,0:T(8,128)} custom-call(s32[8]{0:T(128)S(1)} %get-tuple-element.21.groups, f32[88,1024]{1,0:T(8,128)S(1)} %get-tuple-element.9.columns_ref, f32[1024,4096]{1,0:T(8,128)S(1)} %copy-done.1), custom_call_target="tpu_custom_call" | custom-call | flops 1107296256 | bytes 9469952 | tf_op jit(solution)/shard_map/partial_sums/pallas_call | solution.py:75
  43.2 4.4 %partial_sums.25 = f32[8,88,256]{2,1,0:T(8,128)S(1)} custom-call(s32[8]{0:T(128)S(1)} %get-tuple-element.24.groups, f32[88,1024]{1,0:T(8,128)S(1)} %copy-done.4, f32[1024,4096]{1,0:T(8,128)S(1)} %copy-done.1), custom_call_target="tpu_custom_call" | custom-call | flops 1107296256 | bytes 9469952 | tf_op jit(solution)/shard_map/partial_sums/pallas_call | solution.py:75
  48.5 4.4 %partial_sums.27 = f32[8,88,256]{2,1,0:T(8,128)S(1)} custom-call(s32[8]{0:T(128)S(1)} %get-tuple-element.22.groups, f32[88,1024]{1,0:T(8,128)S(1)} %get-tuple-element.9.columns_ref, f32[1024,4096]{1,0:T(8,128)S(1)} %copy-done.1), custom_call_target="tpu_custom_call" | custom-call | flops 1107296256 | bytes 9469952 | tf_op jit(solution)/shard_map/partial_sums/pallas_call | solution.py:75
  69.3 5.7 %collective-permute-done.9 = f32[4,80,256]{2,1,0:T(8,128)S(1)} collective-permute-done((f32[4,80,256]{2,1,0:T(8,128)S(1)}, f32[4,80,256]{2,1,0:T(8,128)S(1)}, u32[]{:S(2)}, u32[]{:S(2)}) %collective-permute-start.9) | collective-permute-done | bytes 327712 | tf_op jit(solution)/shard_map/ppermute | solution.py:124
  92.4 4.8 %collective-permute-done.3 = f32[1,88,256]{2,1,0:T(8,128)S(1)} collective-permute-done((f32[1,88,256]{2,1,0:T(8,128)S(1)}, f32[1,88,256]{2,1,0:T(8,128)S(1)}, u32[]{:S(2)}, u32[]{:S(2)}) %collective-permute-start.3) | collective-permute-done | bytes 90144 | tf_op jit(solution)/shard_map/ppermute | solution.py:124
  102.5 5.8 %copy-done.2 = f32[1024,4096]{1,0:T(8,128)S(1)} copy-done((f32[1024,4096]{1,0:T(8,128)S(1)}, f32[1024,4096]{1,0:T(8,128)}, u32[]{:S(2)}) %copy-start.2) | copy-done | bytes 16777240
  108.3 4.4 %partial_sums.31 = f32[8,88,256]{2,1,0:T(8,128)S(1)} custom-call(s32[8]{0:T(128)S(1)} %get-tuple-element.24.groups, f32[88,1024]{1,0:T(8,128)S(1)} %get-tuple-element.16.columns_ref, f32[1024,4096]{1,0:T(8,128)S(1)} %copy-done.2), custom_call_target="tpu_custom_call" | custom-call | flops 1107296256 | bytes 9469952 | tf_op jit(solution)/shard_map/partial_sums/pallas_call | solution.py:75
  112.8 4.4 %partial_sums.30 = f32[8,88,256]{2,1,0:T(8,128)S(1)} custom-call(s32[8]{0:T(128)S(1)} %get-tuple-element.23.groups, f32[88,1024]{1,0:T(8,128)S(1)} %get-tuple-element.16.columns_ref, f32[1024,4096]{1,0:T(8,128)S(1)} %copy-done.2), custom_call_target="tpu_custom_call" | custom-call | flops 1107296256 | bytes 9469952 | tf_op jit(solution)/shard_map/partial_sums/pallas_call | solution.py:75
  117.2 4.4 %partial_sums.33 = f32[8,88,256]{2,1,0:T(8,128)S(1)} custom-call(s32[8]{0:T(128)S(1)} %get-tuple-element.22.groups, f32[88,1024]{1,0:T(8,128)S(1)} %get-tuple-element.15.columns_ref, f32[1024,4096]{1,0:T(8,128)S(1)} %copy-done.2), custom_call_target="tpu_custom_call" | custom-call | flops 1107296256 | bytes 9469952 | tf_op jit(solution)/shard_map/partial_sums/pallas_call | solution.py:75
  121.7 4.4 %partial_sums.32 = f32[8,88,256]{2,1,0:T(8,128)S(1)} custom-call(s32[8]{0:T(128)S(1)} %get-tuple-element.21.groups, f32[88,1024]{1,0:T(8,128)S(1)} %get-tuple-element.15.columns_ref, f32[1024,4096]{1,0:T(8,128)S(1)} %copy-done.2), custom_call_target="tpu_custom_call" | custom-call | flops 1107296256 | bytes 9469952 | tf_op jit(solution)/shard_map/partial_sums/pallas_call | solution.py:75
  126.3 4.4 %partial_sums.37 = f32[8,88,256]{2,1,0:T(8,128)S(1)} custom-call(s32[8]{0:T(128)S(1)} %get-tuple-element.24.groups, f32[88,1024]{1,0:T(8,128)S(1)} %get-tuple-element.30.columns_ref, f32[1024,4096]{1,0:T(8,128)S(1)} %copy-done.2), custom_call_target="tpu_custom_call" | custom-call | flops 1107296256 | bytes 9469952 | tf_op jit(solution)/shard_map/partial_sums/pallas_call | solution.py:75
  130.7 4.4 %partial_sums.36 = f32[8,88,256]{2,1,0:T(8,128)S(1)} custom-call(s32[8]{0:T(128)S(1)} %get-tuple-element.23.groups, f32[88,1024]{1,0:T(8,128)S(1)} %get-tuple-element.30.columns_ref, f32[1024,4096]{1,0:T(8,128)S(1)} %copy-done.2), custom_call_target="tpu_custom_call" | custom-call | flops 1107296256 | bytes 9469952 | tf_op jit(solution)/shard_map/partial_sums/pallas_call | solution.py:75
  135.2 4.4 %partial_sums.39 = f32[8,88,256]{2,1,0:T(8,128)S(1)} custom-call(s32[8]{0:T(128)S(1)} %get-tuple-element.22.groups, f32[88,1024]{1,0:T(8,128)S(1)} %get-tuple-element.31.columns_ref, f32[1024,4096]{1,0:T(8,128)S(1)} %copy-done.2), custom_call_target="tpu_custom_call" | custom-call | flops 1107296256 | bytes 9469952 | tf_op jit(solution)/shard_map/partial_sums/pallas_call | solution.py:75
  139.7 4.4 %partial_sums.38 = f32[8,88,256]{2,1,0:T(8,128)S(1)} custom-call(s32[8]{0:T(128)S(1)} %get-tuple-element.21.groups, f32[88,1024]{1,0:T(8,128)S(1)} %get-tuple-element.31.columns_ref, f32[1024,4096]{1,0:T(8,128)S(1)} %copy-done.2), custom_call_target="tpu_custom_call" | custom-call | flops 1107296256 | bytes 9469952 | tf_op jit(solution)/shard_map/partial_sums/pallas_call | solution.py:75
  165.2 4.4 %partial_sums.43 = f32[8,88,256]{2,1,0:T(8,128)S(1)} custom-call(s32[8]{0:T(128)S(1)} %get-tuple-element.24.groups, f32[88,1024]{1,0:T(8,128)S(1)} %get-tuple-element.12.columns_ref, f32[1024,4096]{1,0:T(8,128)S(1)} %copy-done.2), custom_call_target="tpu_custom_call" | custom-call | flops 1107296256 | bytes 9469952 | tf_op jit(solution)/shard_map/partial_sums/pallas_call | solution.py:75
  174.2 4.6 %partial_sums.42 = f32[8,88,256]{2,1,0:T(8,128)S(1)} custom-call(s32[8]{0:T(128)S(1)} %get-tuple-element.23.groups, f32[88,1024]{1,0:T(8,128)S(1)} %get-tuple-element.12.columns_ref, f32[1024,4096]{1,0:T(8,128)S(1)} %copy-done.2), custom_call_target="tpu_custom_call" | custom-call | flops 1107296256 | bytes 9469952 | tf_op jit(solution)/shard_map/partial_sums/pallas_call | solution.py:75
  178.8 4.4 %partial_sums.45 = f32[8,88,256]{2,1,0:T(8,128)S(1)} custom-call(s32[8]{0:T(128)S(1)} %get-tuple-element.22.groups, f32[88,1024]{1,0:T(8,128)S(1)} %get-tuple-element.11.columns_ref, f32[1024,4096]{1,0:T(8,128)S(1)} %copy-done.2), custom_call_target="tpu_custom_call" | custom-call | flops 1107296256 | bytes 9469952 | tf_op jit(solution)/shard_map/partial_sums/pallas_call | solution.py:75
  183.2 4.4 %partial_sums.47 = f32[8,80,256]{2,1,0:T(8,128)S(1)} custom-call(s32[8]{0:T(128)S(1)} %get-tuple-element.18.groups, f32[80,1024]{1,0:T(8,128)S(1)} %slice_bitcast_fusion.8.columns_ref, f32[1024,4096]{1,0:T(8,128)S(1)} %copy-done.2), custom_call_target="tpu_custom_call" | custom-call | flops 1006632960 | bytes 9371648 | tf_op jit(solution)/shard_map/partial_sums/pallas_call | solution.py:75
  187.6 4.4 %partial_sums.44 = f32[8,88,256]{2,1,0:T(8,128)S(1)} custom-call(s32[8]{0:T(128)S(1)} %get-tuple-element.21.groups, f32[88,1024]{1,0:T(8,128)S(1)} %get-tuple-element.11.columns_ref, f32[1024,4096]{1,0:T(8,128)S(1)} %copy-done.2), custom_call_target="tpu_custom_call" | custom-call | flops 1107296256 | bytes 9469952 | tf_op jit(solution)/shard_map/partial_sums/pallas_call | solution.py:75
  195.1 6.8 %collective-permute-done.45 = f32[8,80,256]{2,1,0:T(8,128)S(1)} collective-permute-done((f32[8,80,256]{2,1,0:T(8,128)S(1)}, f32[8,80,256]{2,1,0:T(8,128)S(1)}, u32[]{:S(2)}, u32[]{:S(2)}) %collective-permute-start.45) | collective-permute-done | bytes 655392 | tf_op jit(solution)/shard_map/ppermute | solution.py:124
  205.9 5.4 %collective-permute-done.25 = f32[8,88,256]{2,1,0:T(8,128)S(1)} collective-permute-done((f32[8,88,256]{2,1,0:T(8,128)S(1)}, f32[8,88,256]{2,1,0:T(8,128)S(1)}, u32[]{:S(2)}, u32[]{:S(2)}) %collective-permute-start.25) | collective-permute-done | bytes 720928 | tf_op jit(solution)/shard_map/ppermute | solution.py:124
  214.2 12.5 %collective-permute-done.37 = f32[8,88,256]{2,1,0:T(8,128)S(1)} collective-permute-done((f32[8,88,256]{2,1,0:T(8,128)S(1)}, f32[8,88,256]{2,1,0:T(8,128)S(1)}, u32[]{:S(2)}, u32[]{:S(2)}) %collective-permute-start.37) | collective-permute-done | bytes 720928 | tf_op jit(solution)/shard_map/ppermute | solution.py:124
  229.6 5.8 %collective-permute-done.22 = f32[4,80,256]{2,1,0:T(8,128)S(1)} collective-permute-done((f32[4,80,256]{2,1,0:T(8,128)S(1)}, f32[4,80,256]{2,1,0:T(8,128)S(1)}, u32[]{:S(2)}, u32[]{:S(2)}) %collective-permute-start.22) | collective-permute-done | bytes 327712 | tf_op jit(solution)/shard_map/ppermute | solution.py:124
  237.5 5.0 %collective-permute-done.46 = f32[4,80,256]{2,1,0:T(8,128)S(1)} collective-permute-done((f32[4,80,256]{2,1,0:T(8,128)S(1)}, f32[4,80,256]{2,1,0:T(8,128)S(1)}, u32[]{:S(2)}, u32[]{:S(2)}) %collective-permute-start.46) | collective-permute-done | bytes 327712 | tf_op jit(solution)/shard_map/ppermute | solution.py:124
  243.7 6.5 %collective-permute-done.14 = f32[4,88,256]{2,1,0:T(8,128)S(1)} collective-permute-done((f32[4,88,256]{2,1,0:T(8,128)S(1)}, f32[4,88,256]{2,1,0:T(8,128)S(1)}, u32[]{:S(2)}, u32[]{:S(2)}) %collective-permute-start.14) | collective-permute-done | bytes 360480 | tf_op jit(solution)/shard_map/ppermute | solution.py:124
  252.3 5.5 %collective-permute-done.26 = f32[4,88,256]{2,1,0:T(8,128)S(1)} collective-permute-done((f32[4,88,256]{2,1,0:T(8,128)S(1)}, f32[4,88,256]{2,1,0:T(8,128)S(1)}, u32[]{:S(2)}, u32[]{:S(2)}) %collective-permute-start.26) | collective-permute-done | bytes 360480 | tf_op jit(solution)/shard_map/ppermute | solution.py:124
  273.3 4.7 %collective-permute-done.19 = f32[2,88,256]{2,1,0:T(8,128)S(1)} collective-permute-done((f32[2,88,256]{2,1,0:T(8,128)S(1)}, f32[2,88,256]{2,1,0:T(8,128)S(1)}, u32[]{:S(2)}, u32[]{:S(2)}) %collective-permute-start.19) | collective-permute-done | bytes 180256 | tf_op jit(solution)/shard_map/ppermute | solution.py:124
  293.0 8.3 %collective-permute-done.16 = f32[1,88,256]{2,1,0:T(8,128)S(1)} collective-permute-done((f32[1,88,256]{2,1,0:T(8,128)S(1)}, f32[1,88,256]{2,1,0:T(8,128)S(1)}, u32[]{:S(2)}, u32[]{:S(2)}) %collective-permute-start.16) | collective-permute-done | bytes 90144 | tf_op jit(solution)/shard_map/ppermute | solution.py:124
  (191 shorter events, 139.1 us)
Async XLA Ops:
  12.6 87.4 %collective-permute-start.12 = (f32[3,256,1024]{2,1,0:T(8,128)S(1)}, f32[3,256,1024]{2,1,0:T(8,128)}, u32[]{:S(2)}, u32[]{:S(2)}) collective-permute-start(f32[3,256,1024]{2,1,0:T(8,128)S(1)} %block_columns.1), channel_id=1, source_target_pairs={{0,1},{1,0},{2,3},{3,2},{4,5},{5,4},{6,7},{7,6},{8,9},{9,8},{10,11... | collective-permute-start | bytes 9437192 | tf_op jit(solution)/shard_map/ppermute | solution.py:140
  26.3 38.6 %collective-permute-start = (f32[8,88,256]{2,1,0:T(8,128)}, f32[8,88,256]{2,1,0:T(8,128)}, u32[]{:S(2)}, u32[]{:S(2)}) collective-permute-start(f32[8,88,256]{2,1,0:T(8,128)} %partial_sums.24), channel_id=1, source_target_pairs={{0,2},{2,0},{4,6},{6,4},{8,10},{10,8},{12,14},{14,12},{16,18},{18,... | collective-permute-start | bytes 2162696 | tf_op jit(solution)/shard_map/ppermute | solution.py:124
  34.5 28.6 %collective-permute-start.8 = (f32[8,80,256]{2,1,0:T(8,128)}, f32[8,80,256]{2,1,0:T(8,128)}, u32[]{:S(2)}, u32[]{:S(2)}) collective-permute-start(f32[8,80,256]{2,1,0:T(8,128)} %partial_sums.28), channel_id=1, source_target_pairs={{0,8},{2,10},{4,12},{6,14},{8,0},{10,2},{12,4},{14,6},{16,24},{18,... | collective-permute-start | bytes 1966088 | tf_op jit(solution)/shard_map/ppermute | solution.py:124
  41.7 24.9 %collective-permute-start.4 = (f32[8,88,256]{2,1,0:T(8,128)}, f32[8,88,256]{2,1,0:T(8,128)}, u32[]{:S(2)}, u32[]{:S(2)}) collective-permute-start(f32[8,88,256]{2,1,0:T(8,128)} %partial_sums.26), channel_id=1, source_target_pairs={{0,4},{2,6},{4,0},{6,2},{8,12},{10,14},{12,8},{14,10},{16,20},{18,... | collective-permute-start | bytes 2162696 | tf_op jit(solution)/shard_map/ppermute | solution.py:124
  67.8 13.6 %collective-permute-start.5 = (f32[4,88,256]{2,1,0:T(8,128)S(1)}, f32[4,88,256]{2,1,0:T(8,128)S(1)}, u32[]{:S(2)}, u32[]{:S(2)}) collective-permute-start(f32[4,88,256]{2,1,0:T(8,128)S(1)} %slice_add_fusion.6), channel_id=1, source_target_pairs={{0,2},{2,0},{4,6},{6,4},{8,10},{10,8},{12,14},{14,12},{16,18},{18,... | collective-permute-start | bytes 1081352 | tf_op jit(solution)/shard_map/ppermute | solution.py:124
  83.8 15.3 %collective-permute-start.11 = (f32[1,80,256]{2,1,0:T(8,128)S(1)}, f32[1,80,256]{2,1,0:T(8,128)S(1)}, u32[]{:S(2)}, u32[]{:S(2)}) collective-permute-start(f32[1,80,256]{2,1,0:T(8,128)S(1)} %slice_add_fusion.117), channel_id=1, source_target_pairs={{0,16},{2,18},{4,20},{6,22},{8,24},{10,26},{12,28},{14,30},{16,0},... | collective-permute-start | bytes 245768 | tf_op jit(solution)/shard_map/ppermute | solution.py:124
  153.0 50.6 %collective-permute-start.13 = (f32[8,88,256]{2,1,0:T(8,128)S(1)}, f32[8,88,256]{2,1,0:T(8,128)S(1)}, u32[]{:S(2)}, u32[]{:S(2)}) collective-permute-start(f32[8,88,256]{2,1,0:T(8,128)S(1)} %partial_sums.30), channel_id=1, source_target_pairs={{0,2},{2,0},{4,6},{6,4},{8,10},{10,8},{12,14},{14,12},{16,18},{18,... | collective-permute-start | bytes 2162696 | tf_op jit(solution)/shard_map/ppermute | solution.py:124
  153.7 51.1 %collective-permute-start.17 = (f32[8,88,256]{2,1,0:T(8,128)S(1)}, f32[8,88,256]{2,1,0:T(8,128)S(1)}, u32[]{:S(2)}, u32[]{:S(2)}) collective-permute-start(f32[8,88,256]{2,1,0:T(8,128)S(1)} %partial_sums.32), channel_id=1, source_target_pairs={{0,4},{2,6},{4,0},{6,2},{8,12},{10,14},{12,8},{14,10},{16,20},{18,... | collective-permute-start | bytes 2162696 | tf_op jit(solution)/shard_map/ppermute | solution.py:124
  158.7 33.4 %collective-permute-start.21 = (f32[8,80,256]{2,1,0:T(8,128)S(1)}, f32[8,80,256]{2,1,0:T(8,128)S(1)}, u32[]{:S(2)}, u32[]{:S(2)}) collective-permute-start(f32[8,80,256]{2,1,0:T(8,128)S(1)} %partial_sums.34), channel_id=1, source_target_pairs={{0,8},{2,10},{4,12},{6,14},{8,0},{10,2},{12,4},{14,6},{16,24},{18,... | collective-permute-start | bytes 1966088 | tf_op jit(solution)/shard_map/ppermute | solution.py:124
  158.8 35.0 %collective-permute-start.33 = (f32[8,80,256]{2,1,0:T(8,128)S(1)}, f32[8,80,256]{2,1,0:T(8,128)S(1)}, u32[]{:S(2)}, u32[]{:S(2)}) collective-permute-start(f32[8,80,256]{2,1,0:T(8,128)S(1)} %partial_sums.40), channel_id=1, source_target_pairs={{0,8},{2,10},{4,12},{6,14},{8,0},{10,2},{12,4},{14,6},{16,24},{18,... | collective-permute-start | bytes 1966088 | tf_op jit(solution)/shard_map/ppermute | solution.py:124
  174.0 27.9 %collective-permute-start.45 = (f32[8,80,256]{2,1,0:T(8,128)S(1)}, f32[8,80,256]{2,1,0:T(8,128)S(1)}, u32[]{:S(2)}, u32[]{:S(2)}) collective-permute-start(f32[8,80,256]{2,1,0:T(8,128)S(1)} %partial_sums.46), channel_id=1, source_target_pairs={{0,8},{2,10},{4,12},{6,14},{8,0},{10,2},{12,4},{14,6},{16,24},{18,... | collective-permute-start | bytes 1966088 | tf_op jit(solution)/shard_map/ppermute | solution.py:124
  192.1 19.1 %collective-permute-start.25 = (f32[8,88,256]{2,1,0:T(8,128)S(1)}, f32[8,88,256]{2,1,0:T(8,128)S(1)}, u32[]{:S(2)}, u32[]{:S(2)}) collective-permute-start(f32[8,88,256]{2,1,0:T(8,128)S(1)} %partial_sums.36), channel_id=1, source_target_pairs={{0,2},{2,0},{4,6},{6,4},{8,10},{10,8},{12,14},{14,12},{16,18},{18,... | collective-permute-start | bytes 2162696 | tf_op jit(solution)/shard_map/ppermute | solution.py:124
  193.8 19.1 %collective-permute-start.29 = (f32[8,88,256]{2,1,0:T(8,128)S(1)}, f32[8,88,256]{2,1,0:T(8,128)S(1)}, u32[]{:S(2)}, u32[]{:S(2)}) collective-permute-start(f32[8,88,256]{2,1,0:T(8,128)S(1)} %partial_sums.38), channel_id=1, source_target_pairs={{0,4},{2,6},{4,0},{6,2},{8,12},{10,14},{12,8},{14,10},{16,20},{18,... | collective-permute-start | bytes 2162696 | tf_op jit(solution)/shard_map/ppermute | solution.py:124
  201.9 24.8 %collective-permute-start.37 = (f32[8,88,256]{2,1,0:T(8,128)S(1)}, f32[8,88,256]{2,1,0:T(8,128)S(1)}, u32[]{:S(2)}, u32[]{:S(2)}) collective-permute-start(f32[8,88,256]{2,1,0:T(8,128)S(1)} %partial_sums.42), channel_id=1, source_target_pairs={{0,2},{2,0},{4,6},{6,4},{8,10},{10,8},{12,14},{14,12},{16,18},{18,... | collective-permute-start | bytes 2162696 | tf_op jit(solution)/shard_map/ppermute | solution.py:124
  203.6 24.8 %collective-permute-start.41 = (f32[8,88,256]{2,1,0:T(8,128)S(1)}, f32[8,88,256]{2,1,0:T(8,128)S(1)}, u32[]{:S(2)}, u32[]{:S(2)}) collective-permute-start(f32[8,88,256]{2,1,0:T(8,128)S(1)} %partial_sums.44), channel_id=1, source_target_pairs={{0,4},{2,6},{4,0},{6,2},{8,12},{10,14},{12,8},{14,10},{16,20},{18,... | collective-permute-start | bytes 2162696 | tf_op jit(solution)/shard_map/ppermute | solution.py:124
  204.9 30.5 %collective-permute-start.22 = (f32[4,80,256]{2,1,0:T(8,128)S(1)}, f32[4,80,256]{2,1,0:T(8,128)S(1)}, u32[]{:S(2)}, u32[]{:S(2)}) collective-permute-start(f32[4,80,256]{2,1,0:T(8,128)S(1)} %slice_add_fusion.10), channel_id=1, source_target_pairs={{0,4},{2,6},{4,0},{6,2},{8,12},{10,14},{12,8},{14,10},{16,20},{18,... | collective-permute-start | bytes 983048 | tf_op jit(solution)/shard_map/ppermute | solution.py:124
  211.2 25.4 %collective-permute-start.34 = (f32[4,80,256]{2,1,0:T(8,128)S(1)}, f32[4,80,256]{2,1,0:T(8,128)S(1)}, u32[]{:S(2)}, u32[]{:S(2)}) collective-permute-start(f32[4,80,256]{2,1,0:T(8,128)S(1)} %slice_add_fusion.9), channel_id=1, source_target_pairs={{0,2},{2,0},{4,6},{6,4},{8,10},{10,8},{12,14},{14,12},{16,18},{18,... | collective-permute-start | bytes 983048 | tf_op jit(solution)/shard_map/ppermute | solution.py:124
  212.9 29.5 %collective-permute-start.46 = (f32[4,80,256]{2,1,0:T(8,128)S(1)}, f32[4,80,256]{2,1,0:T(8,128)S(1)}, u32[]{:S(2)}, u32[]{:S(2)}) collective-permute-start(f32[4,80,256]{2,1,0:T(8,128)S(1)} %slice_add_fusion.8), channel_id=1, source_target_pairs={{0,4},{2,6},{4,0},{6,2},{8,12},{10,14},{12,8},{14,10},{16,20},{18,... | collective-permute-start | bytes 983048 | tf_op jit(solution)/shard_map/ppermute | solution.py:124
  226.7 23.5 %collective-permute-start.14 = (f32[4,88,256]{2,1,0:T(8,128)S(1)}, f32[4,88,256]{2,1,0:T(8,128)S(1)}, u32[]{:S(2)}, u32[]{:S(2)}) collective-permute-start(f32[4,88,256]{2,1,0:T(8,128)S(1)} %slice_add_fusion.5), channel_id=1, source_target_pairs={{0,4},{2,6},{4,0},{6,2},{8,12},{10,14},{12,8},{14,10},{16,20},{18,... | collective-permute-start | bytes 1081352 | tf_op jit(solution)/shard_map/ppermute | solution.py:124
  228.4 22.3 %collective-permute-start.18 = (f32[4,88,256]{2,1,0:T(8,128)S(1)}, f32[4,88,256]{2,1,0:T(8,128)S(1)}, u32[]{:S(2)}, u32[]{:S(2)}) collective-permute-start(f32[4,88,256]{2,1,0:T(8,128)S(1)} %slice_add_fusion.4), channel_id=1, source_target_pairs={{0,2},{2,0},{4,6},{6,4},{8,10},{10,8},{12,14},{14,12},{16,18},{18,... | collective-permute-start | bytes 1081352 | tf_op jit(solution)/shard_map/ppermute | solution.py:124
  235.4 22.5 %collective-permute-start.26 = (f32[4,88,256]{2,1,0:T(8,128)S(1)}, f32[4,88,256]{2,1,0:T(8,128)S(1)}, u32[]{:S(2)}, u32[]{:S(2)}) collective-permute-start(f32[4,88,256]{2,1,0:T(8,128)S(1)} %slice_add_fusion.3), channel_id=1, source_target_pairs={{0,4},{2,6},{4,0},{6,2},{8,12},{10,14},{12,8},{14,10},{16,20},{18,... | collective-permute-start | bytes 1081352 | tf_op jit(solution)/shard_map/ppermute | solution.py:124
  236.6 22.5 %collective-permute-start.30 = (f32[4,88,256]{2,1,0:T(8,128)S(1)}, f32[4,88,256]{2,1,0:T(8,128)S(1)}, u32[]{:S(2)}, u32[]{:S(2)}) collective-permute-start(f32[4,88,256]{2,1,0:T(8,128)S(1)} %slice_add_fusion.2), channel_id=1, source_target_pairs={{0,2},{2,0},{4,6},{6,4},{8,10},{10,8},{12,14},{14,12},{16,18},{18,... | collective-permute-start | bytes 1081352 | tf_op jit(solution)/shard_map/ppermute | solution.py:124
  242.4 21.5 %collective-permute-start.38 = (f32[4,88,256]{2,1,0:T(8,128)S(1)}, f32[4,88,256]{2,1,0:T(8,128)S(1)}, u32[]{:S(2)}, u32[]{:S(2)}) collective-permute-start(f32[4,88,256]{2,1,0:T(8,128)S(1)} %slice_add_fusion.1), channel_id=1, source_target_pairs={{0,4},{2,6},{4,0},{6,2},{8,12},{10,14},{12,8},{14,10},{16,20},{18,... | collective-permute-start | bytes 1081352 | tf_op jit(solution)/shard_map/ppermute | solution.py:124
  250.2 15.5 %collective-permute-start.42 = (f32[4,88,256]{2,1,0:T(8,128)S(1)}, f32[4,88,256]{2,1,0:T(8,128)S(1)}, u32[]{:S(2)}, u32[]{:S(2)}) collective-permute-start(f32[4,88,256]{2,1,0:T(8,128)S(1)} %slice_add_fusion), channel_id=1, source_target_pairs={{0,2},{2,0},{4,6},{6,4},{8,10},{10,8},{12,14},{14,12},{16,18},{18,... | collective-permute-start | bytes 1081352 | tf_op jit(solution)/shard_map/ppermute | solution.py:124
  250.7 15.5 %collective-permute-start.23 = (f32[2,80,256]{2,1,0:T(8,128)S(1)}, f32[2,80,256]{2,1,0:T(8,128)S(1)}, u32[]{:S(2)}, u32[]{:S(2)}) collective-permute-start(f32[2,80,256]{2,1,0:T(8,128)S(1)} %slice_add_fusion.32), channel_id=1, source_target_pairs={{0,2},{2,0},{4,6},{6,4},{8,10},{10,8},{12,14},{14,12},{16,18},{18,... | collective-permute-start | bytes 491528 | tf_op jit(solution)/shard_map/ppermute | solution.py:124
  266.2 15.9 %collective-permute-start.27 = (f32[2,88,256]{2,1,0:T(8,128)S(1)}, f32[2,88,256]{2,1,0:T(8,128)S(1)}, u32[]{:S(2)}, u32[]{:S(2)}) collective-permute-start(f32[2,88,256]{2,1,0:T(8,128)S(1)} %slice_add_fusion.18), channel_id=1, source_target_pairs={{0,8},{2,10},{4,12},{6,14},{8,0},{10,2},{12,4},{14,6},{16,24},{18,... | collective-permute-start | bytes 540680 | tf_op jit(solution)/shard_map/ppermute | solution.py:124
  267.9 17.6 %collective-permute-start.31 = (f32[2,88,256]{2,1,0:T(8,128)S(1)}, f32[2,88,256]{2,1,0:T(8,128)S(1)}, u32[]{:S(2)}, u32[]{:S(2)}) collective-permute-start(f32[2,88,256]{2,1,0:T(8,128)S(1)} %slice_add_fusion.16), channel_id=1, source_target_pairs={{0,8},{2,10},{4,12},{6,14},{8,0},{10,2},{12,4},{14,6},{16,24},{18,... | collective-permute-start | bytes 540680 | tf_op jit(solution)/shard_map/ppermute | solution.py:124
  268.4 20.9 %collective-permute-start.39 = (f32[2,88,256]{2,1,0:T(8,128)S(1)}, f32[2,88,256]{2,1,0:T(8,128)S(1)}, u32[]{:S(2)}, u32[]{:S(2)}) collective-permute-start(f32[2,88,256]{2,1,0:T(8,128)S(1)} %slice_add_fusion.14), channel_id=1, source_target_pairs={{0,8},{2,10},{4,12},{6,14},{8,0},{10,2},{12,4},{14,6},{16,24},{18,... | collective-permute-start | bytes 540680 | tf_op jit(solution)/shard_map/ppermute | solution.py:124
  273.2 19.8 %collective-permute-start.43 = (f32[2,88,256]{2,1,0:T(8,128)S(1)}, f32[2,88,256]{2,1,0:T(8,128)S(1)}, u32[]{:S(2)}, u32[]{:S(2)}) collective-permute-start(f32[2,88,256]{2,1,0:T(8,128)S(1)} %slice_add_fusion.12), channel_id=1, source_target_pairs={{0,8},{2,10},{4,12},{6,14},{8,0},{10,2},{12,4},{14,6},{16,24},{18,... | collective-permute-start | bytes 540680 | tf_op jit(solution)/shard_map/ppermute | solution.py:124
  278.0 26.5 %collective-permute-start.24 = (f32[1,80,256]{2,1,0:T(8,128)S(1)}, f32[1,80,256]{2,1,0:T(8,128)S(1)}, u32[]{:S(2)}, u32[]{:S(2)}) collective-permute-start(f32[1,80,256]{2,1,0:T(8,128)S(1)} %slice_add_fusion.110), channel_id=1, source_target_pairs={{0,16},{2,18},{4,20},{6,22},{8,24},{10,26},{12,28},{14,30},{16,0},... | collective-permute-start | bytes 245768 | tf_op jit(solution)/shard_map/ppermute | solution.py:124
  282.1 27.6 %collective-permute-start.36 = (f32[1,80,256]{2,1,0:T(8,128)S(1)}, f32[1,80,256]{2,1,0:T(8,128)S(1)}, u32[]{:S(2)}, u32[]{:S(2)}) collective-permute-start(f32[1,80,256]{2,1,0:T(8,128)S(1)} %slice_add_fusion.103), channel_id=1, source_target_pairs={{0,16},{2,18},{4,20},{6,22},{8,24},{10,26},{12,28},{14,30},{16,0},... | collective-permute-start | bytes 245768 | tf_op jit(solution)/shard_map/ppermute | solution.py:124
  285.5 28.1 %collective-permute-start.48 = (f32[1,80,256]{2,1,0:T(8,128)S(1)}, f32[1,80,256]{2,1,0:T(8,128)S(1)}, u32[]{:S(2)}, u32[]{:S(2)}) collective-permute-start(f32[1,80,256]{2,1,0:T(8,128)S(1)} %slice_add_fusion.96), channel_id=1, source_target_pairs={{0,16},{2,18},{4,20},{6,22},{8,24},{10,26},{12,28},{14,30},{16,0},... | collective-permute-start | bytes 245768 | tf_op jit(solution)/shard_map/ppermute | solution.py:124
  (32 other events, 249.4 us)

commit v2 on v1

v2 whole, which is shorter than its diff:
```python
import functools

import jax
import jax.numpy as jnp
from jax import lax
from jax.experimental import pallas as pl
from jax.experimental.pallas import tpu as pltpu
from jax.sharding import PartitionSpec as P

BLOCK = 128
NBLK = 4
LANES = 128
BUFFERS = 4
STEPS = 8
VMEM = 50 << 20

BITS = {"x": 1, "y": 2, "z": 4, "w": 8}

GROUPS = (
    (("xyzw", 88), ("yxzw", 88), ("zxyw", 80)),
    (("xyzw", 128), ("yxzw", 136), ("zyxw", 120)),
    (("xyzw", 136), ("yxzw", 128), ("zxyw", 120)),
)

ORDER = ("0", "1", 0, 1, 2, "2", 0, 1, 2, 3, 4, 5, 0, 1, 2, 3, 4, 5, 6, 7, 8, 3, 4, 5, 6, 7, 8, 6, 7, 8)


def split(value):
    high = value.astype(jnp.bfloat16)
    low = (value - high.astype(jnp.float32)).astype(jnp.bfloat16)
    return high, low


def ranked(info, rank, local_blocks):
    owned = [(lax.div(info[i], local_blocks) == info[NBLK + 1]).astype(jnp.int32) for i in range(NBLK)]
    mine = sum(owned)
    place, slot = 0, 0
    for i in range(NBLK):
        at = jnp.where(owned[i] == 1, sum(owned[:i]), mine + i - sum(owned[:i]))
        place = jnp.where(at == rank, lax.rem(info[i], local_blocks), place)
        slot = jnp.where(at == rank, i, slot)
    return place, slot


def owned_count(info, local_blocks):
    return sum((lax.div(info[i], local_blocks) == info[NBLK + 1]).astype(jnp.int32) for i in range(NBLK))


def columns_kernel(info, psi_ref, hpsi_ref, out_ref):
    out_ref[0, :BLOCK, :] = psi_ref[...].T
    out_ref[0, BLOCK:, :] = hpsi_ref[...].T


def block_columns(wavefunctions, h_wavefunctions, info, local_blocks):
    nodes = wavefunctions.shape[0]
    count = NBLK - 1
    source = pl.BlockSpec((nodes, BLOCK), lambda i, info: (0, ranked(info, i, local_blocks)[0]))
    return pl.pallas_call(
        columns_kernel,
        grid_spec=pltpu.PrefetchScalarGridSpec(
            num_scalar_prefetch=1,
            grid=(count,),
            in_specs=[source, source],
            out_specs=pl.BlockSpec((1, 2 * BLOCK, nodes), lambda i, info: (i, 0, 0)),
        ),
        out_shape=jax.ShapeDtypeStruct((count, 2 * BLOCK, nodes), jnp.float32),
        compiler_params=pltpu.CompilerParams(vmem_limit_bytes=VMEM),
        cost_estimate=pl.CostEstimate(
            flops=0, bytes_accessed=count * 4 * BLOCK * nodes * 4, transcendentals=0
        ),
        name="block_columns",
    )(info, wavefunctions, h_wavefunctions)


def bit_of(step, axis):
    shift = {"y": 2, "z": 1, "w": 0}[axis]
    return (step >> shift) & 1


def taken(step, axis, sent):
    bit = {"y": 4, "z": 2, "w": 1}[axis]
    before = step & -(2 * bit)
    if sent:
        return jnp.where(step & bit, step, jnp.maximum(before - 1, bit))
    return jnp.where(step & bit, before + bit - 1, step)


def partial_kernel(info, own_ref, other_ref, states_ref, token_ref, *refs, outs, pieces, local_blocks):
    del token_ref
    out_refs, (columns_ref, stack_ref, block_ref, columns_sem, sem) = refs[: len(outs)], refs[len(outs) :]
    width = columns_ref.shape[0]
    share_rows = block_ref.shape[2] // 2
    step = pl.program_id(0)
    slot = step % BUFFERS

    def fetch(at):
        copies = []
        for half in range(2):
            relative = (bit_of(at, "y") << 1) | (bit_of(at, "z") << 2) | (bit_of(at, "w") << 3) | half
            group = relative ^ info[NBLK]
            copies.append(
                pltpu.make_async_copy(
                    states_ref.at[:, pl.ds(pl.multiple_of(group * share_rows, share_rows), share_rows)],
                    block_ref.at[at % BUFFERS, :, pl.ds(half * share_rows, share_rows)],
                    sem.at[at % BUFFERS, half],
                )
            )
        return copies

    @pl.when(step == 0)
    def _():
        for ahead in range(BUFFERS - 1):
            for copy in fetch(ahead):
                copy.start()
        mine = owned_count(info, local_blocks)
        row = 0
        for number, (rank, first, rows) in enumerate(pieces):
            here = columns_ref.at[pl.ds(row, rows)]
            row += rows

            @pl.when(rank < mine)
            def _():
                source = own_ref.at[min(rank, NBLK - 2), pl.ds(first, rows)]
                pltpu.make_async_copy(source, here, columns_sem.at[number]).start()

            @pl.when(rank >= mine)
            def _():
                source = other_ref.at[jnp.clip(rank - mine, 0, NBLK - 2), pl.ds(first, rows)]
                pltpu.make_async_copy(source, here, columns_sem.at[number]).start()

        row = 0
        for number, (rank, first, rows) in enumerate(pieces):
            here = columns_ref.at[pl.ds(row, rows)]
            row += rows
            pltpu.make_async_copy(here, here, columns_sem.at[number]).wait()
        stack_ref[:width], stack_ref[width:] = split(columns_ref[...])

    @pl.when(step + BUFFERS - 1 < STEPS)
    def _():
        for copy in fetch(step + BUFFERS - 1):
            copy.start()

    for copy in fetch(step):
        copy.wait()
    dot = functools.partial(jnp.dot, preferred_element_type=jnp.float32)
    high, low = split(block_ref[slot])
    both = dot(stack_ref[...], high)
    result = both[:width] + (both[width:] + dot(stack_ref[:width], low))
    halves = (result[:, :share_rows], result[:, share_rows:])
    for (bits, start, size, sent), out_ref in zip(outs, out_refs):
        if bits[0] == "x":
            out_ref[0, 0, 0] = halves[sent][start : start + size]
            continue
        at = bits.index("x") - 1

        @pl.when(bit_of(step, bits[0]) == sent)
        def _():
            for half in range(2):
                index = tuple(half if k == at else 0 for k in range(3))
                out_ref[index] = halves[half][start : start + size]


def partial_sums(wavefunctions, own, other, info, share_rows, parts, first, token):
    nodes = wavefunctions.shape[0]
    width = sum(size for _, size in parts)
    outs = []
    for sent in (1, 0):
        start = 0
        for bits, size in parts:
            outs.append((bits, start, size, sent))
            start += size
    pieces = []
    at = first
    while at < first + width:
        rank, row = divmod(at, 2 * BLOCK)
        rows = min(2 * BLOCK - row, first + width - at)
        pieces.append((rank, row, rows))
        at += rows

    def spec(bits, start, size, sent):
        def index(step, info):
            if bits[0] != "x":
                step = taken(step, bits[0], sent)
            return (*(0 if b == "x" else bit_of(step, b) for b in bits[1:]), 0, 0)

        return pl.BlockSpec((*(2 if b == "x" else 1 for b in bits[1:]), size, share_rows), index)

    made = pl.pallas_call(
        functools.partial(
            partial_kernel, outs=outs, pieces=pieces, local_blocks=wavefunctions.shape[1] // BLOCK
        ),
        grid_spec=pltpu.PrefetchScalarGridSpec(
            num_scalar_prefetch=1,
            grid=(STEPS,),
            in_specs=[pl.BlockSpec(memory_space=pl.ANY)] * 4,
            out_specs=[spec(*out) for out in outs],
            scratch_shapes=[
                pltpu.VMEM((width, nodes), jnp.float32),
                pltpu.VMEM((2 * width, nodes), jnp.bfloat16),
                pltpu.VMEM((BUFFERS, nodes, 2 * share_rows), jnp.float32),
                pltpu.SemaphoreType.DMA((len(pieces),)),
                pltpu.SemaphoreType.DMA((BUFFERS, 2)),
            ],
        ),
        out_shape=[jax.ShapeDtypeStruct((2, 2, 2, out[2], share_rows), jnp.float32) for out in outs],
        compiler_params=pltpu.CompilerParams(vmem_limit_bytes=VMEM),
        cost_estimate=pl.CostEstimate(
            flops=12 * STEPS * width * share_rows * nodes,
            bytes_accessed=8 * STEPS * share_rows * (nodes + width),
            transcendentals=0,
        ),
        name="partial_sums",
    )(info, own, other, wavefunctions, token)
    return [m.reshape(8, *m.shape[3:]) for m in made]


def total(leaves, at):
    value = leaves[0][at]
    for leaf in leaves[1:]:
        value = value + leaf[at]
    return value


def add_kernel(*refs):
    refs[-1][0] = total(refs[:-2], 0)


def add_up(leaves, count, token):
    shape = leaves[0].shape[1:]
    return pl.pallas_call(
        add_kernel,
        grid=(count,),
        in_specs=[pl.BlockSpec((1, *shape), lambda i: (count + i, 0, 0))] * len(leaves)
        + [pl.BlockSpec(memory_space=pl.ANY)],
        out_specs=pl.BlockSpec((1, *shape), lambda i: (i, 0, 0)),
        out_shape=jax.ShapeDtypeStruct((count, *shape), jnp.float32),
        compiler_params=pltpu.CompilerParams(vmem_limit_bytes=16 << 20),
        cost_estimate=pl.CostEstimate(
            flops=0, bytes_accessed=4 * count * shape[0] * shape[1] * (len(leaves) + 1), transcendentals=0
        ),
        name="add_up",
    )(*leaves, token)


def place_kernel(info, sums_ref, correlation_ref, energy_ref):
    correlation_ref[...] = sums_ref[0, :BLOCK, :].T
    energy_ref[...] = sums_ref[0, BLOCK:, :].T


def place_columns(sums, info, share_rows, local_blocks):
    out = jax.ShapeDtypeStruct((share_rows, NBLK * BLOCK), jnp.float32)
    target = pl.BlockSpec((share_rows, BLOCK), lambda i, info: (0, ranked(info, i, local_blocks)[1]))
    return pl.pallas_call(
        place_kernel,
        grid_spec=pltpu.PrefetchScalarGridSpec(
            num_scalar_prefetch=1,
            grid=(NBLK,),
            in_specs=[pl.BlockSpec((1, 2 * BLOCK, share_rows), lambda i, info: (i, 0, 0))],
            out_specs=[target, target],
        ),
        out_shape=[out, out],
        compiler_params=pltpu.CompilerParams(vmem_limit_bytes=24 << 20),
        name="place_columns",
    )(info, sums)


def swap(value, axis):
    bit = BITS[axis]
    return lax.ppermute(value, "node", [(i, i ^ bit) for i in range(lax.axis_size("node"))])


def swap_cores(value):
    return lax.ppermute(value, "state", [(0, 1), (1, 0)])


def other_columns(first, more, other, owned_count):
    own, other = jnp.concatenate([first, more]), jnp.concatenate(other)
    return jnp.concatenate(
        [
            jnp.where(
                i < owned_count,
                own[min(i, NBLK - 2)],
                lax.dynamic_index_in_dim(other, jnp.clip(i - owned_count, 0, NBLK - 2), 0, False),
            )
            for i in range(1, NBLK)
        ]
    )


def halved(wavefunctions, h_wavefunctions, block_ids):
    local_states = wavefunctions.shape[1]
    share_rows = local_states // lax.axis_size("node")
    local_blocks = local_states // BLOCK
    info = jnp.concatenate([block_ids, lax.axis_index("node")[None], lax.axis_index("state")[None]])

    own = block_columns(wavefunctions, h_wavefunctions, info, local_blocks)
    other = swap_cores(own)
    last = own
    held, sizes = {}, {}
    first = 0
    for step in ORDER:
        if isinstance(step, str):
            group = int(step)
            parts = GROUPS[group]
            out = partial_sums(
                wavefunctions, own, other if group else own, info, share_rows, parts, first, last
            )
            last = out[0]
            first += sum(size for _, size in parts)
            sent, kept = out[: len(parts)], out[len(parts) :]
            for (bits, size), send, keep in zip(parts, sent, kept):
                held[len(held)] = (bits, [keep, swap(send, bits[0])])
        else:
            bits, leaves = held[step]
            turn = len(leaves) - 1
            last = add_up(leaves, 8 >> turn, last)
            leaves.append(swap(last, bits[turn]))
    results = [total(leaves, 0) for _, leaves in held.values()]
    sums = jnp.concatenate(results).reshape(NBLK, 2 * BLOCK, share_rows)
    return tuple(place_columns(sums, info, share_rows, local_blocks))


def gathered(wavefunctions, h_wavefunctions, block_ids):
    local_states = wavefunctions.shape[1]
    state = lax.axis_index("state")
    columns = []
    for step in range(NBLK):
        first = block_ids[step] * BLOCK
        owner = first // local_states
        offset = first - owner * local_states
        for array in (wavefunctions, h_wavefunctions):
            block = lax.dynamic_slice_in_dim(array, offset, BLOCK, 1)
            columns.append(jnp.where(state == owner, block, 0))
    columns = columns[::2] + columns[1::2]
    columns = lax.psum(jnp.concatenate(columns, axis=1), "state")
    full = jnp.dot(
        wavefunctions.T, columns, preferred_element_type=jnp.float32, precision=lax.Precision.HIGH
    )
    mine = lax.psum_scatter(full, "node", scatter_dimension=0, tiled=True)
    return mine[:, : NBLK * BLOCK], mine[:, NBLK * BLOCK :]


def solution(mesh):
    node_count, state_count = mesh.shape["node"], mesh.shape["state"]

    def body(wavefunctions, h_wavefunctions, block_ids):
        share_rows = wavefunctions.shape[1] // node_count
        fits = node_count == 16 and state_count == 2 and share_rows % LANES == 0
        return (halved if fits else gathered)(wavefunctions, h_wavefunctions, block_ids)

    placed = (P("node", "state"), P("node", "state"), P())
    return jax.shard_map(
        body,
        mesh=mesh,
        in_specs=placed,
        out_specs=(P(("state", "node"), None), P(("state", "node"), None)),
        check_vma=False,
    )
```

time: 317 us -> 193 us (0.61)
  Pallas kernels: 115 us -> 56.6 us
  local copies, waits for them, and re-layouts: 22.9 us -> 1.87 us
  other arithmetic: 17.7 us -> 1.11 us
  starting transfers between devices: 49.8 us -> 37.9 us
  waiting for transfers between devices: 105 us -> 94 us
  between operations: 5.17 us -> 1.01 us
    pallas_call x24 -> x30, Pallas kernels: 110 us -> 50.5 us  [the longest x3 48.6 us: partial_sums(): pl.pallas_call(functools.partial(partial_kernel, outs=outs, pieces=pieces...]
    unnamed x30 -> x12, local copies, waits for them, and re-layouts: 20.9 us -> 1.87 us
    ppermute x49 -> x37, starting transfers between devices: 49.8 us -> 37.9 us  [the longest x36 37.4 us: swap(): lax.ppermute(value, 'node', [(i, i ^ bit) for i in range(lax.axis_size('n...]
    ppermute x49 -> x37, waiting for transfers between devices: 105 us -> 94 us  [the longest x36 94 us: swap(): lax.ppermute(value, 'node', [(i, i ^ bit) for i in range(lax.axis_size('n...]
    add x36 -> x0, other arithmetic: 10.1 us -> none  [halved(): sent = sum((k[half:2 * half] for k in reversed(kept)))]
  transfers between devices with their start and end apart: 49 -> 37, of which waited for: 26 -> 20; matrix products, arithmetic and copies ran while one was open for 5% -> 0% of each run, Pallas kernels for 21% -> 26%
where the time goes in v2:
time: 193 us
  waiting for transfers between devices  94 us (49%)
  Pallas kernels  56.6 us (29%)
  starting transfers between devices  37.9 us (20%)
    ppermute x36, waiting for transfers between devices, swap(): lax.ppermute(value, 'node', [(i, i ^ bit) for i in range(lax.axis_size('n...  94 us
    pallas_call x3, Pallas kernels, partial_sums(): pl.pallas_call(functools.partial(partial_kernel, outs=outs, pieces=pieces...  48.6 us
    ppermute x36, starting transfers between devices, swap(): lax.ppermute(value, 'node', [(i, i ^ bit) for i in range(lax.axis_size('n...  37.4 us
  transfers between devices with their start and end apart: 37, of which 20 were waited for; matrix products, arithmetic and copies ran while one was open for 0% of the time, Pallas kernels for 26%

profile of v2, /device:TPU:0, one launch (start us, length us, event | category | flops | bytes accessed | tf_op | source)
XLA Modules:
  0.0 192.6 jit_solution(139865869069629475)
XLA Ops:
  1.4 3.8 %block_columns.1.own_ref.other_ref.token_ref = f32[3,256,1024]{2,1,0:T(8,128)S(1)} custom-call(s32[6]{0:T(128)S(1)} %pad_add_fusion.info, f32[1024,4096]{1,0:T(8,128)} %states_ref.5, f32[1024,4096]{1,0:T(8,128)} %hpsi_ref.1), custom_call_target="tpu_custom_call" | custom-call | bytes 6291456 | tf_op jit(solution)/shard_map/block_columns/pallas_call | solution.py:58
  6.8 13.6 %partial_sums.3 = (f32[2,2,2,88,256]{4,3,2,1,0:T(8,128)S(1)}, f32[2,2,2,88,256]{4,3,2,1,0:T(8,128)S(1)}, f32[2,2,2,80,256]{4,3,2,1,0:T(8,128)S(1)}, f32[2,2,2,88...) custom-call(s32[6]{0:T(128)S(1)} %pad_add_fusion.info, ...), custom_call_target="tpu_custom_call" | custom-call | flops 6442450944 | bytes 20971520 | tf_op jit(solution)/shard_map/partial_sums/pallas_call | solution.py:188
  20.4 3.1 %collective-permute-start.3 = (f32[8,80,256]{2,1,0:T(8,128)S(1)}, f32[8,80,256]{2,1,0:T(8,128)S(1)}, u32[]{:S(2)}, u32[]{:S(2)}) collective-permute-start(f32[8,80,256]{2,1,0:T(8,128)S(1)} %bitcast.101), channel_id=1, source_target_pairs={{0,8},{2,10},{4,12},{6,14},{8,0},{10,2},{12,4},{14,6},{16,24},{18,... | collective-permute-start | bytes 1966088 | tf_op jit(solution)/shard_map/ppermute | solution.py:269
  26.5 17.5 %partial_sums.4 = (f32[2,2,2,128,256]{4,3,2,1,0:T(8,128)S(1)}, f32[2,2,2,136,256]{4,3,2,1,0:T(8,128)}, f32[2,2,2,120,256]{4,3,2,1,0:T(8,128)}, f32[2,2,2,128,256...) custom-call(s32[6]{0:T(128)S(1)} %pad_add_fusion.info, f32[3,256,1024]{2,1,0:T(8,128)} %copy-done, ...), custom_call_target="tpu_custom_call" | custom-call | flops 9663676416 | bytes 23068672 | tf_op jit(solution)/shard_map/partial_sums/pallas_call | solution.py:188
  45.4 1.6 collective-permute-start.10
  48.0 5.6 %collective-permute-done.2.refs_2_ = f32[4,88,256]{2,1,0:T(8,128)S(1)} collective-permute-done((f32[4,88,256]{2,1,0:T(8,128)S(1)}, f32[4,88,256]{2,1,0:T(8,128)S(1)}, u32[]{:S(2)}, u32[]{:S(2)}) %collective-permute-start.2) | collective-permute-done | bytes 360480 | tf_op jit(solution)/shard_map/ppermute | solution.py:269
  54.1 17.4 %partial_sums.5 = (f32[2,2,2,136,256]{4,3,2,1,0:T(8,128)}, f32[2,2,2,128,256]{4,3,2,1,0:T(8,128)S(1)}, f32[2,2,2,120,256]{4,3,2,1,0:T(8,128)S(1)}, f32[2,2,2,136...) custom-call(s32[6]{0:T(128)S(1)} %pad_add_fusion.info, ...), custom_call_target="tpu_custom_call" | custom-call | flops 9663676416 | bytes 23068672 | tf_op jit(solution)/shard_map/partial_sums/pallas_call | solution.py:188
  71.6 7.0 %collective-permute-done.10.refs_2_ = f32[4,88,256]{2,1,0:T(8,128)S(1)} collective-permute-done((f32[4,88,256]{2,1,0:T(8,128)S(1)}, f32[4,88,256]{2,1,0:T(8,128)S(1)}, u32[]{:S(2)}, u32[]{:S(2)}) %collective-permute-start.10) | collective-permute-done | bytes 360480 | tf_op jit(solution)/shard_map/ppermute | solution.py:269
  78.7 4.6 %collective-permute-done.9.refs_2_ = f32[4,80,256]{2,1,0:T(8,128)S(1)} collective-permute-done((f32[4,80,256]{2,1,0:T(8,128)S(1)}, f32[4,80,256]{2,1,0:T(8,128)S(1)}, u32[]{:S(2)}, u32[]{:S(2)}) %collective-permute-start.9) | collective-permute-done | bytes 327712 | tf_op jit(solution)/shard_map/ppermute | solution.py:269
  83.4 1.6 collective-permute-start.14
  86.1 3.5 %collective-permute-done.14.refs_3_ = f32[2,80,256]{2,1,0:T(8,128)S(1)} collective-permute-done((f32[2,80,256]{2,1,0:T(8,128)S(1)}, f32[2,80,256]{2,1,0:T(8,128)S(1)}, u32[]{:S(2)}, u32[]{:S(2)}) %collective-permute-start.14) | collective-permute-done | bytes 163872 | tf_op jit(solution)/shard_map/ppermute | solution.py:269
  92.0 1.6 collective-permute-start.5
  93.9 21.5 %collective-permute-done.5.refs_3_ = f32[2,88,256]{2,1,0:T(8,128)S(1)} collective-permute-done((f32[2,88,256]{2,1,0:T(8,128)S(1)}, f32[2,88,256]{2,1,0:T(8,128)S(1)}, u32[]{:S(2)}, u32[]{:S(2)}) %collective-permute-start.5) | collective-permute-done | bytes 180256 | tf_op jit(solution)/shard_map/ppermute | solution.py:269
  116.6 16.4 %collective-permute-done.21.refs_2_ = f32[4,120,256]{2,1,0:T(8,128)S(1)} collective-permute-done((f32[4,120,256]{2,1,0:T(8,128)S(1)}, f32[4,120,256]{2,1,0:T(8,128)S(1)}, u32[]{:S(2)}, u32[]{:S(2)}) %collective-permute-start.21) | collective-permute-done | bytes 491552 | tf_op jit(solution)/shard_map/ppermute | solution.py:269
  133.0 2.6 %collective-permute-start.11 = (f32[1,88,256]{2,1,0:T(8,128)S(1)}, f32[1,88,256]{2,1,0:T(8,128)S(1)}, u32[]{:S(2)}, u32[]{:S(2)}) collective-permute-start(f32[1,88,256]{2,1,0:T(8,128)S(1)} %add_up.36.refs_4_), channel_id=1, source_target_pairs={{0,16},{2,18},{4,20},{6,22},{8,24},{10,26},{12,28},{14,30},{16,0},... | collective-permute-start | bytes 270344 | tf_op jit(solution)/shard_map/ppermute | solution.py:269
  137.7 1.9 %collective-permute-start.13 = (f32[1,88,256]{2,1,0:T(8,128)S(1)}, f32[1,88,256]{2,1,0:T(8,128)S(1)}, u32[]{:S(2)}, u32[]{:S(2)}) collective-permute-start(f32[1,88,256]{2,1,0:T(8,128)S(1)} %add_up.37.refs_4_), channel_id=1, source_target_pairs={{0,16},{2,18},{4,20},{6,22},{8,24},{10,26},{12,28},{14,30},{16,0},... | collective-permute-start | bytes 270344 | tf_op jit(solution)/shard_map/ppermute | solution.py:269
  139.7 1.6 collective-permute-start.24
  141.3 1.5 collective-permute-start.28
  143.1 1.6 collective-permute-done.15
  148.0 2.8 %collective-permute-done.24.refs_3_ = f32[2,136,256]{2,1,0:T(8,128)S(1)} collective-permute-done((f32[2,136,256]{2,1,0:T(8,128)S(1)}, f32[2,136,256]{2,1,0:T(8,128)S(1)}, u32[]{:S(2)}, u32[]{:S(2)}) %collective-permute-start.24) | collective-permute-done | bytes 278560 | tf_op jit(solution)/shard_map/ppermute | solution.py:269
  151.3 2.3 %collective-permute-done.26.refs_3_ = f32[2,120,256]{2,1,0:T(8,128)S(1)} collective-permute-done((f32[2,120,256]{2,1,0:T(8,128)S(1)}, f32[2,120,256]{2,1,0:T(8,128)S(1)}, u32[]{:S(2)}, u32[]{:S(2)}) %collective-permute-start.26) | collective-permute-done | bytes 245792 | tf_op jit(solution)/shard_map/ppermute | solution.py:269
  153.6 3.4 %collective-permute-start.25 = (f32[1,136,256]{2,1,0:T(8,128)S(1)}, f32[1,136,256]{2,1,0:T(8,128)S(1)}, u32[]{:S(2)}, u32[]{:S(2)}) collective-permute-start(f32[1,136,256]{2,1,0:T(8,128)S(1)} %add_up.46.refs_4_), channel_id=1, source_target_pairs={{0,16},{2,18},{4,20},{6,22},{8,24},{10,26},{12,28},{14,30},{16,0},... | collective-permute-start | bytes 417800 | tf_op jit(solution)/shard_map/ppermute | solution.py:269
  157.2 3.3 %collective-permute-done.23 = f32[1,128,256]{2,1,0:T(8,128)S(1)} collective-permute-done((f32[1,128,256]{2,1,0:T(8,128)S(1)}, f32[1,128,256]{2,1,0:T(8,128)S(1)}, u32[]{:S(2)}, u32[]{:S(2)}) %collective-permute-start.23) | collective-permute-done | bytes 131104 | tf_op jit(solution)/shard_map/ppermute | solution.py:269
  160.6 2.4 %collective-permute-done.31.refs_2_ = f32[4,128,256]{2,1,0:T(8,128)S(1)} collective-permute-done((f32[4,128,256]{2,1,0:T(8,128)S(1)}, f32[4,128,256]{2,1,0:T(8,128)S(1)}, u32[]{:S(2)}, u32[]{:S(2)}) %collective-permute-start.31) | collective-permute-done | bytes 524320 | tf_op jit(solution)/shard_map/ppermute | solution.py:269
  163.1 5.1 %collective-permute-done.30.refs_2_ = f32[4,120,256]{2,1,0:T(8,128)S(1)} collective-permute-done((f32[4,120,256]{2,1,0:T(8,128)S(1)}, f32[4,120,256]{2,1,0:T(8,128)S(1)}, u32[]{:S(2)}, u32[]{:S(2)}) %collective-permute-start.30) | collective-permute-done | bytes 491552 | tf_op jit(solution)/shard_map/ppermute | solution.py:269
  168.3 1.6 collective-permute-start.35
  169.9 2.8 %collective-permute-done.29.refs_3_ = f32[2,136,256]{2,1,0:T(8,128)S(1)} collective-permute-done((f32[2,136,256]{2,1,0:T(8,128)S(1)}, f32[2,136,256]{2,1,0:T(8,128)S(1)}, u32[]{:S(2)}, u32[]{:S(2)}) %collective-permute-start.29) | collective-permute-done | bytes 278560 | tf_op jit(solution)/shard_map/ppermute | solution.py:269
  172.9 2.6 %collective-permute-done.33.refs_3_ = f32[2,128,256]{2,1,0:T(8,128)S(1)} collective-permute-done((f32[2,128,256]{2,1,0:T(8,128)S(1)}, f32[2,128,256]{2,1,0:T(8,128)S(1)}, u32[]{:S(2)}, u32[]{:S(2)}) %collective-permute-start.33) | collective-permute-done | bytes 262176 | tf_op jit(solution)/shard_map/ppermute | solution.py:269
  175.6 2.1 %collective-permute-start.34 = (f32[1,128,256]{2,1,0:T(8,128)S(1)}, f32[1,128,256]{2,1,0:T(8,128)S(1)}, u32[]{:S(2)}, u32[]{:S(2)}) collective-permute-start(f32[1,128,256]{2,1,0:T(8,128)S(1)} %add_up.52.refs_4_), channel_id=1, source_target_pairs={{0,16},{2,18},{4,20},{6,22},{8,24},{10,26},{12,28},{14,30},{16,0},... | collective-permute-start | bytes 393224 | tf_op jit(solution)/shard_map/ppermute | solution.py:269
  178.7 7.6 %collective-permute-done.32 = f32[1,136,256]{2,1,0:T(8,128)S(1)} collective-permute-done((f32[1,136,256]{2,1,0:T(8,128)S(1)}, f32[1,136,256]{2,1,0:T(8,128)S(1)}, u32[]{:S(2)}, u32[]{:S(2)}) %collective-permute-start.32) | collective-permute-done | bytes 139296 | tf_op jit(solution)/shard_map/ppermute | solution.py:269
  186.3 2.5 %collective-permute-done.34 = f32[1,128,256]{2,1,0:T(8,128)S(1)} collective-permute-done((f32[1,128,256]{2,1,0:T(8,128)S(1)}, f32[1,128,256]{2,1,0:T(8,128)S(1)}, u32[]{:S(2)}, u32[]{:S(2)}) %collective-permute-start.34) | collective-permute-done | bytes 131104 | tf_op jit(solution)/shard_map/ppermute | solution.py:269
  190.2 2.4 %place_columns.1 = (f32[256,512]{1,0:T(8,128)}, f32[256,512]{1,0:T(8,128)}) custom-call(s32[6]{0:T(128)S(1)} %pad_add_fusion.info, f32[4,256,256]{2,1,0:T(8,128)S(1)} %bitcast.93), custom_call_target="tpu_custom_call" | custom-call | tf_op jit(solution)/shard_map/place_columns/pallas_call | solution.py:253
  (96 shorter events, 22.8 us)
Async XLA Ops:
  5.2 21.3 %collective-permute-start.1 = (f32[3,256,1024]{2,1,0:T(8,128)S(1)}, f32[3,256,1024]{2,1,0:T(8,128)}, u32[]{:S(2)}, u32[]{:S(2)}) collective-permute-start(f32[3,256,1024]{2,1,0:T(8,128)S(1)} %block_columns.1.own_ref.other_ref.token_ref), channel_id=1, source_target_pairs={{0,1},{1,0},{2,3},{3,2},{4,5},{5,4},{6,7},{7,6},{8,9},{9,8},{10,11... | collective-permute-start | bytes 9437192 | tf_op jit(solution)/shard_map/ppermute | solution.py:273
  20.4 26.6 %collective-permute-start.3 = (f32[8,80,256]{2,1,0:T(8,128)S(1)}, f32[8,80,256]{2,1,0:T(8,128)S(1)}, u32[]{:S(2)}, u32[]{:S(2)}) collective-permute-start(f32[8,80,256]{2,1,0:T(8,128)S(1)} %bitcast.101), channel_id=1, source_target_pairs={{0,8},{2,10},{4,12},{6,14},{8,0},{10,2},{12,4},{14,6},{16,24},{18,... | collective-permute-start | bytes 1966088 | tf_op jit(solution)/shard_map/ppermute | solution.py:269
  23.5 20.6 %collective-permute-start = (f32[8,88,256]{2,1,0:T(8,128)S(1)}, f32[8,88,256]{2,1,0:T(8,128)S(1)}, u32[]{:S(2)}, u32[]{:S(2)}) collective-permute-start(f32[8,88,256]{2,1,0:T(8,128)S(1)} %bitcast.99), channel_id=1, source_target_pairs={{0,2},{2,0},{4,6},{6,4},{8,10},{10,8},{12,14},{14,12},{16,18},{18,... | collective-permute-start | bytes 2162696 | tf_op jit(solution)/shard_map/ppermute | solution.py:269
  25.0 20.3 %collective-permute-start.4 = (f32[8,88,256]{2,1,0:T(8,128)S(1)}, f32[8,88,256]{2,1,0:T(8,128)S(1)}, u32[]{:S(2)}, u32[]{:S(2)}) collective-permute-start(f32[8,88,256]{2,1,0:T(8,128)S(1)} %bitcast.98), channel_id=1, source_target_pairs={{0,4},{2,6},{4,0},{6,2},{8,12},{10,14},{12,8},{14,10},{16,20},{18,... | collective-permute-start | bytes 2162696 | tf_op jit(solution)/shard_map/ppermute | solution.py:269
  44.2 9.4 %collective-permute-start.2 = (f32[4,88,256]{2,1,0:T(8,128)S(1)}, f32[4,88,256]{2,1,0:T(8,128)S(1)}, u32[]{:S(2)}, u32[]{:S(2)}) collective-permute-start(f32[4,88,256]{2,1,0:T(8,128)S(1)} %add_up.27.refs_2_), channel_id=1, source_target_pairs={{0,4},{2,6},{4,0},{6,2},{8,12},{10,14},{12,8},{14,10},{16,20},{18,... | collective-permute-start | bytes 1081352 | tf_op jit(solution)/shard_map/ppermute | solution.py:269
  44.8 40.6 %collective-permute-start.8 = (f32[8,128,256]{2,1,0:T(8,128)S(1)}, f32[8,128,256]{2,1,0:T(8,128)S(1)}, u32[]{:S(2)}, u32[]{:S(2)}) collective-permute-start(f32[8,128,256]{2,1,0:T(8,128)S(1)} %bitcast.95), channel_id=1, source_target_pairs={{0,2},{2,0},{4,6},{6,4},{8,10},{10,8},{12,14},{14,12},{16,18},{18,... | collective-permute-start | bytes 3145736 | tf_op jit(solution)/shard_map/ppermute | solution.py:269
  45.4 33.2 %collective-permute-start.10 = (f32[4,88,256]{2,1,0:T(8,128)S(1)}, f32[4,88,256]{2,1,0:T(8,128)S(1)}, u32[]{:S(2)}, u32[]{:S(2)}) collective-permute-start(f32[4,88,256]{2,1,0:T(8,128)S(1)} %add_up.28.refs_2_), channel_id=1, source_target_pairs={{0,2},{2,0},{4,6},{6,4},{8,10},{10,8},{12,14},{14,12},{16,18},{18,... | collective-permute-start | bytes 1081352 | tf_op jit(solution)/shard_map/ppermute | solution.py:269
  47.1 36.2 %collective-permute-start.9 = (f32[4,80,256]{2,1,0:T(8,128)S(1)}, f32[4,80,256]{2,1,0:T(8,128)S(1)}, u32[]{:S(2)}, u32[]{:S(2)}) collective-permute-start(f32[4,80,256]{2,1,0:T(8,128)S(1)} %add_up.29.token_ref), channel_id=1, source_target_pairs={{0,2},{2,0},{4,6},{6,4},{8,10},{10,8},{12,14},{14,12},{16,18},{18,... | collective-permute-start | bytes 983048 | tf_op jit(solution)/shard_map/ppermute | solution.py:269
  47.7 43.9 %collective-permute-start.6 = (f32[8,120,256]{2,1,0:T(8,128)}, f32[8,120,256]{2,1,0:T(8,128)S(1)}, u32[]{:S(2)}, u32[]{:S(2)}) collective-permute-start(f32[8,120,256]{2,1,0:T(8,128)} %bitcast.11), channel_id=1, source_target_pairs={{0,8},{2,10},{4,12},{6,14},{8,0},{10,2},{12,4},{14,6},{16,24},{18,... | collective-permute-start | bytes 2949128 | tf_op jit(solution)/shard_map/ppermute | solution.py:269
  53.6 38.4 %collective-permute-start.7 = (f32[8,136,256]{2,1,0:T(8,128)}, f32[8,136,256]{2,1,0:T(8,128)S(1)}, u32[]{:S(2)}, u32[]{:S(2)}) collective-permute-start(f32[8,136,256]{2,1,0:T(8,128)} %bitcast.13), channel_id=1, source_target_pairs={{0,4},{2,6},{4,0},{6,2},{8,12},{10,14},{12,8},{14,10},{16,20},{18,... | collective-permute-start | bytes 3342344 | tf_op jit(solution)/shard_map/ppermute | solution.py:269
  85.4 51.0 %collective-permute-start.20 = (f32[8,136,256]{2,1,0:T(8,128)}, f32[8,136,256]{2,1,0:T(8,128)S(1)}, u32[]{:S(2)}, u32[]{:S(2)}) collective-permute-start(f32[8,136,256]{2,1,0:T(8,128)} %bitcast.9.refs_3_), channel_id=1, source_target_pairs={{0,2},{2,0},{4,6},{6,4},{8,10},{10,8},{12,14},{14,12},{16,18},{18,... | collective-permute-start | bytes 3342344 | tf_op jit(solution)/shard_map/ppermute | solution.py:269
  89.5 26.9 %collective-permute-start.16 = (f32[4,128,256]{2,1,0:T(8,128)S(1)}, f32[4,128,256]{2,1,0:T(8,128)S(1)}, u32[]{:S(2)}, u32[]{:S(2)}) collective-permute-start(f32[4,128,256]{2,1,0:T(8,128)S(1)} %add_up.33.refs_2_), channel_id=1, source_target_pairs={{0,4},{2,6},{4,0},{6,2},{8,12},{10,14},{12,8},{14,10},{16,20},{18,... | collective-permute-start | bytes 1572872 | tf_op jit(solution)/shard_map/ppermute | solution.py:269
  91.2 48.5 %collective-permute-start.19 = (f32[8,128,256]{2,1,0:T(8,128)S(1)}, f32[8,128,256]{2,1,0:T(8,128)S(1)}, u32[]{:S(2)}, u32[]{:S(2)}) collective-permute-start(f32[8,128,256]{2,1,0:T(8,128)S(1)} %bitcast.96), channel_id=1, source_target_pairs={{0,4},{2,6},{4,0},{6,2},{8,12},{10,14},{12,8},{14,10},{16,20},{18,... | collective-permute-start | bytes 3145736 | tf_op jit(solution)/shard_map/ppermute | solution.py:269
  91.6 46.1 %collective-permute-start.18 = (f32[8,120,256]{2,1,0:T(8,128)S(1)}, f32[8,120,256]{2,1,0:T(8,128)S(1)}, u32[]{:S(2)}, u32[]{:S(2)}) collective-permute-start(f32[8,120,256]{2,1,0:T(8,128)S(1)} %bitcast.97), channel_id=1, source_target_pairs={{0,8},{2,10},{4,12},{6,14},{8,0},{10,2},{12,4},{14,6},{16,24},{18,... | collective-permute-start | bytes 2949128 | tf_op jit(solution)/shard_map/ppermute | solution.py:269
  92.0 23.4 %collective-permute-start.5 = (f32[2,88,256]{2,1,0:T(8,128)S(1)}, f32[2,88,256]{2,1,0:T(8,128)S(1)}, u32[]{:S(2)}, u32[]{:S(2)}) collective-permute-start(f32[2,88,256]{2,1,0:T(8,128)S(1)} %add_up.30.refs_3_), channel_id=1, source_target_pairs={{0,8},{2,10},{4,12},{6,14},{8,0},{10,2},{12,4},{14,6},{16,24},{18,... | collective-permute-start | bytes 540680 | tf_op jit(solution)/shard_map/ppermute | solution.py:269
  115.4 17.6 %collective-permute-start.21 = (f32[4,120,256]{2,1,0:T(8,128)S(1)}, f32[4,120,256]{2,1,0:T(8,128)S(1)}, u32[]{:S(2)}, u32[]{:S(2)}) collective-permute-start(f32[4,120,256]{2,1,0:T(8,128)S(1)} %add_up.35.refs_4_), channel_id=1, source_target_pairs={{0,4},{2,6},{4,0},{6,2},{8,12},{10,14},{12,8},{14,10},{16,20},{18,... | collective-permute-start | bytes 1474568 | tf_op jit(solution)/shard_map/ppermute | solution.py:269
  116.4 19.3 %collective-permute-start.22 = (f32[4,136,256]{2,1,0:T(8,128)S(1)}, f32[4,136,256]{2,1,0:T(8,128)S(1)}, u32[]{:S(2)}, u32[]{:S(2)}) collective-permute-start(f32[4,136,256]{2,1,0:T(8,128)S(1)} %add_up.34.refs_2_), channel_id=1, source_target_pairs={{0,2},{2,0},{4,6},{6,4},{8,10},{10,8},{12,14},{14,12},{16,18},{18,... | collective-permute-start | bytes 1671176 | tf_op jit(solution)/shard_map/ppermute | solution.py:269
  135.8 11.5 %collective-permute-start.17 = (f32[2,128,256]{2,1,0:T(8,128)S(1)}, f32[2,128,256]{2,1,0:T(8,128)S(1)}, u32[]{:S(2)}, u32[]{:S(2)}) collective-permute-start(f32[2,128,256]{2,1,0:T(8,128)S(1)} %add_up.39.refs_3_), channel_id=1, source_target_pairs={{0,8},{2,10},{4,12},{6,14},{8,0},{10,2},{12,4},{14,6},{16,24},{18,... | collective-permute-start | bytes 786440 | tf_op jit(solution)/shard_map/ppermute | solution.py:269
  139.7 11.1 %collective-permute-start.24 = (f32[2,136,256]{2,1,0:T(8,128)S(1)}, f32[2,136,256]{2,1,0:T(8,128)S(1)}, u32[]{:S(2)}, u32[]{:S(2)}) collective-permute-start(f32[2,136,256]{2,1,0:T(8,128)S(1)} %add_up.40.refs_3_), channel_id=1, source_target_pairs={{0,8},{2,10},{4,12},{6,14},{8,0},{10,2},{12,4},{14,6},{16,24},{18,... | collective-permute-start | bytes 835592 | tf_op jit(solution)/shard_map/ppermute | solution.py:269
  141.3 15.8 %collective-permute-start.28 = (f32[4,136,256]{2,1,0:T(8,128)S(1)}, f32[4,136,256]{2,1,0:T(8,128)S(1)}, u32[]{:S(2)}, u32[]{:S(2)}) collective-permute-start(f32[4,136,256]{2,1,0:T(8,128)S(1)} %add_up.42.refs_2_), channel_id=1, source_target_pairs={{0,4},{2,6},{4,0},{6,2},{8,12},{10,14},{12,8},{14,10},{16,20},{18,... | collective-permute-start | bytes 1671176 | tf_op jit(solution)/shard_map/ppermute | solution.py:269
  144.7 8.9 %collective-permute-start.26 = (f32[2,120,256]{2,1,0:T(8,128)S(1)}, f32[2,120,256]{2,1,0:T(8,128)S(1)}, u32[]{:S(2)}, u32[]{:S(2)}) collective-permute-start(f32[2,120,256]{2,1,0:T(8,128)S(1)} %add_up.41.refs_2_), channel_id=1, source_target_pairs={{0,2},{2,0},{4,6},{6,4},{8,10},{10,8},{12,14},{14,12},{16,18},{18,... | collective-permute-start | bytes 737288 | tf_op jit(solution)/shard_map/ppermute | solution.py:269
  145.7 17.2 %collective-permute-start.31 = (f32[4,128,256]{2,1,0:T(8,128)S(1)}, f32[4,128,256]{2,1,0:T(8,128)S(1)}, u32[]{:S(2)}, u32[]{:S(2)}) collective-permute-start(f32[4,128,256]{2,1,0:T(8,128)S(1)} %add_up.43.refs_2_), channel_id=1, source_target_pairs={{0,2},{2,0},{4,6},{6,4},{8,10},{10,8},{12,14},{14,12},{16,18},{18,... | collective-permute-start | bytes 1572872 | tf_op jit(solution)/shard_map/ppermute | solution.py:269
  147.3 20.9 %collective-permute-start.30 = (f32[4,120,256]{2,1,0:T(8,128)S(1)}, f32[4,120,256]{2,1,0:T(8,128)S(1)}, u32[]{:S(2)}, u32[]{:S(2)}) collective-permute-start(f32[4,120,256]{2,1,0:T(8,128)S(1)} %add_up.44.refs_4_), channel_id=1, source_target_pairs={{0,2},{2,0},{4,6},{6,4},{8,10},{10,8},{12,14},{14,12},{16,18},{18,... | collective-permute-start | bytes 1474568 | tf_op jit(solution)/shard_map/ppermute | solution.py:269
  150.8 9.7 %collective-permute-start.23 = (f32[1,128,256]{2,1,0:T(8,128)S(1)}, f32[1,128,256]{2,1,0:T(8,128)S(1)}, u32[]{:S(2)}, u32[]{:S(2)}) collective-permute-start(f32[1,128,256]{2,1,0:T(8,128)S(1)} %add_up.45.refs_4_), channel_id=1, source_target_pairs={{0,16},{2,18},{4,20},{6,22},{8,24},{10,26},{12,28},{14,30},{16,0},... | collective-permute-start | bytes 393224 | tf_op jit(solution)/shard_map/ppermute | solution.py:269
  153.6 16.3 %collective-permute-start.25 = (f32[1,136,256]{2,1,0:T(8,128)S(1)}, f32[1,136,256]{2,1,0:T(8,128)S(1)}, u32[]{:S(2)}, u32[]{:S(2)}) collective-permute-start(f32[1,136,256]{2,1,0:T(8,128)S(1)} %add_up.46.refs_4_), channel_id=1, source_target_pairs={{0,16},{2,18},{4,20},{6,22},{8,24},{10,26},{12,28},{14,30},{16,0},... | collective-permute-start | bytes 417800 | tf_op jit(solution)/shard_map/ppermute | solution.py:269
  157.0 15.8 %collective-permute-start.27 = (f32[1,120,256]{2,1,0:T(8,128)S(1)}, f32[1,120,256]{2,1,0:T(8,128)S(1)}, u32[]{:S(2)}, u32[]{:S(2)}) collective-permute-start(f32[1,120,256]{2,1,0:T(8,128)S(1)} %add_up.47.refs_3_), channel_id=1, source_target_pairs={{0,16},{2,18},{4,20},{6,22},{8,24},{10,26},{12,28},{14,30},{16,0},... | collective-permute-start | bytes 368648 | tf_op jit(solution)/shard_map/ppermute | solution.py:269
  160.5 12.2 %collective-permute-start.29 = (f32[2,136,256]{2,1,0:T(8,128)S(1)}, f32[2,136,256]{2,1,0:T(8,128)S(1)}, u32[]{:S(2)}, u32[]{:S(2)}) collective-permute-start(f32[2,136,256]{2,1,0:T(8,128)S(1)} %add_up.48.refs_3_), channel_id=1, source_target_pairs={{0,8},{2,10},{4,12},{6,14},{8,0},{10,2},{12,4},{14,6},{16,24},{18,... | collective-permute-start | bytes 835592 | tf_op jit(solution)/shard_map/ppermute | solution.py:269
  163.0 12.5 %collective-permute-start.33 = (f32[2,128,256]{2,1,0:T(8,128)S(1)}, f32[2,128,256]{2,1,0:T(8,128)S(1)}, u32[]{:S(2)}, u32[]{:S(2)}) collective-permute-start(f32[2,128,256]{2,1,0:T(8,128)S(1)} %add_up.49.refs_3_), channel_id=1, source_target_pairs={{0,8},{2,10},{4,12},{6,14},{8,0},{10,2},{12,4},{14,6},{16,24},{18,... | collective-permute-start | bytes 786440 | tf_op jit(solution)/shard_map/ppermute | solution.py:269
  168.3 9.4 %collective-permute-start.35 = (f32[2,120,256]{2,1,0:T(8,128)S(1)}, f32[2,120,256]{2,1,0:T(8,128)S(1)}, u32[]{:S(2)}, u32[]{:S(2)}) collective-permute-start(f32[2,120,256]{2,1,0:T(8,128)S(1)} %add_up.50.refs_4_), channel_id=1, source_target_pairs={{0,4},{2,6},{4,0},{6,2},{8,12},{10,14},{12,8},{14,10},{16,20},{18,... | collective-permute-start | bytes 737288 | tf_op jit(solution)/shard_map/ppermute | solution.py:269
  172.8 13.5 %collective-permute-start.32 = (f32[1,136,256]{2,1,0:T(8,128)S(1)}, f32[1,136,256]{2,1,0:T(8,128)S(1)}, u32[]{:S(2)}, u32[]{:S(2)}) collective-permute-start(f32[1,136,256]{2,1,0:T(8,128)S(1)} %add_up.51.refs_4_), channel_id=1, source_target_pairs={{0,16},{2,18},{4,20},{6,22},{8,24},{10,26},{12,28},{14,30},{16,0},... | collective-permute-start | bytes 417800 | tf_op jit(solution)/shard_map/ppermute | solution.py:269
  175.6 13.3 %collective-permute-start.34 = (f32[1,128,256]{2,1,0:T(8,128)S(1)}, f32[1,128,256]{2,1,0:T(8,128)S(1)}, u32[]{:S(2)}, u32[]{:S(2)}) collective-permute-start(f32[1,128,256]{2,1,0:T(8,128)S(1)} %add_up.52.refs_4_), channel_id=1, source_target_pairs={{0,16},{2,18},{4,20},{6,22},{8,24},{10,26},{12,28},{14,30},{16,0},... | collective-permute-start | bytes 393224 | tf_op jit(solution)/shard_map/ppermute | solution.py:269
  177.7 12.5 %collective-permute-start.36 = (f32[1,120,256]{2,1,0:T(8,128)S(1)}, f32[1,120,256]{2,1,0:T(8,128)S(1)}, u32[]{:S(2)}, u32[]{:S(2)}) collective-permute-start(f32[1,120,256]{2,1,0:T(8,128)S(1)} %add_up.53), channel_id=1, source_target_pairs={{0,16},{2,18},{4,20},{6,22},{8,24},{10,26},{12,28},{14,30},{16,0},... | collective-permute-start | bytes 368648 | tf_op jit(solution)/shard_map/ppermute | solution.py:269
  (11 other events, 61.2 us)

commit v3 on v2

--- a/solution.py
+++ b/solution.py
@@ -17,12 +17,14 @@
 BITS = {"x": 1, "y": 2, "z": 4, "w": 8}
 
 GROUPS = (
-    (("xyzw", 88), ("yxzw", 88), ("zxyw", 80)),
+    (("xyzw", 88), ("yxzw", 88), ("zwyx", 80)),
     (("xyzw", 128), ("yxzw", 136), ("zyxw", 120)),
-    (("xyzw", 136), ("yxzw", 128), ("zxyw", 120)),
+    (("xyzw", 144), ("yxzw", 112), ("zxyw", 128)),
 )
 
-ORDER = ("0", "1", 0, 1, 2, "2", 0, 1, 2, 3, 4, 5, 0, 1, 2, 3, 4, 5, 6, 7, 8, 3, 4, 5, 6, 7, 8, 6, 7, 8)
+ORDER = (
+    "0", "1", 0, 1, 2, "2", 0, 1, 3, 2, 3, 4, 5, 0, 1, 2, 4, 7, 5, 6, 8, 3, 4, 5, 6, 7, 8, 6, 8, 7,
+)
 
 
 def split(value):
@@ -46,32 +48,6 @@
     return sum((lax.div(info[i], local_blocks) == info[NBLK + 1]).astype(jnp.int32) for i in range(NBLK))
 
 
-def columns_kernel(info, psi_ref, hpsi_ref, out_ref):
-    out_ref[0, :BLOCK, :] = psi_ref[...].T
-    out_ref[0, BLOCK:, :] = hpsi_ref[...].T
-
-
-def block_columns(wavefunctions, h_wavefunctions, info, local_blocks):
-    nodes = wavefunctions.shape[0]
-    count = NBLK - 1
-    source = pl.BlockSpec((nodes, BLOCK), lambda i, info: (0, ranked(info, i, local_blocks)[0]))
-    return pl.pallas_call(
-        columns_kernel,
-        grid_spec=pltpu.PrefetchScalarGridSpec(
-            num_scalar_prefetch=1,
-            grid=(count,),
-            in_specs=[source, source],
-            out_specs=pl.BlockSpec((1, 2 * BLOCK, nodes), lambda i, info: (i, 0, 0)),
-        ),
-        out_shape=jax.ShapeDtypeStruct((count, 2 * BLOCK, nodes), jnp.float32),
-        compiler_params=pltpu.CompilerParams(vmem_limit_bytes=VMEM),
-        cost_estimate=pl.CostEstimate(
-            flops=0, bytes_accessed=count * 4 * BLOCK * nodes * 4, transcendentals=0
-        ),
-        name="block_columns",
-    )(info, wavefunctions, h_wavefunctions)
-
-
 def bit_of(step, axis):
     shift = {"y": 2, "z": 1, "w": 0}[axis]
     return (step >> shift) & 1
@@ -85,13 +61,20 @@
     return jnp.where(step & bit, before + bit - 1, step)
 
 
-def partial_kernel(info, own_ref, other_ref, states_ref, token_ref, *refs, outs, pieces, local_blocks):
-    del token_ref
-    out_refs, (columns_ref, stack_ref, block_ref, columns_sem, sem) = refs[: len(outs)], refs[len(outs) :]
-    width = columns_ref.shape[0]
+def partial_kernel(info, *refs, outs, first, local_blocks):
+    states_ref, refs = refs[0], refs[1:]
+    if first == 0:
+        source_refs, refs = refs[:1], refs[1:]
+    else:
+        source_refs, refs = refs[:2], refs[3:]
+    out_refs, refs = refs[: len(outs)], refs[len(outs) :]
+    if first == 0:
+        own_ref, *refs, held_ref, held_sem, own_sem = refs
+    columns_ref, stack_ref, block_ref, columns_sem, sem = refs
+    blocks = columns_ref.shape[0]
+    width = blocks * BLOCK
     share_rows = block_ref.shape[2] // 2
     step = pl.program_id(0)
-    slot = step % BUFFERS
 
     def fetch(at):
         copies = []
@@ -107,43 +90,77 @@
             )
         return copies
 
+    def gather(rank, which):
+        place = ranked(info, rank, local_blocks)[0]
+        columns = pl.ds(pl.multiple_of(place * BLOCK, BLOCK), BLOCK)
+        source = (states_ref, source_refs[0])[which]
+        return pltpu.make_async_copy(source.at[:, columns], held_ref.at[rank, which], held_sem.at[rank, which])
+
+    def hand_over():
+        return pltpu.make_async_copy(held_ref, own_ref, own_sem)
+
     @pl.when(step == 0)
     def _():
-        for ahead in range(BUFFERS - 1):
+        mine = owned_count(info, local_blocks)
+        for block in range(blocks):
+            rank, which = divmod(first // BLOCK + block, 2)
+            here, semaphore = columns_ref.at[block], columns_sem.at[block]
+
+            def bring(source, at):
+                pltpu.make_async_copy(source.at[at, which], here, semaphore).start()
+
+            if first == 0:
+                gather(rank, which).start()
+            else:
+                pl.when(rank < mine)(functools.partial(bring, source_refs[0], min(rank, NBLK - 2)))
+                pl.when(rank >= mine)(
+                    functools.partial(bring, source_refs[1], jnp.clip(rank - mine, 0, NBLK - 2))
+                )
+        for ahead in range(BUFFERS):
             for copy in fetch(ahead):
                 copy.start()
-        mine = owned_count(info, local_blocks)
-        row = 0
-        for number, (rank, first, rows) in enumerate(pieces):
-            here = columns_ref.at[pl.ds(row, rows)]
-            row += rows
-
-            @pl.when(rank < mine)
-            def _():
-                source = own_ref.at[min(rank, NBLK - 2), pl.ds(first, rows)]
-                pltpu.make_async_copy(source, here, columns_sem.at[number]).start()
-
-            @pl.when(rank >= mine)
-            def _():
-                source = other_ref.at[jnp.clip(rank - mine, 0, NBLK - 2), pl.ds(first, rows)]
-                pltpu.make_async_copy(source, here, columns_sem.at[number]).start()
-
-        row = 0
-        for number, (rank, first, rows) in enumerate(pieces):
-            here = columns_ref.at[pl.ds(row, rows)]
-            row += rows
-            pltpu.make_async_copy(here, here, columns_sem.at[number]).wait()
-        stack_ref[:width], stack_ref[width:] = split(columns_ref[...])
-
-    @pl.when(step + BUFFERS - 1 < STEPS)
+        if first == 0:
+            for block in range(blocks, 2 * (NBLK - 1)):
+                gather(*divmod(block, 2)).start()
+        for block in range(blocks):
+            if first == 0:
+                gather(*divmod(block, 2)).wait()
+                columns = held_ref[block // 2, block % 2]
+            else:
+                here = columns_ref.at[block]
+                pltpu.make_async_copy(here, here, columns_sem.at[block]).wait()
+                columns = columns_ref[block]
+            rows = pl.ds(block * BLOCK, BLOCK)
+            low_rows = pl.ds(width + block * BLOCK, BLOCK)
+            stack_ref[rows], stack_ref[low_rows] = split(columns.T)
+
+    @pl.when((step >= 1) & (step + BUFFERS - 1 < STEPS))
     def _():
         for copy in fetch(step + BUFFERS - 1):
             copy.start()
 
     for copy in fetch(step):
         copy.wait()
+    multiply(step, block_ref.at[step % BUFFERS], stack_ref, outs, out_refs)
+
+    if first == 0:
+
+        @pl.when(step == STEPS // 2)
+        def _():
+            for block in range(blocks, 2 * (NBLK - 1)):
+                gather(*divmod(block, 2)).wait()
+            hand_over().start()
+
+        @pl.when(step == STEPS - 1)
+        def _():
+            hand_over().wait()
+
+
+def multiply(step, block_ref, stack_ref, outs, out_refs):
+    width = stack_ref.shape[0] // 2
+    share_rows = block_ref.shape[1] // 2
     dot = functools.partial(jnp.dot, preferred_element_type=jnp.float32)
-    high, low = split(block_ref[slot])
+    high, low = split(block_ref[...])
     both = dot(stack_ref[...], high)
     result = both[:width] + (both[width:] + dot(stack_ref[:width], low))
     halves = (result[:, :share_rows], result[:, share_rows:])
@@ -160,7 +177,7 @@
                 out_ref[index] = halves[half][start : start + size]
 
 
-def partial_sums(wavefunctions, own, other, info, share_rows, parts, first, token):
+def partial_sums(wavefunctions, sources, info, share_rows, parts, first):
     nodes = wavefunctions.shape[0]
     width = sum(size for _, size in parts)
     outs = []
@@ -169,13 +186,6 @@
         for bits, size in parts:
             outs.append((bits, start, size, sent))
             start += size
-    pieces = []
-    at = first
-    while at < first + width:
-        rank, row = divmod(at, 2 * BLOCK)
-        rows = min(2 * BLOCK - row, first + width - at)
-        pieces.append((rank, row, rows))
-        at += rows
 
     def spec(bits, start, size, sent):
         def index(step, info):
@@ -185,24 +195,39 @@
 
         return pl.BlockSpec((*(2 if b == "x" else 1 for b in bits[1:]), size, share_rows), index)
 
+    columns = []
+    if first == 0:
+        columns = [jax.ShapeDtypeStruct((NBLK - 1, 2, nodes, BLOCK), jnp.float32)]
     made = pl.pallas_call(
         functools.partial(
-            partial_kernel, outs=outs, pieces=pieces, local_blocks=wavefunctions.shape[1] // BLOCK
+            partial_kernel,
+            outs=outs,
+            first=first,
+            local_blocks=wavefunctions.shape[1] // BLOCK,
         ),
         grid_spec=pltpu.PrefetchScalarGridSpec(
             num_scalar_prefetch=1,
             grid=(STEPS,),
-            in_specs=[pl.BlockSpec(memory_space=pl.ANY)] * 4,
-            out_specs=[spec(*out) for out in outs],
+            in_specs=[pl.BlockSpec(memory_space=pl.ANY)] * (len(sources) + 1),
+            out_specs=[spec(*out) for out in outs] + [pl.BlockSpec(memory_space=pl.ANY)] * len(columns),
             scratch_shapes=[
-                pltpu.VMEM((width, nodes), jnp.float32),
+                pltpu.VMEM((width // BLOCK, nodes, BLOCK), jnp.float32),
                 pltpu.VMEM((2 * width, nodes), jnp.bfloat16),
                 pltpu.VMEM((BUFFERS, nodes, 2 * share_rows), jnp.float32),
-                pltpu.SemaphoreType.DMA((len(pieces),)),
+                pltpu.SemaphoreType.DMA((width // BLOCK,)),
                 pltpu.SemaphoreType.DMA((BUFFERS, 2)),
+            ]
+            + [
+                scratch
+                for shape in columns
+                for scratch in (
+                    pltpu.VMEM(shape.shape, shape.dtype),
+                    pltpu.SemaphoreType.DMA((NBLK - 1, 2)),
+                    pltpu.SemaphoreType.DMA,
+                )
             ],
         ),
-        out_shape=[jax.ShapeDtypeStruct((2, 2, 2, out[2], share_rows), jnp.float32) for out in outs],
+        out_shape=[jax.ShapeDtypeStruct((2, 2, 2, out[2], share_rows), jnp.float32) for out in outs] + columns,
         compiler_params=pltpu.CompilerParams(vmem_limit_bytes=VMEM),
         cost_estimate=pl.CostEstimate(
             flops=12 * STEPS * width * share_rows * nodes,
@@ -210,8 +235,8 @@
             transcendentals=0,
         ),
         name="partial_sums",
-    )(info, own, other, wavefunctions, token)
-    return [m.reshape(8, *m.shape[3:]) for m in made]
+    )(info, wavefunctions, *sources)
+    return [m.reshape(8, *m.shape[3:]) for m in made[: len(outs)]] + list(made[len(outs) :])
 
 
 def total(leaves, at):
@@ -293,19 +318,18 @@
     local_blocks = local_states // BLOCK
     info = jnp.concatenate([block_ids, lax.axis_index("node")[None], lax.axis_index("state")[None]])
 
-    own = block_columns(wavefunctions, h_wavefunctions, info, local_blocks)
-    other = swap_cores(own)
-    last = own
-    held, sizes = {}, {}
+    held = {}
     first = 0
     for step in ORDER:
         if isinstance(step, str):
             group = int(step)
             parts = GROUPS[group]
-            out = partial_sums(
-                wavefunctions, own, other if group else own, info, share_rows, parts, first, last
-            )
+            sources = [own, other, last] if group else [h_wavefunctions]
+            out = partial_sums(wavefunctions, sources, info, share_rows, parts, first)
             last = out[0]
+            if group == 0:
+                own = out.pop()
+                other = swap_cores(own)
             first += sum(size for _, size in parts)
             sent, kept = out[: len(parts)], out[len(parts) :]
             for (bits, size), send, keep in zip(parts, sent, kept):

time: 193 us -> 180 us (0.933)
  waiting for transfers between devices: 94 us -> 70.4 us
  starting transfers between devices: 37.9 us -> 51.1 us
  Pallas kernels: 56.6 us -> 52.3 us
    ppermute x36, waiting for transfers between devices: 94 us -> 70.4 us  [swap(): lax.ppermute(value, 'node', [(i, i ^ bit) for i in range(lax.axis_size('n...]
    ppermute x36, starting transfers between devices: 37.4 us -> 50.6 us  [swap(): lax.ppermute(value, 'node', [(i, i ^ bit) for i in range(lax.axis_size('n...]
    pallas_call x4 -> x3, Pallas kernels: 52.4 us -> 48 us  [partial_sums(): pl.pallas_call(functools.partial(partial_kernel, outs=outs, first=first,...]
  transfers between devices with their start and end apart: 37 -> 37, of which waited for: 20 -> 16; matrix products, arithmetic and copies ran while one was open for 0% -> 0% of each run, Pallas kernels for 26% -> 21%
where the time goes in v3:
time: 180 us; the launch traced here: 179 us
  waiting for transfers between devices  70.4 us (39%)
  Pallas kernels  52.3 us (29%)
  starting transfers between devices  51.1 us (28%)
  local copies, waits for them, and re-layouts  2.98 us (2%)
    ppermute x36, waiting for transfers between devices, swap(): lax.ppermute(value, 'node', [(i, i ^ bit) for i in range(lax.axis_size('n...  70.4 us
    ppermute x36, starting transfers between devices, swap(): lax.ppermute(value, 'node', [(i, i ^ bit) for i in range(lax.axis_size('n...  50.6 us
    pallas_call x3, Pallas kernels, partial_sums(): pl.pallas_call(functools.partial(partial_kernel, outs=outs, first=first,...  48 us
  transfers between devices with their start and end apart: 37, of which 16 were waited for; matrix products, arithmetic and copies ran while one was open for 0% of the time, Pallas kernels for 21%

profile of v3, /device:TPU:0, one launch (start us, length us, event | category | flops | bytes accessed | tf_op | source)
XLA Modules:
  0.0 178.9 jit_solution(2229203591140028297)
XLA Ops:
  1.4 12.8 %partial_sums.3 = (f32[2,2,2,88,256]{4,3,2,1,0:T(8,128)S(1)}, f32[2,2,2,88,256]{4,3,2,1,0:T(8,128)S(1)}, f32[2,2,2,80,256]{4,3,2,1,0:T(8,128)S(1)}, f32[2,2,2,88...) custom-call(s32[6]{0:T(128)S(1)} %pad_add_fusion.info, ...), custom_call_target="tpu_custom_call" | custom-call | flops 6442450944 | bytes 20971520 | tf_op jit(solution)/shard_map/partial_sums/pallas_call | solution.py:201
  14.7 2.7 %collective-permute-start.3 = (f32[8,80,256]{2,1,0:T(8,128)S(1)}, f32[8,80,256]{2,1,0:T(8,128)S(1)}, u32[]{:S(2)}, u32[]{:S(2)}) collective-permute-start(f32[8,80,256]{2,1,0:T(8,128)S(1)} %bitcast.103), channel_id=1, source_target_pairs={{0,8},{2,10},{4,12},{6,14},{8,0},{10,2},{12,4},{14,6},{16,24},{18,... | collective-permute-start | bytes 1966088 | tf_op jit(solution)/shard_map/ppermute | solution.py:294
  18.8 1.5 collective-permute-start.4
  20.3 17.6 %partial_sums.4 = (f32[2,2,2,128,256]{4,3,2,1,0:T(8,128)S(1)}, f32[2,2,2,136,256]{4,3,2,1,0:T(8,128)}, f32[2,2,2,120,256]{4,3,2,1,0:T(8,128)}, f32[2,2,2,128,256...) custom-call(s32[6]{0:T(128)S(1)} %pad_add_fusion.info, f32[1024,4096]{1,0:T(8,128)} %refs_0_.5, ...), custom_call_target="tpu_custom_call" | custom-call | flops 9663676416 | bytes 23068672 | tf_op jit(solution)/shard_map/partial_sums/pallas_call | solution.py:201
  38.1 2.9 %collective-permute-start.2 = (f32[4,88,256]{2,1,0:T(8,128)S(1)}, f32[4,88,256]{2,1,0:T(8,128)S(1)}, u32[]{:S(2)}, u32[]{:S(2)}) collective-permute-start(f32[4,88,256]{2,1,0:T(8,128)S(1)} %add_up.27.refs_2_), channel_id=1, source_target_pairs={{0,4},{2,6},{4,0},{6,2},{8,12},{10,14},{12,8},{14,10},{16,20},{18,... | collective-permute-start | bytes 1081352 | tf_op jit(solution)/shard_map/ppermute | solution.py:294
  43.3 2.7 %collective-permute-start.11 = (f32[4,80,256]{2,1,0:T(8,128)S(1)}, f32[4,80,256]{2,1,0:T(8,128)S(1)}, u32[]{:S(2)}, u32[]{:S(2)}) collective-permute-start(f32[4,80,256]{2,1,0:T(8,128)S(1)} %add_up.29.refs_3_), channel_id=1, source_target_pairs={{0,16},{2,18},{4,20},{6,22},{8,24},{10,26},{12,28},{14,30},{16,0},... | collective-permute-start | bytes 983048 | tf_op jit(solution)/shard_map/ppermute | solution.py:294
  45.9 1.6 collective-permute-start.6
  47.5 2.5 %collective-permute-done.2.refs_2_ = f32[4,88,256]{2,1,0:T(8,128)S(1)} collective-permute-done((f32[4,88,256]{2,1,0:T(8,128)S(1)}, f32[4,88,256]{2,1,0:T(8,128)S(1)}, u32[]{:S(2)}, u32[]{:S(2)}) %collective-permute-start.2) | collective-permute-done | bytes 360480 | tf_op jit(solution)/shard_map/ppermute | solution.py:294
  50.0 1.7 collective-permute-start.7
  51.7 17.7 %partial_sums.5 = (f32[2,2,2,144,256]{4,3,2,1,0:T(8,128)}, f32[2,2,2,112,256]{4,3,2,1,0:T(8,128)S(1)}, f32[2,2,2,128,256]{4,3,2,1,0:T(8,128)S(1)}, f32[2,2,2,144...) custom-call(s32[6]{0:T(128)S(1)} %pad_add_fusion.info, ...), custom_call_target="tpu_custom_call" | custom-call | flops 9663676416 | bytes 23068672 | tf_op jit(solution)/shard_map/partial_sums/pallas_call | solution.py:201
  70.7 3.2 %collective-permute-done.9.refs_2_ = f32[4,88,256]{2,1,0:T(8,128)S(1)} collective-permute-done((f32[4,88,256]{2,1,0:T(8,128)S(1)}, f32[4,88,256]{2,1,0:T(8,128)S(1)}, u32[]{:S(2)}, u32[]{:S(2)}) %collective-permute-start.9) | collective-permute-done | bytes 360480 | tf_op jit(solution)/shard_map/ppermute | solution.py:294
  74.0 1.6 collective-permute-start.13
  82.0 8.7 %collective-permute-done.10.refs_2_ = f32[4,128,256]{2,1,0:T(8,128)S(1)} collective-permute-done((f32[4,128,256]{2,1,0:T(8,128)S(1)}, f32[4,128,256]{2,1,0:T(8,128)S(1)}, u32[]{:S(2)}, u32[]{:S(2)}) %collective-permute-start.10) | collective-permute-done | bytes 524320 | tf_op jit(solution)/shard_map/ppermute | solution.py:294
  92.6 1.6 collective-permute-start.22
  94.3 13.7 %collective-permute-done.5.refs_3_ = f32[2,88,256]{2,1,0:T(8,128)S(1)} collective-permute-done((f32[2,88,256]{2,1,0:T(8,128)S(1)}, f32[2,88,256]{2,1,0:T(8,128)S(1)}, u32[]{:S(2)}, u32[]{:S(2)}) %collective-permute-start.5) | collective-permute-done | bytes 180256 | tf_op jit(solution)/shard_map/ppermute | solution.py:294
  110.0 12.4 %collective-permute-done.15.refs_3_ = f32[2,80,256]{2,1,0:T(8,128)S(1)} collective-permute-done((f32[2,80,256]{2,1,0:T(8,128)S(1)}, f32[2,80,256]{2,1,0:T(8,128)S(1)}, u32[]{:S(2)}, u32[]{:S(2)}) %collective-permute-start.15) | collective-permute-done | bytes 163872 | tf_op jit(solution)/shard_map/ppermute | solution.py:294
  122.4 2.6 %collective-permute-start.12 = (f32[1,88,256]{2,1,0:T(8,128)S(1)}, f32[1,88,256]{2,1,0:T(8,128)S(1)}, u32[]{:S(2)}, u32[]{:S(2)}) collective-permute-start(f32[1,88,256]{2,1,0:T(8,128)S(1)} %add_up.37.refs_4_), channel_id=1, source_target_pairs={{0,16},{2,18},{4,20},{6,22},{8,24},{10,26},{12,28},{14,30},{16,0},... | collective-permute-start | bytes 270344 | tf_op jit(solution)/shard_map/ppermute | solution.py:294
  128.0 2.0 %collective-permute-done.12 = f32[1,88,256]{2,1,0:T(8,128)S(1)} collective-permute-done((f32[1,88,256]{2,1,0:T(8,128)S(1)}, f32[1,88,256]{2,1,0:T(8,128)S(1)}, u32[]{:S(2)}, u32[]{:S(2)}) %collective-permute-start.12) | collective-permute-done | bytes 90144 | tf_op jit(solution)/shard_map/ppermute | solution.py:294
  131.0 1.5 collective-permute-start.16
  132.7 2.4 %collective-permute-done.14 = f32[1,88,256]{2,1,0:T(8,128)S(1)} collective-permute-done((f32[1,88,256]{2,1,0:T(8,128)S(1)}, f32[1,88,256]{2,1,0:T(8,128)S(1)}, u32[]{:S(2)}, u32[]{:S(2)}) %collective-permute-start.14) | collective-permute-done | bytes 90144 | tf_op jit(solution)/shard_map/ppermute | solution.py:294
  139.3 2.8 %collective-permute-start.23 = (f32[1,128,256]{2,1,0:T(8,128)S(1)}, f32[1,128,256]{2,1,0:T(8,128)S(1)}, u32[]{:S(2)}, u32[]{:S(2)}) collective-permute-start(f32[1,128,256]{2,1,0:T(8,128)S(1)} %add_up.45.refs_4_), channel_id=1, source_target_pairs={{0,16},{2,18},{4,20},{6,22},{8,24},{10,26},{12,28},{14,30},{16,0},... | collective-permute-start | bytes 393224 | tf_op jit(solution)/shard_map/ppermute | solution.py:294
  142.2 1.8 collective-permute-done.26.refs_3_
  143.9 3.4 %collective-permute-start.25 = (f32[1,136,256]{2,1,0:T(8,128)S(1)}, f32[1,136,256]{2,1,0:T(8,128)S(1)}, u32[]{:S(2)}, u32[]{:S(2)}) collective-permute-start(f32[1,136,256]{2,1,0:T(8,128)S(1)} %add_up.46.refs_4_), channel_id=1, source_target_pairs={{0,16},{2,18},{4,20},{6,22},{8,24},{10,26},{12,28},{14,30},{16,0},... | collective-permute-start | bytes 417800 | tf_op jit(solution)/shard_map/ppermute | solution.py:294
  147.5 1.8 %collective-permute-done.23 = f32[1,128,256]{2,1,0:T(8,128)S(1)} collective-permute-done((f32[1,128,256]{2,1,0:T(8,128)S(1)}, f32[1,128,256]{2,1,0:T(8,128)S(1)}, u32[]{:S(2)}, u32[]{:S(2)}) %collective-permute-start.23) | collective-permute-done | bytes 131104 | tf_op jit(solution)/shard_map/ppermute | solution.py:294
  149.5 8.9 %collective-permute-done.31.refs_2_ = f32[4,112,256]{2,1,0:T(8,128)S(1)} collective-permute-done((f32[4,112,256]{2,1,0:T(8,128)S(1)}, f32[4,112,256]{2,1,0:T(8,128)S(1)}, u32[]{:S(2)}, u32[]{:S(2)}) %collective-permute-start.31) | collective-permute-done | bytes 458784 | tf_op jit(solution)/shard_map/ppermute | solution.py:294
  158.6 2.0 %collective-permute-start.34 = (f32[2,128,256]{2,1,0:T(8,128)S(1)}, f32[2,128,256]{2,1,0:T(8,128)S(1)}, u32[]{:S(2)}, u32[]{:S(2)}) collective-permute-start(f32[2,128,256]{2,1,0:T(8,128)S(1)} %add_up.50.refs_4_), channel_id=1, source_target_pairs={{0,4},{2,6},{4,0},{6,2},{8,12},{10,14},{12,8},{14,10},{16,20},{18,... | collective-permute-start | bytes 786440 | tf_op jit(solution)/shard_map/ppermute | solution.py:294
  162.0 2.9 %collective-permute-done.34.refs_3_ = f32[2,128,256]{2,1,0:T(8,128)S(1)} collective-permute-done((f32[2,128,256]{2,1,0:T(8,128)S(1)}, f32[2,128,256]{2,1,0:T(8,128)S(1)}, u32[]{:S(2)}, u32[]{:S(2)}) %collective-permute-start.34) | collective-permute-done | bytes 262176 | tf_op jit(solution)/shard_map/ppermute | solution.py:294
  165.0 3.1 %collective-permute-start.36 = (f32[1,128,256]{2,1,0:T(8,128)S(1)}, f32[1,128,256]{2,1,0:T(8,128)S(1)}, u32[]{:S(2)}, u32[]{:S(2)}) collective-permute-start(f32[1,128,256]{2,1,0:T(8,128)S(1)} %add_up.52.refs_4_), channel_id=1, source_target_pairs={{0,16},{2,18},{4,20},{6,22},{8,24},{10,26},{12,28},{14,30},{16,0},... | collective-permute-start | bytes 393224 | tf_op jit(solution)/shard_map/ppermute | solution.py:294
  168.2 1.7 collective-permute-done.33.refs_3_
  170.0 2.6 %collective-permute-done.32 = f32[1,144,256]{2,1,0:T(8,128)S(1)} collective-permute-done((f32[1,144,256]{2,1,0:T(8,128)S(1)}, f32[1,144,256]{2,1,0:T(8,128)S(1)}, u32[]{:S(2)}, u32[]{:S(2)}) %collective-permute-start.32) | collective-permute-done | bytes 147488 | tf_op jit(solution)/shard_map/ppermute | solution.py:294
  172.6 3.8 %collective-permute-done.35 = f32[1,112,256]{2,1,0:T(8,128)S(1)} collective-permute-done((f32[1,112,256]{2,1,0:T(8,128)S(1)}, f32[1,112,256]{2,1,0:T(8,128)S(1)}, u32[]{:S(2)}, u32[]{:S(2)}) %collective-permute-start.35) | collective-permute-done | bytes 114720 | tf_op jit(solution)/shard_map/ppermute | solution.py:294
  176.5 2.4 %place_columns.1 = (f32[256,512]{1,0:T(8,128)}, f32[256,512]{1,0:T(8,128)}) custom-call(s32[6]{0:T(128)S(1)} %pad_add_fusion.info, f32[4,256,256]{2,1,0:T(8,128)S(1)} %bitcast.93), custom_call_target="tpu_custom_call" | custom-call | tf_op jit(solution)/shard_map/place_columns/pallas_call | solution.py:278
  (97 shorter events, 27.2 us)
Async XLA Ops:
  14.7 28.5 %collective-permute-start.3 = (f32[8,80,256]{2,1,0:T(8,128)S(1)}, f32[8,80,256]{2,1,0:T(8,128)S(1)}, u32[]{:S(2)}, u32[]{:S(2)}) collective-permute-start(f32[8,80,256]{2,1,0:T(8,128)S(1)} %bitcast.103), channel_id=1, source_target_pairs={{0,8},{2,10},{4,12},{6,14},{8,0},{10,2},{12,4},{14,6},{16,24},{18,... | collective-permute-start | bytes 1966088 | tf_op jit(solution)/shard_map/ppermute | solution.py:294
  17.3 20.6 %collective-permute-start = (f32[8,88,256]{2,1,0:T(8,128)S(1)}, f32[8,88,256]{2,1,0:T(8,128)S(1)}, u32[]{:S(2)}, u32[]{:S(2)}) collective-permute-start(f32[8,88,256]{2,1,0:T(8,128)S(1)} %bitcast.101), channel_id=1, source_target_pairs={{0,2},{2,0},{4,6},{6,4},{8,10},{10,8},{12,14},{14,12},{16,18},{18,... | collective-permute-start | bytes 2162696 | tf_op jit(solution)/shard_map/ppermute | solution.py:294
  18.8 23.7 %collective-permute-start.4 = (f32[8,88,256]{2,1,0:T(8,128)S(1)}, f32[8,88,256]{2,1,0:T(8,128)S(1)}, u32[]{:S(2)}, u32[]{:S(2)}) collective-permute-start(f32[8,88,256]{2,1,0:T(8,128)S(1)} %bitcast.100), channel_id=1, source_target_pairs={{0,4},{2,6},{4,0},{6,2},{8,12},{10,14},{12,8},{14,10},{16,20},{18,... | collective-permute-start | bytes 2162696 | tf_op jit(solution)/shard_map/ppermute | solution.py:294
  38.1 11.9 %collective-permute-start.2 = (f32[4,88,256]{2,1,0:T(8,128)S(1)}, f32[4,88,256]{2,1,0:T(8,128)S(1)}, u32[]{:S(2)}, u32[]{:S(2)}) collective-permute-start(f32[4,88,256]{2,1,0:T(8,128)S(1)} %add_up.27.refs_2_), channel_id=1, source_target_pairs={{0,4},{2,6},{4,0},{6,2},{8,12},{10,14},{12,8},{14,10},{16,20},{18,... | collective-permute-start | bytes 1081352 | tf_op jit(solution)/shard_map/ppermute | solution.py:294
  41.0 34.7 %collective-permute-start.8 = (f32[8,128,256]{2,1,0:T(8,128)S(1)}, f32[8,128,256]{2,1,0:T(8,128)S(1)}, u32[]{:S(2)}, u32[]{:S(2)}) collective-permute-start(f32[8,128,256]{2,1,0:T(8,128)S(1)} %bitcast.97), channel_id=1, source_target_pairs={{0,2},{2,0},{4,6},{6,4},{8,10},{10,8},{12,14},{14,12},{16,18},{18,... | collective-permute-start | bytes 3145736 | tf_op jit(solution)/shard_map/ppermute | solution.py:294
  42.6 31.3 %collective-permute-start.9 = (f32[4,88,256]{2,1,0:T(8,128)S(1)}, f32[4,88,256]{2,1,0:T(8,128)S(1)}, u32[]{:S(2)}, u32[]{:S(2)}) collective-permute-start(f32[4,88,256]{2,1,0:T(8,128)S(1)} %add_up.28.refs_2_), channel_id=1, source_target_pairs={{0,2},{2,0},{4,6},{6,4},{8,10},{10,8},{12,14},{14,12},{16,18},{18,... | collective-permute-start | bytes 1081352 | tf_op jit(solution)/shard_map/ppermute | solution.py:294
  43.3 33.1 %collective-permute-start.11 = (f32[4,80,256]{2,1,0:T(8,128)S(1)}, f32[4,80,256]{2,1,0:T(8,128)S(1)}, u32[]{:S(2)}, u32[]{:S(2)}) collective-permute-start(f32[4,80,256]{2,1,0:T(8,128)S(1)} %add_up.29.refs_3_), channel_id=1, source_target_pairs={{0,16},{2,18},{4,20},{6,22},{8,24},{10,26},{12,28},{14,30},{16,0},... | collective-permute-start | bytes 983048 | tf_op jit(solution)/shard_map/ppermute | solution.py:294
  45.9 46.6 %collective-permute-start.6 = (f32[8,120,256]{2,1,0:T(8,128)}, f32[8,120,256]{2,1,0:T(8,128)S(1)}, u32[]{:S(2)}, u32[]{:S(2)}) collective-permute-start(f32[8,120,256]{2,1,0:T(8,128)} %bitcast.11), channel_id=1, source_target_pairs={{0,8},{2,10},{4,12},{6,14},{8,0},{10,2},{12,4},{14,6},{16,24},{18,... | collective-permute-start | bytes 2949128 | tf_op jit(solution)/shard_map/ppermute | solution.py:294
  50.0 30.5 %collective-permute-start.7 = (f32[8,136,256]{2,1,0:T(8,128)}, f32[8,136,256]{2,1,0:T(8,128)S(1)}, u32[]{:S(2)}, u32[]{:S(2)}) collective-permute-start(f32[8,136,256]{2,1,0:T(8,128)} %bitcast.13), channel_id=1, source_target_pairs={{0,4},{2,6},{4,0},{6,2},{8,12},{10,14},{12,8},{14,10},{16,20},{18,... | collective-permute-start | bytes 3342344 | tf_op jit(solution)/shard_map/ppermute | solution.py:294
  75.8 14.9 %collective-permute-start.10 = (f32[4,128,256]{2,1,0:T(8,128)S(1)}, f32[4,128,256]{2,1,0:T(8,128)S(1)}, u32[]{:S(2)}, u32[]{:S(2)}) collective-permute-start(f32[4,128,256]{2,1,0:T(8,128)S(1)} %add_up.32.refs_3_), channel_id=1, source_target_pairs={{0,4},{2,6},{4,0},{6,2},{8,12},{10,14},{12,8},{14,10},{16,20},{18,... | collective-permute-start | bytes 1572872 | tf_op jit(solution)/shard_map/ppermute | solution.py:294
  76.9 49.6 %collective-permute-start.19 = (f32[8,144,256]{2,1,0:T(8,128)S(1)}, f32[8,144,256]{2,1,0:T(8,128)S(1)}, u32[]{:S(2)}, u32[]{:S(2)}) collective-permute-start(f32[8,144,256]{2,1,0:T(8,128)S(1)} %bitcast.95), channel_id=1, source_target_pairs={{0,2},{2,0},{4,6},{6,4},{8,10},{10,8},{12,14},{14,12},{16,18},{18,... | collective-permute-start | bytes 3538952 | tf_op jit(solution)/shard_map/ppermute | solution.py:294
  79.9 29.1 %collective-permute-start.21 = (f32[8,112,256]{2,1,0:T(8,128)S(1)}, f32[8,112,256]{2,1,0:T(8,128)S(1)}, u32[]{:S(2)}, u32[]{:S(2)}) collective-permute-start(f32[8,112,256]{2,1,0:T(8,128)S(1)} %bitcast.99), channel_id=1, source_target_pairs={{0,4},{2,6},{4,0},{6,2},{8,12},{10,14},{12,8},{14,10},{16,20},{18,... | collective-permute-start | bytes 2752520 | tf_op jit(solution)/shard_map/ppermute | solution.py:294
  80.5 50.5 %collective-permute-start.18 = (f32[8,128,256]{2,1,0:T(8,128)S(1)}, f32[8,128,256]{2,1,0:T(8,128)S(1)}, u32[]{:S(2)}, u32[]{:S(2)}) collective-permute-start(f32[8,128,256]{2,1,0:T(8,128)S(1)} %bitcast.98), channel_id=1, source_target_pairs={{0,8},{2,10},{4,12},{6,14},{8,0},{10,2},{12,4},{14,6},{16,24},{18,... | collective-permute-start | bytes 3145736 | tf_op jit(solution)/shard_map/ppermute | solution.py:294
  90.7 17.3 %collective-permute-start.5 = (f32[2,88,256]{2,1,0:T(8,128)S(1)}, f32[2,88,256]{2,1,0:T(8,128)S(1)}, u32[]{:S(2)}, u32[]{:S(2)}) collective-permute-start(f32[2,88,256]{2,1,0:T(8,128)S(1)} %add_up.30.refs_3_), channel_id=1, source_target_pairs={{0,8},{2,10},{4,12},{6,14},{8,0},{10,2},{12,4},{14,6},{16,24},{18,... | collective-permute-start | bytes 540680 | tf_op jit(solution)/shard_map/ppermute | solution.py:294
  92.6 32.5 %collective-permute-start.22 = (f32[4,136,256]{2,1,0:T(8,128)S(1)}, f32[4,136,256]{2,1,0:T(8,128)S(1)}, u32[]{:S(2)}, u32[]{:S(2)}) collective-permute-start(f32[4,136,256]{2,1,0:T(8,128)S(1)} %add_up.35.refs_2_), channel_id=1, source_target_pairs={{0,2},{2,0},{4,6},{6,4},{8,10},{10,8},{12,14},{14,12},{16,18},{18,... | collective-permute-start | bytes 1671176 | tf_op jit(solution)/shard_map/ppermute | solution.py:294
  108.0 18.0 %collective-permute-start.20 = (f32[4,120,256]{2,1,0:T(8,128)S(1)}, f32[4,120,256]{2,1,0:T(8,128)S(1)}, u32[]{:S(2)}, u32[]{:S(2)}) collective-permute-start(f32[4,120,256]{2,1,0:T(8,128)S(1)} %add_up.36.refs_4_), channel_id=1, source_target_pairs={{0,4},{2,6},{4,0},{6,2},{8,12},{10,14},{12,8},{14,10},{16,20},{18,... | collective-permute-start | bytes 1474568 | tf_op jit(solution)/shard_map/ppermute | solution.py:294
  109.0 13.5 %collective-permute-start.15 = (f32[2,80,256]{2,1,0:T(8,128)S(1)}, f32[2,80,256]{2,1,0:T(8,128)S(1)}, u32[]{:S(2)}, u32[]{:S(2)}) collective-permute-start(f32[2,80,256]{2,1,0:T(8,128)S(1)} %add_up.33.refs_3_), channel_id=1, source_target_pairs={{0,4},{2,6},{4,0},{6,2},{8,12},{10,14},{12,8},{14,10},{16,20},{18,... | collective-permute-start | bytes 491528 | tf_op jit(solution)/shard_map/ppermute | solution.py:294
  122.4 7.6 %collective-permute-start.12 = (f32[1,88,256]{2,1,0:T(8,128)S(1)}, f32[1,88,256]{2,1,0:T(8,128)S(1)}, u32[]{:S(2)}, u32[]{:S(2)}) collective-permute-start(f32[1,88,256]{2,1,0:T(8,128)S(1)} %add_up.37.refs_4_), channel_id=1, source_target_pairs={{0,16},{2,18},{4,20},{6,22},{8,24},{10,26},{12,28},{14,30},{16,0},... | collective-permute-start | bytes 270344 | tf_op jit(solution)/shard_map/ppermute | solution.py:294
  125.0 11.5 %collective-permute-start.17 = (f32[2,128,256]{2,1,0:T(8,128)S(1)}, f32[2,128,256]{2,1,0:T(8,128)S(1)}, u32[]{:S(2)}, u32[]{:S(2)}) collective-permute-start(f32[2,128,256]{2,1,0:T(8,128)S(1)} %add_up.34.refs_2_), channel_id=1, source_target_pairs={{0,8},{2,10},{4,12},{6,14},{8,0},{10,2},{12,4},{14,6},{16,24},{18,... | collective-permute-start | bytes 786440 | tf_op jit(solution)/shard_map/ppermute | solution.py:294
  126.0 9.1 %collective-permute-start.14 = (f32[1,88,256]{2,1,0:T(8,128)S(1)}, f32[1,88,256]{2,1,0:T(8,128)S(1)}, u32[]{:S(2)}, u32[]{:S(2)}) collective-permute-start(f32[1,88,256]{2,1,0:T(8,128)S(1)} %add_up.38.refs_4_), channel_id=1, source_target_pairs={{0,16},{2,18},{4,20},{6,22},{8,24},{10,26},{12,28},{14,30},{16,0},... | collective-permute-start | bytes 270344 | tf_op jit(solution)/shard_map/ppermute | solution.py:294
  126.5 12.8 %collective-permute-start.24 = (f32[2,136,256]{2,1,0:T(8,128)S(1)}, f32[2,136,256]{2,1,0:T(8,128)S(1)}, u32[]{:S(2)}, u32[]{:S(2)}) collective-permute-start(f32[2,136,256]{2,1,0:T(8,128)S(1)} %add_up.40.refs_2_), channel_id=1, source_target_pairs={{0,8},{2,10},{4,12},{6,14},{8,0},{10,2},{12,4},{14,6},{16,24},{18,... | collective-permute-start | bytes 835592 | tf_op jit(solution)/shard_map/ppermute | solution.py:294
  130.1 17.3 %collective-permute-start.28 = (f32[4,144,256]{2,1,0:T(8,128)S(1)}, f32[4,144,256]{2,1,0:T(8,128)S(1)}, u32[]{:S(2)}, u32[]{:S(2)}) collective-permute-start(f32[4,144,256]{2,1,0:T(8,128)S(1)} %add_up.43.refs_2_), channel_id=1, source_target_pairs={{0,4},{2,6},{4,0},{6,2},{8,12},{10,14},{12,8},{14,10},{16,20},{18,... | collective-permute-start | bytes 1769480 | tf_op jit(solution)/shard_map/ppermute | solution.py:294
  135.0 8.9 %collective-permute-start.26 = (f32[2,120,256]{2,1,0:T(8,128)S(1)}, f32[2,120,256]{2,1,0:T(8,128)S(1)}, u32[]{:S(2)}, u32[]{:S(2)}) collective-permute-start(f32[2,120,256]{2,1,0:T(8,128)S(1)} %add_up.42.refs_2_), channel_id=1, source_target_pairs={{0,2},{2,0},{4,6},{6,4},{8,10},{10,8},{12,14},{14,12},{16,18},{18,... | collective-permute-start | bytes 737288 | tf_op jit(solution)/shard_map/ppermute | solution.py:294
  136.5 21.9 %collective-permute-start.30 = (f32[4,128,256]{2,1,0:T(8,128)S(1)}, f32[4,128,256]{2,1,0:T(8,128)S(1)}, u32[]{:S(2)}, u32[]{:S(2)}) collective-permute-start(f32[4,128,256]{2,1,0:T(8,128)S(1)} %add_up.44.refs_4_), channel_id=1, source_target_pairs={{0,2},{2,0},{4,6},{6,4},{8,10},{10,8},{12,14},{14,12},{16,18},{18,... | collective-permute-start | bytes 1572872 | tf_op jit(solution)/shard_map/ppermute | solution.py:294
  137.4 20.9 %collective-permute-start.31 = (f32[4,112,256]{2,1,0:T(8,128)S(1)}, f32[4,112,256]{2,1,0:T(8,128)S(1)}, u32[]{:S(2)}, u32[]{:S(2)}) collective-permute-start(f32[4,112,256]{2,1,0:T(8,128)S(1)} %add_up.41.refs_3_), channel_id=1, source_target_pairs={{0,2},{2,0},{4,6},{6,4},{8,10},{10,8},{12,14},{14,12},{16,18},{18,... | collective-permute-start | bytes 1376264 | tf_op jit(solution)/shard_map/ppermute | solution.py:294
  139.3 10.1 %collective-permute-start.23 = (f32[1,128,256]{2,1,0:T(8,128)S(1)}, f32[1,128,256]{2,1,0:T(8,128)S(1)}, u32[]{:S(2)}, u32[]{:S(2)}) collective-permute-start(f32[1,128,256]{2,1,0:T(8,128)S(1)} %add_up.45.refs_4_), channel_id=1, source_target_pairs={{0,16},{2,18},{4,20},{6,22},{8,24},{10,26},{12,28},{14,30},{16,0},... | collective-permute-start | bytes 393224 | tf_op jit(solution)/shard_map/ppermute | solution.py:294
  143.9 16.6 %collective-permute-start.25 = (f32[1,136,256]{2,1,0:T(8,128)S(1)}, f32[1,136,256]{2,1,0:T(8,128)S(1)}, u32[]{:S(2)}, u32[]{:S(2)}) collective-permute-start(f32[1,136,256]{2,1,0:T(8,128)S(1)} %add_up.46.refs_4_), channel_id=1, source_target_pairs={{0,16},{2,18},{4,20},{6,22},{8,24},{10,26},{12,28},{14,30},{16,0},... | collective-permute-start | bytes 417800 | tf_op jit(solution)/shard_map/ppermute | solution.py:294
  147.5 13.2 %collective-permute-start.29 = (f32[2,144,256]{2,1,0:T(8,128)S(1)}, f32[2,144,256]{2,1,0:T(8,128)S(1)}, u32[]{:S(2)}, u32[]{:S(2)}) collective-permute-start(f32[2,144,256]{2,1,0:T(8,128)S(1)} %add_up.48.refs_3_), channel_id=1, source_target_pairs={{0,8},{2,10},{4,12},{6,14},{8,0},{10,2},{12,4},{14,6},{16,24},{18,... | collective-permute-start | bytes 884744 | tf_op jit(solution)/shard_map/ppermute | solution.py:294
  149.4 12.6 %collective-permute-start.27 = (f32[1,120,256]{2,1,0:T(8,128)S(1)}, f32[1,120,256]{2,1,0:T(8,128)S(1)}, u32[]{:S(2)}, u32[]{:S(2)}) collective-permute-start(f32[1,120,256]{2,1,0:T(8,128)S(1)} %add_up.47.refs_3_), channel_id=1, source_target_pairs={{0,16},{2,18},{4,20},{6,22},{8,24},{10,26},{12,28},{14,30},{16,0},... | collective-permute-start | bytes 368648 | tf_op jit(solution)/shard_map/ppermute | solution.py:294
  160.6 9.2 %collective-permute-start.33 = (f32[2,112,256]{2,1,0:T(8,128)S(1)}, f32[2,112,256]{2,1,0:T(8,128)S(1)}, u32[]{:S(2)}, u32[]{:S(2)}) collective-permute-start(f32[2,112,256]{2,1,0:T(8,128)S(1)} %add_up.49.refs_3_), channel_id=1, source_target_pairs={{0,8},{2,10},{4,12},{6,14},{8,0},{10,2},{12,4},{14,6},{16,24},{18,... | collective-permute-start | bytes 688136 | tf_op jit(solution)/shard_map/ppermute | solution.py:294
  160.8 11.8 %collective-permute-start.32 = (f32[1,144,256]{2,1,0:T(8,128)S(1)}, f32[1,144,256]{2,1,0:T(8,128)S(1)}, u32[]{:S(2)}, u32[]{:S(2)}) collective-permute-start(f32[1,144,256]{2,1,0:T(8,128)S(1)} %add_up.51.refs_4_), channel_id=1, source_target_pairs={{0,16},{2,18},{4,20},{6,22},{8,24},{10,26},{12,28},{14,30},{16,0},... | collective-permute-start | bytes 442376 | tf_op jit(solution)/shard_map/ppermute | solution.py:294
  165.0 11.4 %collective-permute-start.36 = (f32[1,128,256]{2,1,0:T(8,128)S(1)}, f32[1,128,256]{2,1,0:T(8,128)S(1)}, u32[]{:S(2)}, u32[]{:S(2)}) collective-permute-start(f32[1,128,256]{2,1,0:T(8,128)S(1)} %add_up.52.refs_4_), channel_id=1, source_target_pairs={{0,16},{2,18},{4,20},{6,22},{8,24},{10,26},{12,28},{14,30},{16,0},... | collective-permute-start | bytes 393224 | tf_op jit(solution)/shard_map/ppermute | solution.py:294
  (12 other events, 51.3 us)

commit v4 on v3

--- a/solution.py
+++ b/solution.py
@@ -12,18 +12,21 @@
 LANES = 128
 BUFFERS = 4
 STEPS = 8
+FLOPS = 115_000_000
 VMEM = 50 << 20
 
 BITS = {"x": 1, "y": 2, "z": 4, "w": 8}
 
 GROUPS = (
-    (("xyzw", 88), ("yxzw", 88), ("zwyx", 80)),
-    (("xyzw", 128), ("yxzw", 136), ("zyxw", 120)),
-    (("xyzw", 144), ("yxzw", 112), ("zxyw", 128)),
+    (("yzxw", 136), ("xzyw", 120)),
+    (("yzxw", 104), ("xyzw", 144), ("xzwy", 136)),
+    (("yzxw", 176), ("zyxw", 104), ("xyzw", 104)),
 )
 
 ORDER = (
-    "0", "1", 0, 1, 2, "2", 0, 1, 3, 2, 3, 4, 5, 0, 1, 2, 4, 7, 5, 6, 8, 3, 4, 5, 6, 7, 8, 6, 8, 7,
+    ("0", 50), ("1", 70), (1, 6), (0, 3), ("2", 52), (1, 3), (2, 13), (0, 3), (3, 5), (1, 18), (0, 3),
+    (2, 21), (3, 3), (2, 25), (3, 48), (4, 14), (6, 21), (5, 17), (4, 6), (7, 6), (6, 22), (6, 8), (7, 3),
+    (4, 3), (5, 20), (7, 12), (5, 6),
 )
 
 
@@ -177,7 +180,7 @@
                 out_ref[index] = halves[half][start : start + size]
 
 
-def partial_sums(wavefunctions, sources, info, share_rows, parts, first):
+def partial_sums(wavefunctions, sources, info, share_rows, parts, first, beside):
     nodes = wavefunctions.shape[0]
     width = sum(size for _, size in parts)
     outs = []
@@ -230,7 +233,7 @@
         out_shape=[jax.ShapeDtypeStruct((2, 2, 2, out[2], share_rows), jnp.float32) for out in outs] + columns,
         compiler_params=pltpu.CompilerParams(vmem_limit_bytes=VMEM),
         cost_estimate=pl.CostEstimate(
-            flops=12 * STEPS * width * share_rows * nodes,
+            flops=beside * FLOPS,
             bytes_accessed=8 * STEPS * share_rows * (nodes + width),
             transcendentals=0,
         ),
@@ -250,7 +253,7 @@
     refs[-1][0] = total(refs[:-2], 0)
 
 
-def add_up(leaves, count, token):
+def add_up(leaves, count, token, beside):
     shape = leaves[0].shape[1:]
     return pl.pallas_call(
         add_kernel,
@@ -261,7 +264,9 @@
         out_shape=jax.ShapeDtypeStruct((count, *shape), jnp.float32),
         compiler_params=pltpu.CompilerParams(vmem_limit_bytes=16 << 20),
         cost_estimate=pl.CostEstimate(
-            flops=0, bytes_accessed=4 * count * shape[0] * shape[1] * (len(leaves) + 1), transcendentals=0
+            flops=beside * FLOPS,
+            bytes_accessed=4 * count * shape[0] * shape[1] * (len(leaves) + 1),
+            transcendentals=0,
         ),
         name="add_up",
     )(*leaves, token)
@@ -320,12 +325,12 @@
 
     held = {}
     first = 0
-    for step in ORDER:
+    for step, beside in ORDER:
         if isinstance(step, str):
             group = int(step)
             parts = GROUPS[group]
             sources = [own, other, last] if group else [h_wavefunctions]
-            out = partial_sums(wavefunctions, sources, info, share_rows, parts, first)
+            out = partial_sums(wavefunctions, sources, info, share_rows, parts, first, beside)
             last = out[0]
             if group == 0:
                 own = out.pop()
@@ -337,7 +342,7 @@
         else:
             bits, leaves = held[step]
             turn = len(leaves) - 1
-            last = add_up(leaves, 8 >> turn, last)
+            last = add_up(leaves, 8 >> turn, last, beside)
             leaves.append(swap(last, bits[turn]))
     results = [total(leaves, 0) for _, leaves in held.values()]
     sums = jnp.concatenate(results).reshape(NBLK, 2 * BLOCK, share_rows)

time: 180 us -> 174 us (0.967)
  waiting for transfers between devices: 70.4 us -> 61.7 us
  Pallas kernels: 52.3 us -> 55.1 us
    ppermute x36 -> x32, waiting for transfers between devices: 70.4 us -> 60.2 us  [swap(): lax.ppermute(value, 'node', [(i, i ^ bit) for i in range(lax.axis_size('n...]
    pallas_call x27 -> x24, Pallas kernels: 1.89 us -> 5.35 us  [add_up(): pl.pallas_call(add_kernel, grid=(count,), in_specs=[pl.BlockSpec((1, *sha...]
    ppermute x36 -> x32, starting transfers between devices: 50.6 us -> 51.4 us  [swap(): lax.ppermute(value, 'node', [(i, i ^ bit) for i in range(lax.axis_size('n...]
  transfers between devices with their start and end apart: 37 -> 33, of which waited for: 16 -> 17; matrix products, arithmetic and copies ran while one was open for 0% -> 1% of each run, Pallas kernels for 21% -> 23%
where the time goes in v4:
time: 174 us
  waiting for transfers between devices  61.7 us (35%)
  Pallas kernels  55.1 us (32%)
  starting transfers between devices  51.9 us (30%)
  local copies, waits for them, and re-layouts  2.19 us (1%)
  other arithmetic  1.99 us (1%)
    ppermute x32, waiting for transfers between devices, swap(): lax.ppermute(value, 'node', [(i, i ^ bit) for i in range(lax.axis_size('n...  60.2 us
    ppermute x32, starting transfers between devices, swap(): lax.ppermute(value, 'node', [(i, i ^ bit) for i in range(lax.axis_size('n...  51.4 us
    pallas_call x3, Pallas kernels, partial_sums(): pl.pallas_call(functools.partial(partial_kernel, outs=outs, first=first,...  47.3 us
    pallas_call x24, Pallas kernels, add_up(): pl.pallas_call(add_kernel, grid=(count,), in_specs=[pl.BlockSpec((1, *sha...  5.35 us
  transfers between devices with their start and end apart: 33, of which 17 were waited for; matrix products, arithmetic and copies ran while one was open for 1% of the time, Pallas kernels for 23%

profile of v4, /device:TPU:0, one launch (start us, length us, event | category | flops | bytes accessed | tf_op | source)
XLA Modules:
  0.0 173.8 jit_solution(410521223062464200)
XLA Ops:
  1.4 12.6 %partial_sums.3 = (f32[2,2,2,136,256]{4,3,2,1,0:T(8,128)S(1)}, f32[2,2,2,120,256]{4,3,2,1,0:T(8,128)S(1)}, f32[2,2,2,136,256]{4,3,2,1,0:T(8,128)}, f32[2,2,2,120,256]{4,3,2,1,0:T(8,128)S(1)}, f32[3,2,1024,128]{3,2,1,0:T(8,128)}) custom-call(s32[6]{0:T(128)S(1)} %pad_add_fusion.info, f32[1024,4096]{1,0:T(8,128)} %refs_0_.5, f32[1024,4096]{1,0:T(8,128)} %refs_1_.1), custom_call_target="tpu_custom_call" | custom-call | flops 5750000128 | bytes 20971520 | tf_op jit(solution)/shard_map/partial_sums/pallas_call | solution.py:204
  14.6 2.6 %collective-permute-start.1 = (f32[8,120,256]{2,1,0:T(8,128)S(1)}, f32[8,120,256]{2,1,0:T(8,128)S(1)}, u32[]{:S(2)}, u32[]{:S(2)}) collective-permute-start(f32[8,120,256]{2,1,0:T(8,128)S(1)} %bitcast.91), channel_id=1, source_target_pairs={{0,2},{2,0},{4,6},{6,4},{8,10},{10,8},{12,14},{14,12},{16,18},{18,... | collective-permute-start | bytes 2949128 | tf_op jit(solution)/shard_map/ppermute | solution.py:299
  18.6 1.6 collective-permute-done.2.refs_2_
  20.2 17.0 %partial_sums.4 = (f32[2,2,2,104,256]{4,3,2,1,0:T(8,128)S(1)}, f32[2,2,2,144,256]{4,3,2,1,0:T(8,128)}, f32[2,2,2,136,256]{4,3,2,1,0:T(8,128)S(1)}, f32[2,2,2,104...) custom-call(s32[6]{0:T(128)S(1)} %pad_add_fusion.info, ...), custom_call_target="tpu_custom_call" | custom-call | flops 8049999872 | bytes 23068672 | tf_op jit(solution)/shard_map/partial_sums/pallas_call | solution.py:204
  37.2 2.9 %collective-permute-start.8 = (f32[8,144,256]{2,1,0:T(8,128)}, f32[8,144,256]{2,1,0:T(8,128)S(1)}, u32[]{:S(2)}, u32[]{:S(2)}) collective-permute-start(f32[8,144,256]{2,1,0:T(8,128)} %bitcast.94), channel_id=1, source_target_pairs={{0,2},{2,0},{4,6},{6,4},{8,10},{10,8},{12,14},{14,12},{16,18},{18,... | collective-permute-start | bytes 3538952 | tf_op jit(solution)/shard_map/ppermute | solution.py:299
  41.8 1.7 collective-permute-start.5
  44.7 1.6 collective-permute-start.3
  46.3 17.7 %partial_sums.5 = (f32[2,2,2,176,256]{4,3,2,1,0:T(8,128)}, f32[2,2,2,104,256]{4,3,2,1,0:T(8,128)S(1)}, f32[2,2,2,104,256]{4,3,2,1,0:T(8,128)S(1)}, f32[2,2,2,176...) custom-call(s32[6]{0:T(128)S(1)} %pad_add_fusion.info, ...), custom_call_target="tpu_custom_call" | custom-call | flops 5980000256 | bytes 23068672 | tf_op jit(solution)/shard_map/partial_sums/pallas_call | solution.py:204
  65.4 1.6 collective-permute-start.7
  67.0 1.9 %add_up.27.refs_3_ = f32[4,104,256]{2,1,0:T(8,128)S(1)} custom-call(f32[8,104,256]{2,1,0:T(8,128)S(1)} %bitcast.84, f32[8,104,256]{2,1,0:T(8,128)} %collective-permute-done.4.refs_1_, f32[2,120,256]{2,1,0:T(8,128)S(1)} %add_up.26.refs_2_), custom_call_target="tpu_custom_call" | custom-call | flops 1495000064 | bytes 1277952 | tf_op jit(solution)/shard_map/add_up/pallas_call | solution.py:258
  74.0 4.0 %collective-permute-done.6.refs_3_ = f32[2,136,256]{2,1,0:T(8,128)S(1)} collective-permute-done((f32[2,136,256]{2,1,0:T(8,128)S(1)}, f32[2,136,256]{2,1,0:T(8,128)S(1)}, u32[]{:S(2)}, u32[]{:S(2)}) %collective-permute-start.6) | collective-permute-done | bytes 278560 | tf_op jit(solution)/shard_map/ppermute | solution.py:299
  78.3 4.9 %collective-permute-done.11.refs_2_ = f32[4,104,256]{2,1,0:T(8,128)S(1)} collective-permute-done((f32[4,104,256]{2,1,0:T(8,128)S(1)}, f32[4,104,256]{2,1,0:T(8,128)S(1)}, u32[]{:S(2)}, u32[]{:S(2)}) %collective-permute-start.11) | collective-permute-done | bytes 426016 | tf_op jit(solution)/shard_map/ppermute | solution.py:299
  87.3 10.7 %collective-permute-done.9 = f32[1,136,256]{2,1,0:T(8,128)S(1)} collective-permute-done((f32[1,136,256]{2,1,0:T(8,128)S(1)}, f32[1,136,256]{2,1,0:T(8,128)S(1)}, u32[]{:S(2)}, u32[]{:S(2)}) %collective-permute-start.9) | collective-permute-done | bytes 139296 | tf_op jit(solution)/shard_map/ppermute | solution.py:299
  97.9 6.4 %collective-permute-start.15 = (f32[2,144,256]{2,1,0:T(8,128)S(1)}, f32[2,144,256]{2,1,0:T(8,128)S(1)}, u32[]{:S(2)}, u32[]{:S(2)}) collective-permute-start(f32[2,144,256]{2,1,0:T(8,128)S(1)} %add_up.33.refs_4_), channel_id=1, source_target_pairs={{0,8},{2,10},{4,12},{6,14},{8,0},{10,2},{12,4},{14,6},{16,24},{18,... | collective-permute-start | bytes 884744 | tf_op jit(solution)/shard_map/ppermute | solution.py:299
  104.4 2.8 %collective-permute-done.12.refs_3_ = f32[2,104,256]{2,1,0:T(8,128)S(1)} collective-permute-done((f32[2,104,256]{2,1,0:T(8,128)S(1)}, f32[2,104,256]{2,1,0:T(8,128)S(1)}, u32[]{:S(2)}, u32[]{:S(2)}) %collective-permute-start.12) | collective-permute-done | bytes 213024 | tf_op jit(solution)/shard_map/ppermute | solution.py:299
  108.5 2.0 %collective-permute-done.15.refs_3_ = f32[2,144,256]{2,1,0:T(8,128)S(1)} collective-permute-done((f32[2,144,256]{2,1,0:T(8,128)S(1)}, f32[2,144,256]{2,1,0:T(8,128)S(1)}, u32[]{:S(2)}, u32[]{:S(2)}) %collective-permute-start.15) | collective-permute-done | bytes 294944 | tf_op jit(solution)/shard_map/ppermute | solution.py:299
  111.4 1.7 collective-permute-start.18
  114.1 2.2 %collective-permute-done.10 = f32[1,120,256]{2,1,0:T(8,128)S(1)} collective-permute-done((f32[1,120,256]{2,1,0:T(8,128)S(1)}, f32[1,120,256]{2,1,0:T(8,128)S(1)}, u32[]{:S(2)}, u32[]{:S(2)}) %collective-permute-start.10) | collective-permute-done | bytes 122912 | tf_op jit(solution)/shard_map/ppermute | solution.py:299
  116.4 2.1 %collective-permute-start.14 = (f32[1,104,256]{2,1,0:T(8,128)S(1)}, f32[1,104,256]{2,1,0:T(8,128)S(1)}, u32[]{:S(2)}, u32[]{:S(2)}) collective-permute-start(f32[1,104,256]{2,1,0:T(8,128)S(1)} %add_up.34.refs_4_), channel_id=1, source_target_pairs={{0,16},{2,18},{4,20},{6,22},{8,24},{10,26},{12,28},{14,30},{16,0},... | collective-permute-start | bytes 319496 | tf_op jit(solution)/shard_map/ppermute | solution.py:299
  118.6 2.5 %collective-permute-start.27 = (f32[4,176,256]{2,1,0:T(8,128)S(1)}, f32[4,176,256]{2,1,0:T(8,128)S(1)}, u32[]{:S(2)}, u32[]{:S(2)}) collective-permute-start(f32[4,176,256]{2,1,0:T(8,128)S(1)} %add_up.38.refs_3_), channel_id=1, source_target_pairs={{0,8},{2,10},{4,12},{6,14},{8,0},{10,2},{12,4},{14,6},{16,24},{18,... | collective-permute-start | bytes 2162696 | tf_op jit(solution)/shard_map/ppermute | solution.py:299
  121.1 12.9 %collective-permute-done.18.refs_2_ = f32[4,136,256]{2,1,0:T(8,128)S(1)} collective-permute-done((f32[4,136,256]{2,1,0:T(8,128)S(1)}, f32[4,136,256]{2,1,0:T(8,128)S(1)}, u32[]{:S(2)}, u32[]{:S(2)}) %collective-permute-start.18) | collective-permute-done | bytes 557088 | tf_op jit(solution)/shard_map/ppermute | solution.py:299
  134.1 2.2 %collective-permute-start.21 = (f32[2,136,256]{2,1,0:T(8,128)S(1)}, f32[2,136,256]{2,1,0:T(8,128)S(1)}, u32[]{:S(2)}, u32[]{:S(2)}) collective-permute-start(f32[2,136,256]{2,1,0:T(8,128)S(1)} %add_up.39.refs_2_), channel_id=1, source_target_pairs={{0,16},{2,18},{4,20},{6,22},{8,24},{10,26},{12,28},{14,30},{16,0},... | collective-permute-start | bytes 835592 | tf_op jit(solution)/shard_map/ppermute | solution.py:299
  138.5 2.9 %collective-permute-start.16 = (f32[1,144,256]{2,1,0:T(8,128)S(1)}, f32[1,144,256]{2,1,0:T(8,128)S(1)}, u32[]{:S(2)}, u32[]{:S(2)}) collective-permute-start(f32[1,144,256]{2,1,0:T(8,128)S(1)} %add_up.35.refs_2_), channel_id=1, source_target_pairs={{0,16},{2,18},{4,20},{6,22},{8,24},{10,26},{12,28},{14,30},{16,0},... | collective-permute-start | bytes 442376 | tf_op jit(solution)/shard_map/ppermute | solution.py:299
  142.5 2.1 %collective-permute-done.23.refs_2_ = f32[4,104,256]{2,1,0:T(8,128)S(1)} collective-permute-done((f32[4,104,256]{2,1,0:T(8,128)S(1)}, f32[4,104,256]{2,1,0:T(8,128)S(1)}, u32[]{:S(2)}, u32[]{:S(2)}) %collective-permute-start.23) | collective-permute-done | bytes 426016 | tf_op jit(solution)/shard_map/ppermute | solution.py:299
  144.6 2.5 %collective-permute-start.29 = (f32[2,104,256]{2,1,0:T(8,128)S(1)}, f32[2,104,256]{2,1,0:T(8,128)S(1)}, u32[]{:S(2)}, u32[]{:S(2)}) collective-permute-start(f32[2,104,256]{2,1,0:T(8,128)S(1)} %add_up.43.refs_4_), channel_id=1, source_target_pairs={{0,8},{2,10},{4,12},{6,14},{8,0},{10,2},{12,4},{14,6},{16,24},{18,... | collective-permute-start | bytes 638984 | tf_op jit(solution)/shard_map/ppermute | solution.py:299
  147.2 3.5 %collective-permute-done.21.refs_3_ = f32[2,136,256]{2,1,0:T(8,128)S(1)} collective-permute-done((f32[2,136,256]{2,1,0:T(8,128)S(1)}, f32[2,136,256]{2,1,0:T(8,128)S(1)}, u32[]{:S(2)}, u32[]{:S(2)}) %collective-permute-start.21) | collective-permute-done | bytes 278560 | tf_op jit(solution)/shard_map/ppermute | solution.py:299
  150.7 2.2 %collective-permute-done.27.refs_2_ = f32[4,176,256]{2,1,0:T(8,128)S(1)} collective-permute-done((f32[4,176,256]{2,1,0:T(8,128)S(1)}, f32[4,176,256]{2,1,0:T(8,128)S(1)}, u32[]{:S(2)}, u32[]{:S(2)}) %collective-permute-start.27) | collective-permute-done | bytes 720928 | tf_op jit(solution)/shard_map/ppermute | solution.py:299
  153.7 3.4 %collective-permute-start.31 = (f32[1,104,256]{2,1,0:T(8,128)S(1)}, f32[1,104,256]{2,1,0:T(8,128)S(1)}, u32[]{:S(2)}, u32[]{:S(2)}) collective-permute-start(f32[1,104,256]{2,1,0:T(8,128)S(1)} %add_up.42.refs_3_), channel_id=1, source_target_pairs={{0,16},{2,18},{4,20},{6,22},{8,24},{10,26},{12,28},{14,30},{16,0},... | collective-permute-start | bytes 319496 | tf_op jit(solution)/shard_map/ppermute | solution.py:299
  157.0 1.7 %collective-permute-start.26 = (f32[1,136,256]{2,1,0:T(8,128)S(1)}, f32[1,136,256]{2,1,0:T(8,128)S(1)}, u32[]{:S(2)}, u32[]{:S(2)}) collective-permute-start(f32[1,136,256]{2,1,0:T(8,128)S(1)} %add_up.44.refs_3_), channel_id=1, source_target_pairs={{0,4},{2,6},{4,0},{6,2},{8,12},{10,14},{12,8},{14,10},{16,20},{18,... | collective-permute-start | bytes 417800 | tf_op jit(solution)/shard_map/ppermute | solution.py:299
  158.8 1.7 collective-permute-done.28.refs_3_
  163.6 6.6 %collective-permute-done.30 = f32[1,176,256]{2,1,0:T(8,128)S(1)} collective-permute-done((f32[1,176,256]{2,1,0:T(8,128)S(1)}, f32[1,176,256]{2,1,0:T(8,128)S(1)}, u32[]{:S(2)}, u32[]{:S(2)}) %collective-permute-start.30) | collective-permute-done | bytes 180256 | tf_op jit(solution)/shard_map/ppermute | solution.py:299
  171.4 2.4 %place_columns.1 = (f32[256,512]{1,0:T(8,128)}, f32[256,512]{1,0:T(8,128)}) custom-call(s32[6]{0:T(128)S(1)} %pad_add_fusion.info, f32[4,256,256]{2,1,0:T(8,128)S(1)} %bitcast.73), custom_call_target="tpu_custom_call" | custom-call | tf_op jit(solution)/shard_map/place_columns/pallas_call | solution.py:283
  (87 shorter events, 28.3 us)
Async XLA Ops:
  14.0 6.2 %collective-permute-start.2 = (f32[3,2,1024,128]{3,2,1,0:T(8,128)}, f32[3,2,1024,128]{3,2,1,0:T(8,128)}, u32[]{:S(2)}, u32[]{:S(2)}) collective-permute-start(f32[3,2,1024,128]{3,2,1,0:T(8,128)} %get-tuple-element.23.refs_1_), channel_id=1, source_target_pairs={{0,1},{1,0},{2,3},{3,2},{4,5},{5,4},{6,7},{7,6},{8,9},{9,8},{10,11... | collective-permute-start | bytes 9437192 | tf_op jit(solution)/shard_map/ppermute | solution.py:303
  14.6 27.1 %collective-permute-start.1 = (f32[8,120,256]{2,1,0:T(8,128)S(1)}, f32[8,120,256]{2,1,0:T(8,128)S(1)}, u32[]{:S(2)}, u32[]{:S(2)}) collective-permute-start(f32[8,120,256]{2,1,0:T(8,128)S(1)} %bitcast.91), channel_id=1, source_target_pairs={{0,2},{2,0},{4,6},{6,4},{8,10},{10,8},{12,14},{14,12},{16,18},{18,... | collective-permute-start | bytes 2949128 | tf_op jit(solution)/shard_map/ppermute | solution.py:299
  17.1 27.4 %collective-permute-start = (f32[8,136,256]{2,1,0:T(8,128)S(1)}, f32[8,136,256]{2,1,0:T(8,128)S(1)}, u32[]{:S(2)}, u32[]{:S(2)}) collective-permute-start(f32[8,136,256]{2,1,0:T(8,128)S(1)} %bitcast.89), channel_id=1, source_target_pairs={{0,4},{2,6},{4,0},{6,2},{8,12},{10,14},{12,8},{14,10},{16,20},{18,... | collective-permute-start | bytes 3342344 | tf_op jit(solution)/shard_map/ppermute | solution.py:299
  37.2 32.3 %collective-permute-start.8 = (f32[8,144,256]{2,1,0:T(8,128)}, f32[8,144,256]{2,1,0:T(8,128)S(1)}, u32[]{:S(2)}, u32[]{:S(2)}) collective-permute-start(f32[8,144,256]{2,1,0:T(8,128)} %bitcast.94), channel_id=1, source_target_pairs={{0,2},{2,0},{4,6},{6,4},{8,10},{10,8},{12,14},{14,12},{16,18},{18,... | collective-permute-start | bytes 3538952 | tf_op jit(solution)/shard_map/ppermute | solution.py:299
  40.1 26.9 %collective-permute-start.4 = (f32[8,104,256]{2,1,0:T(8,128)S(1)}, f32[8,104,256]{2,1,0:T(8,128)}, u32[]{:S(2)}, u32[]{:S(2)}) collective-permute-start(f32[8,104,256]{2,1,0:T(8,128)S(1)} %bitcast.78), channel_id=1, source_target_pairs={{0,4},{2,6},{4,0},{6,2},{8,12},{10,14},{12,8},{14,10},{16,20},{18,... | collective-permute-start | bytes 2555912 | tf_op jit(solution)/shard_map/ppermute | solution.py:299
  41.8 22.2 %collective-permute-start.5 = (f32[4,120,256]{2,1,0:T(8,128)S(1)}, f32[4,120,256]{2,1,0:T(8,128)S(1)}, u32[]{:S(2)}, u32[]{:S(2)}) collective-permute-start(f32[4,120,256]{2,1,0:T(8,128)S(1)} %add_up.24.refs_2_), channel_id=1, source_target_pairs={{0,8},{2,10},{4,12},{6,14},{8,0},{10,2},{12,4},{14,6},{16,24},{18,... | collective-permute-start | bytes 1474568 | tf_op jit(solution)/shard_map/ppermute | solution.py:299
  44.7 24.8 %collective-permute-start.3 = (f32[4,136,256]{2,1,0:T(8,128)S(1)}, f32[4,136,256]{2,1,0:T(8,128)S(1)}, u32[]{:S(2)}, u32[]{:S(2)}) collective-permute-start(f32[4,136,256]{2,1,0:T(8,128)S(1)} %add_up.25.refs_3_), channel_id=1, source_target_pairs={{0,8},{2,10},{4,12},{6,14},{8,0},{10,2},{12,4},{14,6},{16,24},{18,... | collective-permute-start | bytes 1671176 | tf_op jit(solution)/shard_map/ppermute | solution.py:299
  65.4 7.5 %collective-permute-start.7 = (f32[2,120,256]{2,1,0:T(8,128)S(1)}, f32[2,120,256]{2,1,0:T(8,128)S(1)}, u32[]{:S(2)}, u32[]{:S(2)}) collective-permute-start(f32[2,120,256]{2,1,0:T(8,128)S(1)} %add_up.26.refs_2_), channel_id=1, source_target_pairs={{0,4},{2,6},{4,0},{6,2},{8,12},{10,14},{12,8},{14,10},{16,20},{18,... | collective-permute-start | bytes 737288 | tf_op jit(solution)/shard_map/ppermute | solution.py:299
  69.0 14.3 %collective-permute-start.11 = (f32[4,104,256]{2,1,0:T(8,128)S(1)}, f32[4,104,256]{2,1,0:T(8,128)S(1)}, u32[]{:S(2)}, u32[]{:S(2)}) collective-permute-start(f32[4,104,256]{2,1,0:T(8,128)S(1)} %add_up.27.refs_3_), channel_id=1, source_target_pairs={{0,8},{2,10},{4,12},{6,14},{8,0},{10,2},{12,4},{14,6},{16,24},{18,... | collective-permute-start | bytes 1277960 | tf_op jit(solution)/shard_map/ppermute | solution.py:299
  70.3 16.3 %collective-permute-start.13 = (f32[4,144,256]{2,1,0:T(8,128)S(1)}, f32[4,144,256]{2,1,0:T(8,128)S(1)}, u32[]{:S(2)}, u32[]{:S(2)}) collective-permute-start(f32[4,144,256]{2,1,0:T(8,128)S(1)} %add_up.29.refs_4_), channel_id=1, source_target_pairs={{0,4},{2,6},{4,0},{6,2},{8,12},{10,14},{12,8},{14,10},{16,20},{18,... | collective-permute-start | bytes 1769480 | tf_op jit(solution)/shard_map/ppermute | solution.py:299
  70.9 7.0 %collective-permute-start.6 = (f32[2,136,256]{2,1,0:T(8,128)S(1)}, f32[2,136,256]{2,1,0:T(8,128)S(1)}, u32[]{:S(2)}, u32[]{:S(2)}) collective-permute-start(f32[2,136,256]{2,1,0:T(8,128)S(1)} %add_up.28.refs_2_), channel_id=1, source_target_pairs={{0,2},{2,0},{4,6},{6,4},{8,10},{10,8},{12,14},{14,12},{16,18},{18,... | collective-permute-start | bytes 835592 | tf_op jit(solution)/shard_map/ppermute | solution.py:299
  71.6 46.9 %collective-permute-start.19 = (f32[8,176,256]{2,1,0:T(8,128)S(1)}, f32[8,176,256]{2,1,0:T(8,128)S(1)}, u32[]{:S(2)}, u32[]{:S(2)}) collective-permute-start(f32[8,176,256]{2,1,0:T(8,128)S(1)} %bitcast.72), channel_id=1, source_target_pairs={{0,4},{2,6},{4,0},{6,2},{8,12},{10,14},{12,8},{14,10},{16,20},{18,... | collective-permute-start | bytes 4325384 | tf_op jit(solution)/shard_map/ppermute | solution.py:299
  73.0 40.1 %collective-permute-start.20 = (f32[8,104,256]{2,1,0:T(8,128)S(1)}, f32[8,104,256]{2,1,0:T(8,128)S(1)}, u32[]{:S(2)}, u32[]{:S(2)}) collective-permute-start(f32[8,104,256]{2,1,0:T(8,128)S(1)} %bitcast.93), channel_id=1, source_target_pairs={{0,8},{2,10},{4,12},{6,14},{8,0},{10,2},{12,4},{14,6},{16,24},{18,... | collective-permute-start | bytes 2555912 | tf_op jit(solution)/shard_map/ppermute | solution.py:299
  77.9 33.3 %collective-permute-start.17 = (f32[8,136,256]{2,1,0:T(8,128)S(1)}, f32[8,136,256]{2,1,0:T(8,128)S(1)}, u32[]{:S(2)}, u32[]{:S(2)}) collective-permute-start(f32[8,136,256]{2,1,0:T(8,128)S(1)} %bitcast.88), channel_id=1, source_target_pairs={{0,2},{2,0},{4,6},{6,4},{8,10},{10,8},{12,14},{14,12},{16,18},{18,... | collective-permute-start | bytes 3342344 | tf_op jit(solution)/shard_map/ppermute | solution.py:299
  83.3 14.7 %collective-permute-start.9 = (f32[1,136,256]{2,1,0:T(8,128)S(1)}, f32[1,136,256]{2,1,0:T(8,128)S(1)}, u32[]{:S(2)}, u32[]{:S(2)}) collective-permute-start(f32[1,136,256]{2,1,0:T(8,128)S(1)} %add_up.31.refs_3_), channel_id=1, source_target_pairs={{0,16},{2,18},{4,20},{6,22},{8,24},{10,26},{12,28},{14,30},{16,0},... | collective-permute-start | bytes 417800 | tf_op jit(solution)/shard_map/ppermute | solution.py:299
  86.7 20.5 %collective-permute-start.12 = (f32[2,104,256]{2,1,0:T(8,128)S(1)}, f32[2,104,256]{2,1,0:T(8,128)S(1)}, u32[]{:S(2)}, u32[]{:S(2)}) collective-permute-start(f32[2,104,256]{2,1,0:T(8,128)S(1)} %add_up.32.refs_3_), channel_id=1, source_target_pairs={{0,2},{2,0},{4,6},{6,4},{8,10},{10,8},{12,14},{14,12},{16,18},{18,... | collective-permute-start | bytes 638984 | tf_op jit(solution)/shard_map/ppermute | solution.py:299
  97.9 12.6 %collective-permute-start.15 = (f32[2,144,256]{2,1,0:T(8,128)S(1)}, f32[2,144,256]{2,1,0:T(8,128)S(1)}, u32[]{:S(2)}, u32[]{:S(2)}) collective-permute-start(f32[2,144,256]{2,1,0:T(8,128)S(1)} %add_up.33.refs_4_), channel_id=1, source_target_pairs={{0,8},{2,10},{4,12},{6,14},{8,0},{10,2},{12,4},{14,6},{16,24},{18,... | collective-permute-start | bytes 884744 | tf_op jit(solution)/shard_map/ppermute | solution.py:299
  107.2 29.1 %collective-permute-start.22 = (f32[8,104,256]{2,1,0:T(8,128)S(1)}, f32[8,104,256]{2,1,0:T(8,128)S(1)}, u32[]{:S(2)}, u32[]{:S(2)}) collective-permute-start(f32[8,104,256]{2,1,0:T(8,128)S(1)} %bitcast.92), channel_id=1, source_target_pairs={{0,2},{2,0},{4,6},{6,4},{8,10},{10,8},{12,14},{14,12},{16,18},{18,... | collective-permute-start | bytes 2555912 | tf_op jit(solution)/shard_map/ppermute | solution.py:299
  110.5 5.8 %collective-permute-start.10 = (f32[1,120,256]{2,1,0:T(8,128)S(1)}, f32[1,120,256]{2,1,0:T(8,128)S(1)}, u32[]{:S(2)}, u32[]{:S(2)}) collective-permute-start(f32[1,120,256]{2,1,0:T(8,128)S(1)} %add_up.30.refs_4_), channel_id=1, source_target_pairs={{0,16},{2,18},{4,20},{6,22},{8,24},{10,26},{12,28},{14,30},{16,0},... | collective-permute-start | bytes 368648 | tf_op jit(solution)/shard_map/ppermute | solution.py:299
  111.4 22.6 %collective-permute-start.18 = (f32[4,136,256]{2,1,0:T(8,128)S(1)}, f32[4,136,256]{2,1,0:T(8,128)S(1)}, u32[]{:S(2)}, u32[]{:S(2)}) collective-permute-start(f32[4,136,256]{2,1,0:T(8,128)S(1)} %add_up.36.refs_2_), channel_id=1, source_target_pairs={{0,8},{2,10},{4,12},{6,14},{8,0},{10,2},{12,4},{14,6},{16,24},{18,... | collective-permute-start | bytes 1671176 | tf_op jit(solution)/shard_map/ppermute | solution.py:299
  113.2 23.3 %collective-permute-start.24 = (f32[4,104,256]{2,1,0:T(8,128)S(1)}, f32[4,104,256]{2,1,0:T(8,128)S(1)}, u32[]{:S(2)}, u32[]{:S(2)}) collective-permute-start(f32[4,104,256]{2,1,0:T(8,128)S(1)} %add_up.37.refs_2_), channel_id=1, source_target_pairs={{0,4},{2,6},{4,0},{6,2},{8,12},{10,14},{12,8},{14,10},{16,20},{18,... | collective-permute-start | bytes 1277960 | tf_op jit(solution)/shard_map/ppermute | solution.py:299
  116.4 21.1 %collective-permute-start.14 = (f32[1,104,256]{2,1,0:T(8,128)S(1)}, f32[1,104,256]{2,1,0:T(8,128)S(1)}, u32[]{:S(2)}, u32[]{:S(2)}) collective-permute-start(f32[1,104,256]{2,1,0:T(8,128)S(1)} %add_up.34.refs_4_), channel_id=1, source_target_pairs={{0,16},{2,18},{4,20},{6,22},{8,24},{10,26},{12,28},{14,30},{16,0},... | collective-permute-start | bytes 319496 | tf_op jit(solution)/shard_map/ppermute | solution.py:299
  118.6 34.3 %collective-permute-start.27 = (f32[4,176,256]{2,1,0:T(8,128)S(1)}, f32[4,176,256]{2,1,0:T(8,128)S(1)}, u32[]{:S(2)}, u32[]{:S(2)}) collective-permute-start(f32[4,176,256]{2,1,0:T(8,128)S(1)} %add_up.38.refs_3_), channel_id=1, source_target_pairs={{0,8},{2,10},{4,12},{6,14},{8,0},{10,2},{12,4},{14,6},{16,24},{18,... | collective-permute-start | bytes 2162696 | tf_op jit(solution)/shard_map/ppermute | solution.py:299
  134.1 16.6 %collective-permute-start.21 = (f32[2,136,256]{2,1,0:T(8,128)S(1)}, f32[2,136,256]{2,1,0:T(8,128)S(1)}, u32[]{:S(2)}, u32[]{:S(2)}) collective-permute-start(f32[2,136,256]{2,1,0:T(8,128)S(1)} %add_up.39.refs_2_), channel_id=1, source_target_pairs={{0,16},{2,18},{4,20},{6,22},{8,24},{10,26},{12,28},{14,30},{16,0},... | collective-permute-start | bytes 835592 | tf_op jit(solution)/shard_map/ppermute | solution.py:299
  136.4 8.2 %collective-permute-start.23 = (f32[4,104,256]{2,1,0:T(8,128)S(1)}, f32[4,104,256]{2,1,0:T(8,128)S(1)}, u32[]{:S(2)}, u32[]{:S(2)}) collective-permute-start(f32[4,104,256]{2,1,0:T(8,128)S(1)} %add_up.40.refs_3_), channel_id=1, source_target_pairs={{0,4},{2,6},{4,0},{6,2},{8,12},{10,14},{12,8},{14,10},{16,20},{18,... | collective-permute-start | bytes 1277960 | tf_op jit(solution)/shard_map/ppermute | solution.py:299
  136.6 5.9 %collective-permute-start.25 = (f32[2,104,256]{2,1,0:T(8,128)S(1)}, f32[2,104,256]{2,1,0:T(8,128)S(1)}, u32[]{:S(2)}, u32[]{:S(2)}) collective-permute-start(f32[2,104,256]{2,1,0:T(8,128)S(1)} %add_up.41.refs_4_), channel_id=1, source_target_pairs={{0,2},{2,0},{4,6},{6,4},{8,10},{10,8},{12,14},{14,12},{16,18},{18,... | collective-permute-start | bytes 638984 | tf_op jit(solution)/shard_map/ppermute | solution.py:299
  138.5 15.1 %collective-permute-start.16 = (f32[1,144,256]{2,1,0:T(8,128)S(1)}, f32[1,144,256]{2,1,0:T(8,128)S(1)}, u32[]{:S(2)}, u32[]{:S(2)}) collective-permute-start(f32[1,144,256]{2,1,0:T(8,128)S(1)} %add_up.35.refs_2_), channel_id=1, source_target_pairs={{0,16},{2,18},{4,20},{6,22},{8,24},{10,26},{12,28},{14,30},{16,0},... | collective-permute-start | bytes 442376 | tf_op jit(solution)/shard_map/ppermute | solution.py:299
  144.6 14.1 %collective-permute-start.29 = (f32[2,104,256]{2,1,0:T(8,128)S(1)}, f32[2,104,256]{2,1,0:T(8,128)S(1)}, u32[]{:S(2)}, u32[]{:S(2)}) collective-permute-start(f32[2,104,256]{2,1,0:T(8,128)S(1)} %add_up.43.refs_4_), channel_id=1, source_target_pairs={{0,8},{2,10},{4,12},{6,14},{8,0},{10,2},{12,4},{14,6},{16,24},{18,... | collective-permute-start | bytes 638984 | tf_op jit(solution)/shard_map/ppermute | solution.py:299
  153.0 7.5 %collective-permute-start.28 = (f32[2,176,256]{2,1,0:T(8,128)S(1)}, f32[2,176,256]{2,1,0:T(8,128)S(1)}, u32[]{:S(2)}, u32[]{:S(2)}) collective-permute-start(f32[2,176,256]{2,1,0:T(8,128)S(1)} %add_up.45.refs_4_), channel_id=1, source_target_pairs={{0,2},{2,0},{4,6},{6,4},{8,10},{10,8},{12,14},{14,12},{16,18},{18,... | collective-permute-start | bytes 1081352 | tf_op jit(solution)/shard_map/ppermute | solution.py:299
  153.7 16.7 %collective-permute-start.31 = (f32[1,104,256]{2,1,0:T(8,128)S(1)}, f32[1,104,256]{2,1,0:T(8,128)S(1)}, u32[]{:S(2)}, u32[]{:S(2)}) collective-permute-start(f32[1,104,256]{2,1,0:T(8,128)S(1)} %add_up.42.refs_3_), channel_id=1, source_target_pairs={{0,16},{2,18},{4,20},{6,22},{8,24},{10,26},{12,28},{14,30},{16,0},... | collective-permute-start | bytes 319496 | tf_op jit(solution)/shard_map/ppermute | solution.py:299
  160.5 9.7 %collective-permute-start.30 = (f32[1,176,256]{2,1,0:T(8,128)S(1)}, f32[1,176,256]{2,1,0:T(8,128)S(1)}, u32[]{:S(2)}, u32[]{:S(2)}) collective-permute-start(f32[1,176,256]{2,1,0:T(8,128)S(1)} %add_up.47), channel_id=1, source_target_pairs={{0,16},{2,18},{4,20},{6,22},{8,24},{10,26},{12,28},{14,30},{16,0},... | collective-permute-start | bytes 540680 | tf_op jit(solution)/shard_map/ppermute | solution.py:299
  162.1 9.3 %collective-permute-start.32 = (f32[1,104,256]{2,1,0:T(8,128)S(1)}, f32[1,104,256]{2,1,0:T(8,128)S(1)}, u32[]{:S(2)}, u32[]{:S(2)}) collective-permute-start(f32[1,104,256]{2,1,0:T(8,128)S(1)} %add_up.46.refs_4_), channel_id=1, source_target_pairs={{0,16},{2,18},{4,20},{6,22},{8,24},{10,26},{12,28},{14,30},{16,0},... | collective-permute-start | bytes 319496 | tf_op jit(solution)/shard_map/ppermute | solution.py:299
  (9 other events, 33.0 us)

commit v5 on v4

--- a/solution.py
+++ b/solution.py
@@ -13,7 +13,7 @@
 BUFFERS = 4
 STEPS = 8
 FLOPS = 115_000_000
-VMEM = 50 << 20
+VMEM = 32 << 20
 
 BITS = {"x": 1, "y": 2, "z": 4, "w": 8}
 

time: 174 us -> 169 us (0.971)
  Pallas kernels: 55.1 us -> 45.5 us
  starting transfers between devices: 51.9 us -> 57 us
  waiting for transfers between devices: 61.7 us -> 64.7 us
  local copies, waits for them, and re-layouts: 2.19 us -> 0 us
    pallas_call x3, Pallas kernels: 47.3 us -> 41.4 us  [partial_sums(): pl.pallas_call(functools.partial(partial_kernel, outs=outs, first=first,...]
    ppermute x32, starting transfers between devices: 51.4 us -> 56.5 us  [swap(): lax.ppermute(value, 'node', [(i, i ^ bit) for i in range(lax.axis_size('n...]
    pallas_call x24, Pallas kernels: 5.35 us -> 1.75 us  [add_up(): pl.pallas_call(add_kernel, grid=(count,), in_specs=[pl.BlockSpec((1, *sha...]
    ppermute x32, waiting for transfers between devices: 60.2 us -> 63.5 us  [swap(): lax.ppermute(value, 'node', [(i, i ^ bit) for i in range(lax.axis_size('n...]
    unnamed x16 -> x0, local copies, waits for them, and re-layouts: 2.19 us -> none
  transfers between devices with their start and end apart: 33 -> 33, of which waited for: 17 -> 17; matrix products, arithmetic and copies ran while one was open for 1% -> 0% of each run, Pallas kernels for 23% -> 18%
where the time goes in v5:
time: 169 us
  waiting for transfers between devices  64.7 us (38%)
  starting transfers between devices  57 us (34%)
  Pallas kernels  45.5 us (27%)
    ppermute x32, waiting for transfers between devices, swap(): lax.ppermute(value, 'node', [(i, i ^ bit) for i in range(lax.axis_size('n...  63.5 us
    ppermute x32, starting transfers between devices, swap(): lax.ppermute(value, 'node', [(i, i ^ bit) for i in range(lax.axis_size('n...  56.5 us
    pallas_call x3, Pallas kernels, partial_sums(): pl.pallas_call(functools.partial(partial_kernel, outs=outs, first=first,...  41.4 us
  transfers between devices with their start and end apart: 33, of which 17 were waited for; matrix products, arithmetic and copies ran while one was open for 0% of the time, Pallas kernels for 18%

profile of v5, /device:TPU:0, one launch (start us, length us, event | category | flops | bytes accessed | tf_op | source)
XLA Modules:
  0.0 169.2 jit_solution(9152167274713694374)
XLA Ops:
  1.4 12.1 %partial_sums.3 = (f32[2,2,2,136,256]{4,3,2,1,0:T(8,128)S(1)}, f32[2,2,2,120,256]{4,3,2,1,0:T(8,128)S(1)}, f32[2,2,2,136,256]{4,3,2,1,0:T(8,128)S(1)}, f32[2,2,2...) custom-call(s32[6]{0:T(128)S(1)} %pad_add_fusion.info, f32[1024,4096]{1,0:T(8,128)} %refs_0_.5, f32[1024,4096]{1,0:T(8,128)} %refs_1_.1), custom_call_target="tpu_custom_call" | custom-call | flops 5750000128 | bytes 20971520 | tf_op jit(solution)/shard_map/partial_sums/pallas_call | solution.py:204
  14.0 2.6 %collective-permute-start.1 = (f32[8,120,256]{2,1,0:T(8,128)S(1)}, f32[8,120,256]{2,1,0:T(8,128)S(1)}, u32[]{:S(2)}, u32[]{:S(2)}) collective-permute-start(f32[8,120,256]{2,1,0:T(8,128)S(1)} %bitcast.92), channel_id=1, source_target_pairs={{0,2},{2,0},{4,6},{6,4},{8,10},{10,8},{12,14},{14,12},{16,18},{18,... | collective-permute-start | bytes 2949128 | tf_op jit(solution)/shard_map/ppermute | solution.py:299
  19.3 14.4 %partial_sums.4 = (f32[2,2,2,104,256]{4,3,2,1,0:T(8,128)S(1)}, f32[2,2,2,144,256]{4,3,2,1,0:T(8,128)S(1)}, f32[2,2,2,136,256]{4,3,2,1,0:T(8,128)S(1)}, f32[2,2,2...) custom-call(s32[6]{0:T(128)S(1)} %pad_add_fusion.info, ...), custom_call_target="tpu_custom_call" | custom-call | flops 8049999872 | bytes 23068672 | tf_op jit(solution)/shard_map/partial_sums/pallas_call | solution.py:204
  33.7 2.9 %collective-permute-start.8 = (f32[8,144,256]{2,1,0:T(8,128)S(1)}, f32[8,144,256]{2,1,0:T(8,128)S(1)}, u32[]{:S(2)}, u32[]{:S(2)}) collective-permute-start(f32[8,144,256]{2,1,0:T(8,128)S(1)} %bitcast.88), channel_id=1, source_target_pairs={{0,2},{2,0},{4,6},{6,4},{8,10},{10,8},{12,14},{14,12},{16,18},{18,... | collective-permute-start | bytes 3538952 | tf_op jit(solution)/shard_map/ppermute | solution.py:299
  39.3 2.1 %collective-permute-start.5 = (f32[4,120,256]{2,1,0:T(8,128)S(1)}, f32[4,120,256]{2,1,0:T(8,128)S(1)}, u32[]{:S(2)}, u32[]{:S(2)}) collective-permute-start(f32[4,120,256]{2,1,0:T(8,128)S(1)} %add_up.24.refs_2_), channel_id=1, source_target_pairs={{0,8},{2,10},{4,12},{6,14},{8,0},{10,2},{12,4},{14,6},{16,24},{18,... | collective-permute-start | bytes 1474568 | tf_op jit(solution)/shard_map/ppermute | solution.py:299
  41.4 2.6 %collective-permute-done.refs_1_ = f32[8,136,256]{2,1,0:T(8,128)S(1)} collective-permute-done((f32[8,136,256]{2,1,0:T(8,128)S(1)}, f32[8,136,256]{2,1,0:T(8,128)S(1)}, u32[]{:S(2)}, u32[]{:S(2)}) %collective-permute-start) | collective-permute-done | bytes 1114144 | tf_op jit(solution)/shard_map/ppermute | solution.py:299
  44.1 1.6 collective-permute-start.3
  45.8 14.8 %partial_sums.5 = (f32[2,2,2,176,256]{4,3,2,1,0:T(8,128)S(1)}, f32[2,2,2,104,256]{4,3,2,1,0:T(8,128)S(1)}, f32[2,2,2,104,256]{4,3,2,1,0:T(8,128)S(1)}, f32[2,2,2...) custom-call(s32[6]{0:T(128)S(1)} %pad_add_fusion.info, ...), custom_call_target="tpu_custom_call" | custom-call | flops 5980000256 | bytes 23068672 | tf_op jit(solution)/shard_map/partial_sums/pallas_call | solution.py:204
  64.6 1.7 %collective-permute-start.13 = (f32[4,144,256]{2,1,0:T(8,128)S(1)}, f32[4,144,256]{2,1,0:T(8,128)S(1)}, u32[]{:S(2)}, u32[]{:S(2)}) collective-permute-start(f32[4,144,256]{2,1,0:T(8,128)S(1)} %add_up.29.refs_4_), channel_id=1, source_target_pairs={{0,4},{2,6},{4,0},{6,2},{8,12},{10,14},{12,8},{14,10},{16,20},{18,... | collective-permute-start | bytes 1769480 | tf_op jit(solution)/shard_map/ppermute | solution.py:299
  66.4 2.4 %collective-permute-start.6 = (f32[2,136,256]{2,1,0:T(8,128)S(1)}, f32[2,136,256]{2,1,0:T(8,128)S(1)}, u32[]{:S(2)}, u32[]{:S(2)}) collective-permute-start(f32[2,136,256]{2,1,0:T(8,128)S(1)} %add_up.28.refs_2_), channel_id=1, source_target_pairs={{0,2},{2,0},{4,6},{6,4},{8,10},{10,8},{12,14},{14,12},{16,18},{18,... | collective-permute-start | bytes 835592 | tf_op jit(solution)/shard_map/ppermute | solution.py:299
  70.9 3.2 %collective-permute-done.6.refs_3_ = f32[2,136,256]{2,1,0:T(8,128)S(1)} collective-permute-done((f32[2,136,256]{2,1,0:T(8,128)S(1)}, f32[2,136,256]{2,1,0:T(8,128)S(1)}, u32[]{:S(2)}, u32[]{:S(2)}) %collective-permute-start.6) | collective-permute-done | bytes 278560 | tf_op jit(solution)/shard_map/ppermute | solution.py:299
  75.7 2.7 %collective-permute-start.9 = (f32[1,136,256]{2,1,0:T(8,128)S(1)}, f32[1,136,256]{2,1,0:T(8,128)S(1)}, u32[]{:S(2)}, u32[]{:S(2)}) collective-permute-start(f32[1,136,256]{2,1,0:T(8,128)S(1)} %add_up.31.refs_3_), channel_id=1, source_target_pairs={{0,16},{2,18},{4,20},{6,22},{8,24},{10,26},{12,28},{14,30},{16,0},... | collective-permute-start | bytes 417800 | tf_op jit(solution)/shard_map/ppermute | solution.py:299
  78.4 2.6 %collective-permute-done.13.refs_2_ = f32[4,144,256]{2,1,0:T(8,128)S(1)} collective-permute-done((f32[4,144,256]{2,1,0:T(8,128)S(1)}, f32[4,144,256]{2,1,0:T(8,128)S(1)}, u32[]{:S(2)}, u32[]{:S(2)}) %collective-permute-start.13) | collective-permute-done | bytes 589856 | tf_op jit(solution)/shard_map/ppermute | solution.py:299
  81.0 2.6 %collective-permute-start.12 = (f32[2,104,256]{2,1,0:T(8,128)S(1)}, f32[2,104,256]{2,1,0:T(8,128)S(1)}, u32[]{:S(2)}, u32[]{:S(2)}) collective-permute-start(f32[2,104,256]{2,1,0:T(8,128)S(1)} %add_up.32.refs_3_), channel_id=1, source_target_pairs={{0,2},{2,0},{4,6},{6,4},{8,10},{10,8},{12,14},{14,12},{16,18},{18,... | collective-permute-start | bytes 638984 | tf_op jit(solution)/shard_map/ppermute | solution.py:299
  83.6 10.0 %collective-permute-done.9 = f32[1,136,256]{2,1,0:T(8,128)S(1)} collective-permute-done((f32[1,136,256]{2,1,0:T(8,128)S(1)}, f32[1,136,256]{2,1,0:T(8,128)S(1)}, u32[]{:S(2)}, u32[]{:S(2)}) %collective-permute-start.9) | collective-permute-done | bytes 139296 | tf_op jit(solution)/shard_map/ppermute | solution.py:299
  93.6 3.5 %collective-permute-start.15 = (f32[2,144,256]{2,1,0:T(8,128)S(1)}, f32[2,144,256]{2,1,0:T(8,128)S(1)}, u32[]{:S(2)}, u32[]{:S(2)}) collective-permute-start(f32[2,144,256]{2,1,0:T(8,128)S(1)} %add_up.33.refs_4_), channel_id=1, source_target_pairs={{0,8},{2,10},{4,12},{6,14},{8,0},{10,2},{12,4},{14,6},{16,24},{18,... | collective-permute-start | bytes 884744 | tf_op jit(solution)/shard_map/ppermute | solution.py:299
  97.1 6.3 %collective-permute-done.12.refs_3_ = f32[2,104,256]{2,1,0:T(8,128)S(1)} collective-permute-done((f32[2,104,256]{2,1,0:T(8,128)S(1)}, f32[2,104,256]{2,1,0:T(8,128)S(1)}, u32[]{:S(2)}, u32[]{:S(2)}) %collective-permute-start.12) | collective-permute-done | bytes 213024 | tf_op jit(solution)/shard_map/ppermute | solution.py:299
  105.0 2.7 %collective-permute-start.10 = (f32[1,120,256]{2,1,0:T(8,128)S(1)}, f32[1,120,256]{2,1,0:T(8,128)S(1)}, u32[]{:S(2)}, u32[]{:S(2)}) collective-permute-start(f32[1,120,256]{2,1,0:T(8,128)S(1)} %add_up.30.refs_4_), channel_id=1, source_target_pairs={{0,16},{2,18},{4,20},{6,22},{8,24},{10,26},{12,28},{14,30},{16,0},... | collective-permute-start | bytes 368648 | tf_op jit(solution)/shard_map/ppermute | solution.py:299
  110.2 2.6 %collective-permute-done.10 = f32[1,120,256]{2,1,0:T(8,128)S(1)} collective-permute-done((f32[1,120,256]{2,1,0:T(8,128)S(1)}, f32[1,120,256]{2,1,0:T(8,128)S(1)}, u32[]{:S(2)}, u32[]{:S(2)}) %collective-permute-start.10) | collective-permute-done | bytes 122912 | tf_op jit(solution)/shard_map/ppermute | solution.py:299
  112.9 2.0 %collective-permute-start.14 = (f32[1,104,256]{2,1,0:T(8,128)S(1)}, f32[1,104,256]{2,1,0:T(8,128)S(1)}, u32[]{:S(2)}, u32[]{:S(2)}) collective-permute-start(f32[1,104,256]{2,1,0:T(8,128)S(1)} %add_up.34.refs_4_), channel_id=1, source_target_pairs={{0,16},{2,18},{4,20},{6,22},{8,24},{10,26},{12,28},{14,30},{16,0},... | collective-permute-start | bytes 319496 | tf_op jit(solution)/shard_map/ppermute | solution.py:299
  115.0 2.9 %collective-permute-start.27 = (f32[4,176,256]{2,1,0:T(8,128)S(1)}, f32[4,176,256]{2,1,0:T(8,128)S(1)}, u32[]{:S(2)}, u32[]{:S(2)}) collective-permute-start(f32[4,176,256]{2,1,0:T(8,128)S(1)} %add_up.38.refs_3_), channel_id=1, source_target_pairs={{0,8},{2,10},{4,12},{6,14},{8,0},{10,2},{12,4},{14,6},{16,24},{18,... | collective-permute-start | bytes 2162696 | tf_op jit(solution)/shard_map/ppermute | solution.py:299
  117.9 12.2 %collective-permute-done.18.refs_2_ = f32[4,136,256]{2,1,0:T(8,128)S(1)} collective-permute-done((f32[4,136,256]{2,1,0:T(8,128)S(1)}, f32[4,136,256]{2,1,0:T(8,128)S(1)}, u32[]{:S(2)}, u32[]{:S(2)}) %collective-permute-start.18) | collective-permute-done | bytes 557088 | tf_op jit(solution)/shard_map/ppermute | solution.py:299
  132.5 1.9 %collective-permute-start.16 = (f32[1,144,256]{2,1,0:T(8,128)S(1)}, f32[1,144,256]{2,1,0:T(8,128)S(1)}, u32[]{:S(2)}, u32[]{:S(2)}) collective-permute-start(f32[1,144,256]{2,1,0:T(8,128)S(1)} %add_up.35.refs_2_), channel_id=1, source_target_pairs={{0,16},{2,18},{4,20},{6,22},{8,24},{10,26},{12,28},{14,30},{16,0},... | collective-permute-start | bytes 442376 | tf_op jit(solution)/shard_map/ppermute | solution.py:299
  134.4 3.5 %collective-permute-done.25.refs_3_ = f32[2,104,256]{2,1,0:T(8,128)S(1)} collective-permute-done((f32[2,104,256]{2,1,0:T(8,128)S(1)}, f32[2,104,256]{2,1,0:T(8,128)S(1)}, u32[]{:S(2)}, u32[]{:S(2)}) %collective-permute-start.25) | collective-permute-done | bytes 213024 | tf_op jit(solution)/shard_map/ppermute | solution.py:299
  139.6 2.5 %collective-permute-start.29 = (f32[2,104,256]{2,1,0:T(8,128)S(1)}, f32[2,104,256]{2,1,0:T(8,128)S(1)}, u32[]{:S(2)}, u32[]{:S(2)}) collective-permute-start(f32[2,104,256]{2,1,0:T(8,128)S(1)} %add_up.43.refs_4_), channel_id=1, source_target_pairs={{0,8},{2,10},{4,12},{6,14},{8,0},{10,2},{12,4},{14,6},{16,24},{18,... | collective-permute-start | bytes 638984 | tf_op jit(solution)/shard_map/ppermute | solution.py:299
  142.1 3.8 %collective-permute-done.21.refs_3_ = f32[2,136,256]{2,1,0:T(8,128)S(1)} collective-permute-done((f32[2,136,256]{2,1,0:T(8,128)S(1)}, f32[2,136,256]{2,1,0:T(8,128)S(1)}, u32[]{:S(2)}, u32[]{:S(2)}) %collective-permute-start.21) | collective-permute-done | bytes 278560 | tf_op jit(solution)/shard_map/ppermute | solution.py:299
  145.9 2.3 %collective-permute-done.27.refs_2_ = f32[4,176,256]{2,1,0:T(8,128)S(1)} collective-permute-done((f32[4,176,256]{2,1,0:T(8,128)S(1)}, f32[4,176,256]{2,1,0:T(8,128)S(1)}, u32[]{:S(2)}, u32[]{:S(2)}) %collective-permute-start.27) | collective-permute-done | bytes 720928 | tf_op jit(solution)/shard_map/ppermute | solution.py:299
  148.3 2.3 %collective-permute-start.28 = (f32[2,176,256]{2,1,0:T(8,128)S(1)}, f32[2,176,256]{2,1,0:T(8,128)S(1)}, u32[]{:S(2)}, u32[]{:S(2)}) collective-permute-start(f32[2,176,256]{2,1,0:T(8,128)S(1)} %add_up.45.refs_4_), channel_id=1, source_target_pairs={{0,2},{2,0},{4,6},{6,4},{8,10},{10,8},{12,14},{14,12},{16,18},{18,... | collective-permute-start | bytes 1081352 | tf_op jit(solution)/shard_map/ppermute | solution.py:299
  152.1 3.9 %collective-permute-done.28.refs_3_ = f32[2,176,256]{2,1,0:T(8,128)S(1)} collective-permute-done((f32[2,176,256]{2,1,0:T(8,128)S(1)}, f32[2,176,256]{2,1,0:T(8,128)S(1)}, u32[]{:S(2)}, u32[]{:S(2)}) %collective-permute-start.28) | collective-permute-done | bytes 360480 | tf_op jit(solution)/shard_map/ppermute | solution.py:299
  157.1 2.0 %collective-permute-start.32 = (f32[1,104,256]{2,1,0:T(8,128)S(1)}, f32[1,104,256]{2,1,0:T(8,128)S(1)}, u32[]{:S(2)}, u32[]{:S(2)}) collective-permute-start(f32[1,104,256]{2,1,0:T(8,128)S(1)} %add_up.46.refs_4_), channel_id=1, source_target_pairs={{0,16},{2,18},{4,20},{6,22},{8,24},{10,26},{12,28},{14,30},{16,0},... | collective-permute-start | bytes 319496 | tf_op jit(solution)/shard_map/ppermute | solution.py:299
  159.1 6.5 %collective-permute-done.30 = f32[1,176,256]{2,1,0:T(8,128)S(1)} collective-permute-done((f32[1,176,256]{2,1,0:T(8,128)S(1)}, f32[1,176,256]{2,1,0:T(8,128)S(1)}, u32[]{:S(2)}, u32[]{:S(2)}) %collective-permute-start.30) | collective-permute-done | bytes 180256 | tf_op jit(solution)/shard_map/ppermute | solution.py:299
  166.8 2.4 %place_columns.1 = (f32[256,512]{1,0:T(8,128)}, f32[256,512]{1,0:T(8,128)}) custom-call(s32[6]{0:T(128)S(1)} %pad_add_fusion.info, f32[4,256,256]{2,1,0:T(8,128)S(1)} %bitcast.73), custom_call_target="tpu_custom_call" | custom-call | tf_op jit(solution)/shard_map/place_columns/pallas_call | solution.py:283
  (71 shorter events, 26.8 us)
Async XLA Ops:
  13.5 5.8 %collective-permute-start.2 = (f32[3,2,1024,128]{3,2,1,0:T(8,128)S(1)}, f32[3,2,1024,128]{3,2,1,0:T(8,128)S(1)}, u32[]{:S(2)}, u32[]{:S(2)}) collective-permute-start(f32[3,2,1024,128]{3,2,1,0:T(8,128)S(1)} %get-tuple-element.23.refs_1_), channel_id=1, source_target_pairs={{0,1},{1,0},{2,3},{3,2},{4,5},{5,4},{6,7},{7,6},{8,9},{9,8},{10,11... | collective-permute-start | bytes 9437192 | tf_op jit(solution)/shard_map/ppermute | solution.py:303
  14.0 25.2 %collective-permute-start.1 = (f32[8,120,256]{2,1,0:T(8,128)S(1)}, f32[8,120,256]{2,1,0:T(8,128)S(1)}, u32[]{:S(2)}, u32[]{:S(2)}) collective-permute-start(f32[8,120,256]{2,1,0:T(8,128)S(1)} %bitcast.92), channel_id=1, source_target_pairs={{0,2},{2,0},{4,6},{6,4},{8,10},{10,8},{12,14},{14,12},{16,18},{18,... | collective-permute-start | bytes 2949128 | tf_op jit(solution)/shard_map/ppermute | solution.py:299
  16.6 27.4 %collective-permute-start = (f32[8,136,256]{2,1,0:T(8,128)S(1)}, f32[8,136,256]{2,1,0:T(8,128)S(1)}, u32[]{:S(2)}, u32[]{:S(2)}) collective-permute-start(f32[8,136,256]{2,1,0:T(8,128)S(1)} %bitcast.90), channel_id=1, source_target_pairs={{0,4},{2,6},{4,0},{6,2},{8,12},{10,14},{12,8},{14,10},{16,20},{18,... | collective-permute-start | bytes 3342344 | tf_op jit(solution)/shard_map/ppermute | solution.py:299
  33.7 30.8 %collective-permute-start.8 = (f32[8,144,256]{2,1,0:T(8,128)S(1)}, f32[8,144,256]{2,1,0:T(8,128)S(1)}, u32[]{:S(2)}, u32[]{:S(2)}) collective-permute-start(f32[8,144,256]{2,1,0:T(8,128)S(1)} %bitcast.88), channel_id=1, source_target_pairs={{0,2},{2,0},{4,6},{6,4},{8,10},{10,8},{12,14},{14,12},{16,18},{18,... | collective-permute-start | bytes 3538952 | tf_op jit(solution)/shard_map/ppermute | solution.py:299
  36.6 25.6 %collective-permute-start.4 = (f32[8,104,256]{2,1,0:T(8,128)S(1)}, f32[8,104,256]{2,1,0:T(8,128)S(1)}, u32[]{:S(2)}, u32[]{:S(2)}) collective-permute-start(f32[8,104,256]{2,1,0:T(8,128)S(1)} %bitcast.78), channel_id=1, source_target_pairs={{0,4},{2,6},{4,0},{6,2},{8,12},{10,14},{12,8},{14,10},{16,20},{18,... | collective-permute-start | bytes 2555912 | tf_op jit(solution)/shard_map/ppermute | solution.py:299
  39.3 21.3 %collective-permute-start.5 = (f32[4,120,256]{2,1,0:T(8,128)S(1)}, f32[4,120,256]{2,1,0:T(8,128)S(1)}, u32[]{:S(2)}, u32[]{:S(2)}) collective-permute-start(f32[4,120,256]{2,1,0:T(8,128)S(1)} %add_up.24.refs_2_), channel_id=1, source_target_pairs={{0,8},{2,10},{4,12},{6,14},{8,0},{10,2},{12,4},{14,6},{16,24},{18,... | collective-permute-start | bytes 1474568 | tf_op jit(solution)/shard_map/ppermute | solution.py:299
  44.1 20.3 %collective-permute-start.3 = (f32[4,136,256]{2,1,0:T(8,128)S(1)}, f32[4,136,256]{2,1,0:T(8,128)S(1)}, u32[]{:S(2)}, u32[]{:S(2)}) collective-permute-start(f32[4,136,256]{2,1,0:T(8,128)S(1)} %add_up.25.refs_3_), channel_id=1, source_target_pairs={{0,8},{2,10},{4,12},{6,14},{8,0},{10,2},{12,4},{14,6},{16,24},{18,... | collective-permute-start | bytes 1671176 | tf_op jit(solution)/shard_map/ppermute | solution.py:299
  60.7 8.6 %collective-permute-start.7 = (f32[2,120,256]{2,1,0:T(8,128)S(1)}, f32[2,120,256]{2,1,0:T(8,128)S(1)}, u32[]{:S(2)}, u32[]{:S(2)}) collective-permute-start(f32[2,120,256]{2,1,0:T(8,128)S(1)} %add_up.26.refs_2_), channel_id=1, source_target_pairs={{0,4},{2,6},{4,0},{6,2},{8,12},{10,14},{12,8},{14,10},{16,20},{18,... | collective-permute-start | bytes 737288 | tf_op jit(solution)/shard_map/ppermute | solution.py:299
  62.4 13.3 %collective-permute-start.11 = (f32[4,104,256]{2,1,0:T(8,128)S(1)}, f32[4,104,256]{2,1,0:T(8,128)S(1)}, u32[]{:S(2)}, u32[]{:S(2)}) collective-permute-start(f32[4,104,256]{2,1,0:T(8,128)S(1)} %add_up.27.refs_3_), channel_id=1, source_target_pairs={{0,8},{2,10},{4,12},{6,14},{8,0},{10,2},{12,4},{14,6},{16,24},{18,... | collective-permute-start | bytes 1277960 | tf_op jit(solution)/shard_map/ppermute | solution.py:299
  64.6 16.3 %collective-permute-start.13 = (f32[4,144,256]{2,1,0:T(8,128)S(1)}, f32[4,144,256]{2,1,0:T(8,128)S(1)}, u32[]{:S(2)}, u32[]{:S(2)}) collective-permute-start(f32[4,144,256]{2,1,0:T(8,128)S(1)} %add_up.29.refs_4_), channel_id=1, source_target_pairs={{0,4},{2,6},{4,0},{6,2},{8,12},{10,14},{12,8},{14,10},{16,20},{18,... | collective-permute-start | bytes 1769480 | tf_op jit(solution)/shard_map/ppermute | solution.py:299
  66.4 7.7 %collective-permute-start.6 = (f32[2,136,256]{2,1,0:T(8,128)S(1)}, f32[2,136,256]{2,1,0:T(8,128)S(1)}, u32[]{:S(2)}, u32[]{:S(2)}) collective-permute-start(f32[2,136,256]{2,1,0:T(8,128)S(1)} %add_up.28.refs_2_), channel_id=1, source_target_pairs={{0,2},{2,0},{4,6},{6,4},{8,10},{10,8},{12,14},{14,12},{16,18},{18,... | collective-permute-start | bytes 835592 | tf_op jit(solution)/shard_map/ppermute | solution.py:299
  68.8 46.1 %collective-permute-start.19 = (f32[8,176,256]{2,1,0:T(8,128)S(1)}, f32[8,176,256]{2,1,0:T(8,128)S(1)}, u32[]{:S(2)}, u32[]{:S(2)}) collective-permute-start(f32[8,176,256]{2,1,0:T(8,128)S(1)} %bitcast.72), channel_id=1, source_target_pairs={{0,4},{2,6},{4,0},{6,2},{8,12},{10,14},{12,8},{14,10},{16,20},{18,... | collective-permute-start | bytes 4325384 | tf_op jit(solution)/shard_map/ppermute | solution.py:299
  69.3 40.2 %collective-permute-start.20 = (f32[8,104,256]{2,1,0:T(8,128)S(1)}, f32[8,104,256]{2,1,0:T(8,128)S(1)}, u32[]{:S(2)}, u32[]{:S(2)}) collective-permute-start(f32[8,104,256]{2,1,0:T(8,128)S(1)} %bitcast.94), channel_id=1, source_target_pairs={{0,8},{2,10},{4,12},{6,14},{8,0},{10,2},{12,4},{14,6},{16,24},{18,... | collective-permute-start | bytes 2555912 | tf_op jit(solution)/shard_map/ppermute | solution.py:299
  74.1 33.5 %collective-permute-start.17 = (f32[8,136,256]{2,1,0:T(8,128)S(1)}, f32[8,136,256]{2,1,0:T(8,128)S(1)}, u32[]{:S(2)}, u32[]{:S(2)}) collective-permute-start(f32[8,136,256]{2,1,0:T(8,128)S(1)} %bitcast.89), channel_id=1, source_target_pairs={{0,2},{2,0},{4,6},{6,4},{8,10},{10,8},{12,14},{14,12},{16,18},{18,... | collective-permute-start | bytes 3342344 | tf_op jit(solution)/shard_map/ppermute | solution.py:299
  75.7 17.9 %collective-permute-start.9 = (f32[1,136,256]{2,1,0:T(8,128)S(1)}, f32[1,136,256]{2,1,0:T(8,128)S(1)}, u32[]{:S(2)}, u32[]{:S(2)}) collective-permute-start(f32[1,136,256]{2,1,0:T(8,128)S(1)} %add_up.31.refs_3_), channel_id=1, source_target_pairs={{0,16},{2,18},{4,20},{6,22},{8,24},{10,26},{12,28},{14,30},{16,0},... | collective-permute-start | bytes 417800 | tf_op jit(solution)/shard_map/ppermute | solution.py:299
  81.0 22.5 %collective-permute-start.12 = (f32[2,104,256]{2,1,0:T(8,128)S(1)}, f32[2,104,256]{2,1,0:T(8,128)S(1)}, u32[]{:S(2)}, u32[]{:S(2)}) collective-permute-start(f32[2,104,256]{2,1,0:T(8,128)S(1)} %add_up.32.refs_3_), channel_id=1, source_target_pairs={{0,2},{2,0},{4,6},{6,4},{8,10},{10,8},{12,14},{14,12},{16,18},{18,... | collective-permute-start | bytes 638984 | tf_op jit(solution)/shard_map/ppermute | solution.py:299
  93.6 11.4 %collective-permute-start.15 = (f32[2,144,256]{2,1,0:T(8,128)S(1)}, f32[2,144,256]{2,1,0:T(8,128)S(1)}, u32[]{:S(2)}, u32[]{:S(2)}) collective-permute-start(f32[2,144,256]{2,1,0:T(8,128)S(1)} %add_up.33.refs_4_), channel_id=1, source_target_pairs={{0,8},{2,10},{4,12},{6,14},{8,0},{10,2},{12,4},{14,6},{16,24},{18,... | collective-permute-start | bytes 884744 | tf_op jit(solution)/shard_map/ppermute | solution.py:299
  103.4 27.8 %collective-permute-start.22 = (f32[8,104,256]{2,1,0:T(8,128)S(1)}, f32[8,104,256]{2,1,0:T(8,128)S(1)}, u32[]{:S(2)}, u32[]{:S(2)}) collective-permute-start(f32[8,104,256]{2,1,0:T(8,128)S(1)} %bitcast.93), channel_id=1, source_target_pairs={{0,2},{2,0},{4,6},{6,4},{8,10},{10,8},{12,14},{14,12},{16,18},{18,... | collective-permute-start | bytes 2555912 | tf_op jit(solution)/shard_map/ppermute | solution.py:299
  105.0 7.9 %collective-permute-start.10 = (f32[1,120,256]{2,1,0:T(8,128)S(1)}, f32[1,120,256]{2,1,0:T(8,128)S(1)}, u32[]{:S(2)}, u32[]{:S(2)}) collective-permute-start(f32[1,120,256]{2,1,0:T(8,128)S(1)} %add_up.30.refs_4_), channel_id=1, source_target_pairs={{0,16},{2,18},{4,20},{6,22},{8,24},{10,26},{12,28},{14,30},{16,0},... | collective-permute-start | bytes 368648 | tf_op jit(solution)/shard_map/ppermute | solution.py:299
  107.8 22.3 %collective-permute-start.18 = (f32[4,136,256]{2,1,0:T(8,128)S(1)}, f32[4,136,256]{2,1,0:T(8,128)S(1)}, u32[]{:S(2)}, u32[]{:S(2)}) collective-permute-start(f32[4,136,256]{2,1,0:T(8,128)S(1)} %add_up.36.refs_2_), channel_id=1, source_target_pairs={{0,8},{2,10},{4,12},{6,14},{8,0},{10,2},{12,4},{14,6},{16,24},{18,... | collective-permute-start | bytes 1671176 | tf_op jit(solution)/shard_map/ppermute | solution.py:299
  109.6 22.3 %collective-permute-start.24 = (f32[4,104,256]{2,1,0:T(8,128)S(1)}, f32[4,104,256]{2,1,0:T(8,128)S(1)}, u32[]{:S(2)}, u32[]{:S(2)}) collective-permute-start(f32[4,104,256]{2,1,0:T(8,128)S(1)} %add_up.37.refs_2_), channel_id=1, source_target_pairs={{0,4},{2,6},{4,0},{6,2},{8,12},{10,14},{12,8},{14,10},{16,20},{18,... | collective-permute-start | bytes 1277960 | tf_op jit(solution)/shard_map/ppermute | solution.py:299
  112.9 19.5 %collective-permute-start.14 = (f32[1,104,256]{2,1,0:T(8,128)S(1)}, f32[1,104,256]{2,1,0:T(8,128)S(1)}, u32[]{:S(2)}, u32[]{:S(2)}) collective-permute-start(f32[1,104,256]{2,1,0:T(8,128)S(1)} %add_up.34.refs_4_), channel_id=1, source_target_pairs={{0,16},{2,18},{4,20},{6,22},{8,24},{10,26},{12,28},{14,30},{16,0},... | collective-permute-start | bytes 319496 | tf_op jit(solution)/shard_map/ppermute | solution.py:299
  115.0 33.2 %collective-permute-start.27 = (f32[4,176,256]{2,1,0:T(8,128)S(1)}, f32[4,176,256]{2,1,0:T(8,128)S(1)}, u32[]{:S(2)}, u32[]{:S(2)}) collective-permute-start(f32[4,176,256]{2,1,0:T(8,128)S(1)} %add_up.38.refs_3_), channel_id=1, source_target_pairs={{0,8},{2,10},{4,12},{6,14},{8,0},{10,2},{12,4},{14,6},{16,24},{18,... | collective-permute-start | bytes 2162696 | tf_op jit(solution)/shard_map/ppermute | solution.py:299
  130.2 15.7 %collective-permute-start.21 = (f32[2,136,256]{2,1,0:T(8,128)S(1)}, f32[2,136,256]{2,1,0:T(8,128)S(1)}, u32[]{:S(2)}, u32[]{:S(2)}) collective-permute-start(f32[2,136,256]{2,1,0:T(8,128)S(1)} %add_up.39.refs_2_), channel_id=1, source_target_pairs={{0,16},{2,18},{4,20},{6,22},{8,24},{10,26},{12,28},{14,30},{16,0},... | collective-permute-start | bytes 835592 | tf_op jit(solution)/shard_map/ppermute | solution.py:299
  131.3 8.2 %collective-permute-start.23 = (f32[4,104,256]{2,1,0:T(8,128)S(1)}, f32[4,104,256]{2,1,0:T(8,128)S(1)}, u32[]{:S(2)}, u32[]{:S(2)}) collective-permute-start(f32[4,104,256]{2,1,0:T(8,128)S(1)} %add_up.40.refs_3_), channel_id=1, source_target_pairs={{0,4},{2,6},{4,0},{6,2},{8,12},{10,14},{12,8},{14,10},{16,20},{18,... | collective-permute-start | bytes 1277960 | tf_op jit(solution)/shard_map/ppermute | solution.py:299
  131.9 5.9 %collective-permute-start.25 = (f32[2,104,256]{2,1,0:T(8,128)S(1)}, f32[2,104,256]{2,1,0:T(8,128)S(1)}, u32[]{:S(2)}, u32[]{:S(2)}) collective-permute-start(f32[2,104,256]{2,1,0:T(8,128)S(1)} %add_up.41.refs_4_), channel_id=1, source_target_pairs={{0,2},{2,0},{4,6},{6,4},{8,10},{10,8},{12,14},{14,12},{16,18},{18,... | collective-permute-start | bytes 638984 | tf_op jit(solution)/shard_map/ppermute | solution.py:299
  132.5 18.1 %collective-permute-start.16 = (f32[1,144,256]{2,1,0:T(8,128)S(1)}, f32[1,144,256]{2,1,0:T(8,128)S(1)}, u32[]{:S(2)}, u32[]{:S(2)}) collective-permute-start(f32[1,144,256]{2,1,0:T(8,128)S(1)} %add_up.35.refs_2_), channel_id=1, source_target_pairs={{0,16},{2,18},{4,20},{6,22},{8,24},{10,26},{12,28},{14,30},{16,0},... | collective-permute-start | bytes 442376 | tf_op jit(solution)/shard_map/ppermute | solution.py:299
  139.6 12.5 %collective-permute-start.29 = (f32[2,104,256]{2,1,0:T(8,128)S(1)}, f32[2,104,256]{2,1,0:T(8,128)S(1)}, u32[]{:S(2)}, u32[]{:S(2)}) collective-permute-start(f32[2,104,256]{2,1,0:T(8,128)S(1)} %add_up.43.refs_4_), channel_id=1, source_target_pairs={{0,8},{2,10},{4,12},{6,14},{8,0},{10,2},{12,4},{14,6},{16,24},{18,... | collective-permute-start | bytes 638984 | tf_op jit(solution)/shard_map/ppermute | solution.py:299
  148.3 7.7 %collective-permute-start.28 = (f32[2,176,256]{2,1,0:T(8,128)S(1)}, f32[2,176,256]{2,1,0:T(8,128)S(1)}, u32[]{:S(2)}, u32[]{:S(2)}) collective-permute-start(f32[2,176,256]{2,1,0:T(8,128)S(1)} %add_up.45.refs_4_), channel_id=1, source_target_pairs={{0,2},{2,0},{4,6},{6,4},{8,10},{10,8},{12,14},{14,12},{16,18},{18,... | collective-permute-start | bytes 1081352 | tf_op jit(solution)/shard_map/ppermute | solution.py:299
  150.6 15.0 %collective-permute-start.31 = (f32[1,104,256]{2,1,0:T(8,128)S(1)}, f32[1,104,256]{2,1,0:T(8,128)S(1)}, u32[]{:S(2)}, u32[]{:S(2)}) collective-permute-start(f32[1,104,256]{2,1,0:T(8,128)S(1)} %add_up.42.refs_3_), channel_id=1, source_target_pairs={{0,16},{2,18},{4,20},{6,22},{8,24},{10,26},{12,28},{14,30},{16,0},... | collective-permute-start | bytes 319496 | tf_op jit(solution)/shard_map/ppermute | solution.py:299
  156.0 9.6 %collective-permute-start.30 = (f32[1,176,256]{2,1,0:T(8,128)S(1)}, f32[1,176,256]{2,1,0:T(8,128)S(1)}, u32[]{:S(2)}, u32[]{:S(2)}) collective-permute-start(f32[1,176,256]{2,1,0:T(8,128)S(1)} %add_up.47), channel_id=1, source_target_pairs={{0,16},{2,18},{4,20},{6,22},{8,24},{10,26},{12,28},{14,30},{16,0},... | collective-permute-start | bytes 540680 | tf_op jit(solution)/shard_map/ppermute | solution.py:299
  157.1 9.6 %collective-permute-start.32 = (f32[1,104,256]{2,1,0:T(8,128)S(1)}, f32[1,104,256]{2,1,0:T(8,128)S(1)}, u32[]{:S(2)}, u32[]{:S(2)}) collective-permute-start(f32[1,104,256]{2,1,0:T(8,128)S(1)} %add_up.46.refs_4_), channel_id=1, source_target_pairs={{0,16},{2,18},{4,20},{6,22},{8,24},{10,26},{12,28},{14,30},{16,0},... | collective-permute-start | bytes 319496 | tf_op jit(solution)/shard_map/ppermute | solution.py:299
  (1 other events, 5.3 us)

commit v6 on v5

--- a/solution.py
+++ b/solution.py
@@ -19,14 +19,14 @@
 
 GROUPS = (
     (("yzxw", 136), ("xzyw", 120)),
-    (("yzxw", 104), ("xyzw", 144), ("xzwy", 136)),
-    (("yzxw", 176), ("zyxw", 104), ("xyzw", 104)),
+    (("yzxw", 112), ("xyzw", 152), ("xzwy", 120)),
+    (("yzxw", 144), ("zyxw", 104), ("xyzw", 136)),
 )
 
 ORDER = (
-    ("0", 50), ("1", 70), (1, 6), (0, 3), ("2", 52), (1, 3), (2, 13), (0, 3), (3, 5), (1, 18), (0, 3),
-    (2, 21), (3, 3), (2, 25), (3, 48), (4, 14), (6, 21), (5, 17), (4, 6), (7, 6), (6, 22), (6, 8), (7, 3),
-    (4, 3), (5, 20), (7, 12), (5, 6),
+    ("0", 80), ("1", 70), ((1,), 6), ((0,), 3), ("2", 52), ((1,), 3), ((2,), 13), ((3,), 5), ((0,), 3),
+    ((1,), 18), ((0,), 0), ((2,), 21), ((3,), 0), ((2,), 25), ((3,), 48), ((4,), 14), ((6,), 20), ((5,), 17),
+    ((4,), 20), ((7,), 6), ((6,), 22), ((7,), 3), ((4,), 1), ((5,), 6), ((6,), 8), ((5,), 40), ((7,), 18),
 )
 
 
@@ -242,34 +242,44 @@
     return [m.reshape(8, *m.shape[3:]) for m in made[: len(outs)]] + list(made[len(outs) :])
 
 
-def total(leaves, at):
-    value = leaves[0][at]
-    for leaf in leaves[1:]:
-        value = value + leaf[at]
-    return value
-
-
-def add_kernel(*refs):
-    refs[-1][0] = total(refs[:-2], 0)
-
-
-def add_up(leaves, count, token, beside):
-    shape = leaves[0].shape[1:]
+def add_kernel(*refs, parts):
+    refs, out_ref = refs[:-2], refs[-1]
+    start = 0
+    for width, leaves in parts:
+        value = None
+        for number, row in leaves:
+            term = refs[number][0, row : row + width]
+            value = term if value is None else value + term
+        out_ref[0, start : start + width] = value
+        start += width
+
+
+def add_up(stream, count, token, beside):
+    arrays = []
+    parts = []
+    for width, leaves in stream:
+        numbers = []
+        for array, row in leaves:
+            if not any(array is other for other in arrays):
+                arrays.append(array)
+            numbers.append(([array is other for other in arrays].index(True), row))
+        parts.append((width, numbers))
+    width = sum(part[0] for part in parts)
+    share_rows = arrays[0].shape[2]
+    size = sum(array.shape[1] for array in arrays) + width
     return pl.pallas_call(
-        add_kernel,
+        functools.partial(add_kernel, parts=parts),
         grid=(count,),
-        in_specs=[pl.BlockSpec((1, *shape), lambda i: (count + i, 0, 0))] * len(leaves)
+        in_specs=[pl.BlockSpec((1, *array.shape[1:]), lambda i: (count + i, 0, 0)) for array in arrays]
         + [pl.BlockSpec(memory_space=pl.ANY)],
-        out_specs=pl.BlockSpec((1, *shape), lambda i: (i, 0, 0)),
-        out_shape=jax.ShapeDtypeStruct((count, *shape), jnp.float32),
+        out_specs=pl.BlockSpec((1, width, share_rows), lambda i: (i, 0, 0)),
+        out_shape=jax.ShapeDtypeStruct((count, width, share_rows), jnp.float32),
         compiler_params=pltpu.CompilerParams(vmem_limit_bytes=16 << 20),
         cost_estimate=pl.CostEstimate(
-            flops=beside * FLOPS,
-            bytes_accessed=4 * count * shape[0] * shape[1] * (len(leaves) + 1),
-            transcendentals=0,
+            flops=beside * FLOPS, bytes_accessed=4 * count * share_rows * size, transcendentals=0
         ),
         name="add_up",
-    )(*leaves, token)
+    )(*arrays, token)
 
 
 def place_kernel(info, sums_ref, correlation_ref, energy_ref):
@@ -323,7 +333,7 @@
     local_blocks = local_states // BLOCK
     info = jnp.concatenate([block_ids, lax.axis_index("node")[None], lax.axis_index("state")[None]])
 
-    held = {}
+    streams, parts_made = {}, []
     first = 0
     for step, beside in ORDER:
         if isinstance(step, str):
@@ -336,15 +346,24 @@
                 own = out.pop()
                 other = swap_cores(own)
             first += sum(size for _, size in parts)
-            sent, kept = out[: len(parts)], out[len(parts) :]
-            for (bits, size), send, keep in zip(parts, sent, kept):
-                held[len(held)] = (bits, [keep, swap(send, bits[0])])
+            for (bits, size), send, keep in zip(parts, out[: len(parts)], out[len(parts) :]):
+                part = (size, [(keep, 0), (swap(send, bits[0]), 0)])
+                streams[len(parts_made)] = (bits[1:], [part])
+                parts_made.append(part)
         else:
-            bits, leaves = held[step]
-            turn = len(leaves) - 1
-            last = add_up(leaves, 8 >> turn, last, beside)
-            leaves.append(swap(last, bits[turn]))
-    results = [total(leaves, 0) for _, leaves in held.values()]
+            bits = streams[step[0]][0]
+            stream = [part for number in step for part in streams[number][1]]
+            last = add_up(stream, 1 << (len(bits) - 1), last, beside)
+            received = swap(last, bits[0])
+            row = 0
+            for size, leaves in stream:
+                leaves.append((received, row))
+                row += size
+            streams[step[0]] = (bits[1:], stream)
+    results = []
+    for size, leaves in parts_made:
+        terms = [array[0, row : row + size] for array, row in leaves]
+        results.append(sum(terms[1:], terms[0]))
     sums = jnp.concatenate(results).reshape(NBLK, 2 * BLOCK, share_rows)
     return tuple(place_columns(sums, info, share_rows, local_blocks))
 

time: 169 us -> 168 us (level)
  starting transfers between devices: 57 us -> 54.9 us
    ppermute x32, starting transfers between devices: 56.5 us -> 54.4 us  [swap(): lax.ppermute(value, 'node', [(i, i ^ bit) for i in range(lax.axis_size('n...]
where the time goes in v6:
time: 168 us; the launch traced here: 167 us
  waiting for transfers between devices  65.1 us (39%)
  starting transfers between devices  54.9 us (33%)
  Pallas kernels  45.4 us (27%)
    ppermute x32, waiting for transfers between devices, swap(): lax.ppermute(value, 'node', [(i, i ^ bit) for i in range(lax.axis_size('n...  63.9 us
    ppermute x32, starting transfers between devices, swap(): lax.ppermute(value, 'node', [(i, i ^ bit) for i in range(lax.axis_size('n...  54.4 us
    pallas_call x3, Pallas kernels, partial_sums(): pl.pallas_call(functools.partial(partial_kernel, outs=outs, first=first,...  41.3 us
  transfers between devices with their start and end apart: 33, of which 17 were waited for; matrix products, arithmetic and copies ran while one was open for 0% of the time, Pallas kernels for 18%

profile of v6, /device:TPU:0, one launch (start us, length us, event | category | flops | bytes accessed | tf_op | source)
XLA Modules:
  0.0 167.5 jit_solution(9676555521887993357)
XLA Ops:
  1.4 12.1 %partial_sums.3 = (f32[2,2,2,136,256]{4,3,2,1,0:T(8,128)S(1)}, f32[2,2,2,120,256]{4,3,2,1,0:T(8,128)S(1)}, f32[2,2,2,136,256]{4,3,2,1,0:T(8,128)S(1)}, f32[2,2,2...) custom-call(s32[6]{0:T(128)S(1)} %pad_add_fusion.info, f32[1024,4096]{1,0:T(8,128)} %refs_0_.5, f32[1024,4096]{1,0:T(8,128)} %refs_1_.1), custom_call_target="tpu_custom_call" | custom-call | flops 9200000000 | bytes 20971520 | tf_op jit(solution)/shard_map/partial_sums/pallas_call | solution.py:204
  14.0 2.6 %collective-permute-start.1 = (f32[8,120,256]{2,1,0:T(8,128)S(1)}, f32[8,120,256]{2,1,0:T(8,128)S(1)}, u32[]{:S(2)}, u32[]{:S(2)}) collective-permute-start(f32[8,120,256]{2,1,0:T(8,128)S(1)} %bitcast.93), channel_id=1, source_target_pairs={{0,2},{2,0},{4,6},{6,4},{8,10},{10,8},{12,14},{14,12},{16,18},{18,... | collective-permute-start | bytes 2949128 | tf_op jit(solution)/shard_map/ppermute | solution.py:309
  19.3 14.4 %partial_sums.4 = (f32[2,2,2,112,256]{4,3,2,1,0:T(8,128)S(1)}, f32[2,2,2,152,256]{4,3,2,1,0:T(8,128)S(1)}, f32[2,2,2,120,256]{4,3,2,1,0:T(8,128)S(1)}, f32[2,2,2...) custom-call(s32[6]{0:T(128)S(1)} %pad_add_fusion.info, ...), custom_call_target="tpu_custom_call" | custom-call | flops 8049999872 | bytes 23068672 | tf_op jit(solution)/shard_map/partial_sums/pallas_call | solution.py:204
  33.7 2.9 %collective-permute-start.4 = (f32[8,152,256]{2,1,0:T(8,128)S(1)}, f32[8,152,256]{2,1,0:T(8,128)S(1)}, u32[]{:S(2)}, u32[]{:S(2)}) collective-permute-start(f32[8,152,256]{2,1,0:T(8,128)S(1)} %bitcast.88), channel_id=1, source_target_pairs={{0,2},{2,0},{4,6},{6,4},{8,10},{10,8},{12,14},{14,12},{16,18},{18,... | collective-permute-start | bytes 3735560 | tf_op jit(solution)/shard_map/ppermute | solution.py:309
  39.3 2.1 %collective-permute-start.6 = (f32[4,120,256]{2,1,0:T(8,128)S(1)}, f32[4,120,256]{2,1,0:T(8,128)S(1)}, u32[]{:S(2)}, u32[]{:S(2)}) collective-permute-start(f32[4,120,256]{2,1,0:T(8,128)S(1)} %add_up.24.refs_2_), channel_id=1, source_target_pairs={{0,8},{2,10},{4,12},{6,14},{8,0},{10,2},{12,4},{14,6},{16,24},{18,... | collective-permute-start | bytes 1474568 | tf_op jit(solution)/shard_map/ppermute | solution.py:309
  41.4 2.6 %collective-permute-done.refs_1_ = f32[8,136,256]{2,1,0:T(8,128)S(1)} collective-permute-done((f32[8,136,256]{2,1,0:T(8,128)S(1)}, f32[8,136,256]{2,1,0:T(8,128)S(1)}, u32[]{:S(2)}, u32[]{:S(2)}) %collective-permute-start) | collective-permute-done | bytes 1114144 | tf_op jit(solution)/shard_map/ppermute | solution.py:309
  44.1 1.6 collective-permute-start.3
  45.8 14.8 %partial_sums.5 = (f32[2,2,2,144,256]{4,3,2,1,0:T(8,128)S(1)}, f32[2,2,2,104,256]{4,3,2,1,0:T(8,128)S(1)}, f32[2,2,2,136,256]{4,3,2,1,0:T(8,128)S(1)}, f32[2,2,2...) custom-call(s32[6]{0:T(128)S(1)} %pad_add_fusion.info, ...), custom_call_target="tpu_custom_call" | custom-call | flops 5980000256 | bytes 23068672 | tf_op jit(solution)/shard_map/partial_sums/pallas_call | solution.py:204
  60.7 2.2 %collective-permute-done.5.refs_1_ = f32[8,112,256]{2,1,0:T(8,128)S(1)} collective-permute-done((f32[8,112,256]{2,1,0:T(8,128)S(1)}, f32[8,112,256]{2,1,0:T(8,128)S(1)}, u32[]{:S(2)}, u32[]{:S(2)}) %collective-permute-start.5) | collective-permute-done | bytes 917536 | tf_op jit(solution)/shard_map/ppermute | solution.py:309
  69.8 3.8 %collective-permute-done.8.refs_3_ = f32[2,120,256]{2,1,0:T(8,128)S(1)} collective-permute-done((f32[2,120,256]{2,1,0:T(8,128)S(1)}, f32[2,120,256]{2,1,0:T(8,128)S(1)}, u32[]{:S(2)}, u32[]{:S(2)}) %collective-permute-start.8) | collective-permute-done | bytes 245792 | tf_op jit(solution)/shard_map/ppermute | solution.py:309
  74.0 1.7 %collective-permute-done.7.refs_3_ = f32[2,136,256]{2,1,0:T(8,128)S(1)} collective-permute-done((f32[2,136,256]{2,1,0:T(8,128)S(1)}, f32[2,136,256]{2,1,0:T(8,128)S(1)}, u32[]{:S(2)}, u32[]{:S(2)}) %collective-permute-start.7) | collective-permute-done | bytes 278560 | tf_op jit(solution)/shard_map/ppermute | solution.py:309
  77.2 2.7 %collective-permute-start.9 = (f32[1,136,256]{2,1,0:T(8,128)S(1)}, f32[1,136,256]{2,1,0:T(8,128)S(1)}, u32[]{:S(2)}, u32[]{:S(2)}) collective-permute-start(f32[1,136,256]{2,1,0:T(8,128)S(1)} %add_up.31.refs_3_), channel_id=1, source_target_pairs={{0,16},{2,18},{4,20},{6,22},{8,24},{10,26},{12,28},{14,30},{16,0},... | collective-permute-start | bytes 417800 | tf_op jit(solution)/shard_map/ppermute | solution.py:309
  80.0 6.9 %collective-permute-done.13.refs_2_ = f32[4,152,256]{2,1,0:T(8,128)S(1)} collective-permute-done((f32[4,152,256]{2,1,0:T(8,128)S(1)}, f32[4,152,256]{2,1,0:T(8,128)S(1)}, u32[]{:S(2)}, u32[]{:S(2)}) %collective-permute-start.13) | collective-permute-done | bytes 622624 | tf_op jit(solution)/shard_map/ppermute | solution.py:309
  87.5 7.7 %collective-permute-done.9 = f32[1,136,256]{2,1,0:T(8,128)S(1)} collective-permute-done((f32[1,136,256]{2,1,0:T(8,128)S(1)}, f32[1,136,256]{2,1,0:T(8,128)S(1)}, u32[]{:S(2)}, u32[]{:S(2)}) %collective-permute-start.9) | collective-permute-done | bytes 139296 | tf_op jit(solution)/shard_map/ppermute | solution.py:309
  95.2 3.5 %collective-permute-start.15 = (f32[2,152,256]{2,1,0:T(8,128)S(1)}, f32[2,152,256]{2,1,0:T(8,128)S(1)}, u32[]{:S(2)}, u32[]{:S(2)}) collective-permute-start(f32[2,152,256]{2,1,0:T(8,128)S(1)} %add_up.33.refs_4_), channel_id=1, source_target_pairs={{0,8},{2,10},{4,12},{6,14},{8,0},{10,2},{12,4},{14,6},{16,24},{18,... | collective-permute-start | bytes 933896 | tf_op jit(solution)/shard_map/ppermute | solution.py:309
  98.7 4.0 %collective-permute-done.12.refs_3_ = f32[2,112,256]{2,1,0:T(8,128)S(1)} collective-permute-done((f32[2,112,256]{2,1,0:T(8,128)S(1)}, f32[2,112,256]{2,1,0:T(8,128)S(1)}, u32[]{:S(2)}, u32[]{:S(2)}) %collective-permute-start.12) | collective-permute-done | bytes 229408 | tf_op jit(solution)/shard_map/ppermute | solution.py:309
  104.2 2.7 %collective-permute-start.10 = (f32[1,120,256]{2,1,0:T(8,128)S(1)}, f32[1,120,256]{2,1,0:T(8,128)S(1)}, u32[]{:S(2)}, u32[]{:S(2)}) collective-permute-start(f32[1,120,256]{2,1,0:T(8,128)S(1)} %add_up.30.refs_4_), channel_id=1, source_target_pairs={{0,16},{2,18},{4,20},{6,22},{8,24},{10,26},{12,28},{14,30},{16,0},... | collective-permute-start | bytes 368648 | tf_op jit(solution)/shard_map/ppermute | solution.py:309
  108.7 2.0 %collective-permute-done.10 = f32[1,120,256]{2,1,0:T(8,128)S(1)} collective-permute-done((f32[1,120,256]{2,1,0:T(8,128)S(1)}, f32[1,120,256]{2,1,0:T(8,128)S(1)}, u32[]{:S(2)}, u32[]{:S(2)}) %collective-permute-start.10) | collective-permute-done | bytes 122912 | tf_op jit(solution)/shard_map/ppermute | solution.py:309
  110.7 3.4 %collective-permute-start.14 = (f32[1,112,256]{2,1,0:T(8,128)S(1)}, f32[1,112,256]{2,1,0:T(8,128)S(1)}, u32[]{:S(2)}, u32[]{:S(2)}) collective-permute-start(f32[1,112,256]{2,1,0:T(8,128)S(1)} %add_up.34.refs_4_), channel_id=1, source_target_pairs={{0,16},{2,18},{4,20},{6,22},{8,24},{10,26},{12,28},{14,30},{16,0},... | collective-permute-start | bytes 344072 | tf_op jit(solution)/shard_map/ppermute | solution.py:309
  115.0 1.7 %collective-permute-start.26 = (f32[4,144,256]{2,1,0:T(8,128)S(1)}, f32[4,144,256]{2,1,0:T(8,128)S(1)}, u32[]{:S(2)}, u32[]{:S(2)}) collective-permute-start(f32[4,144,256]{2,1,0:T(8,128)S(1)} %add_up.38.refs_3_), channel_id=1, source_target_pairs={{0,8},{2,10},{4,12},{6,14},{8,0},{10,2},{12,4},{14,6},{16,24},{18,... | collective-permute-start | bytes 1769480 | tf_op jit(solution)/shard_map/ppermute | solution.py:309
  116.8 7.0 %collective-permute-done.18.refs_2_ = f32[4,120,256]{2,1,0:T(8,128)S(1)} collective-permute-done((f32[4,120,256]{2,1,0:T(8,128)S(1)}, f32[4,120,256]{2,1,0:T(8,128)S(1)}, u32[]{:S(2)}, u32[]{:S(2)}) %collective-permute-start.18) | collective-permute-done | bytes 491552 | tf_op jit(solution)/shard_map/ppermute | solution.py:309
  123.8 2.9 %collective-permute-done.22.refs_1_ = f32[8,136,256]{2,1,0:T(8,128)S(1)} collective-permute-done((f32[8,136,256]{2,1,0:T(8,128)S(1)}, f32[8,136,256]{2,1,0:T(8,128)S(1)}, u32[]{:S(2)}, u32[]{:S(2)}) %collective-permute-start.22) | collective-permute-done | bytes 1114144 | tf_op jit(solution)/shard_map/ppermute | solution.py:309
  127.2 2.6 %collective-permute-start.16 = (f32[1,152,256]{2,1,0:T(8,128)S(1)}, f32[1,152,256]{2,1,0:T(8,128)S(1)}, u32[]{:S(2)}, u32[]{:S(2)}) collective-permute-start(f32[1,152,256]{2,1,0:T(8,128)S(1)} %add_up.35.refs_2_), channel_id=1, source_target_pairs={{0,16},{2,18},{4,20},{6,22},{8,24},{10,26},{12,28},{14,30},{16,0},... | collective-permute-start | bytes 466952 | tf_op jit(solution)/shard_map/ppermute | solution.py:309
  130.3 1.8 %collective-permute-start.28 = (f32[2,104,256]{2,1,0:T(8,128)S(1)}, f32[2,104,256]{2,1,0:T(8,128)S(1)}, u32[]{:S(2)}, u32[]{:S(2)}) collective-permute-start(f32[2,104,256]{2,1,0:T(8,128)S(1)} %add_up.41.refs_3_), channel_id=1, source_target_pairs={{0,2},{2,0},{4,6},{6,4},{8,10},{10,8},{12,14},{14,12},{16,18},{18,... | collective-permute-start | bytes 638984 | tf_op jit(solution)/shard_map/ppermute | solution.py:309
  132.1 7.6 %collective-permute-done.16 = f32[1,152,256]{2,1,0:T(8,128)S(1)} collective-permute-done((f32[1,152,256]{2,1,0:T(8,128)S(1)}, f32[1,152,256]{2,1,0:T(8,128)S(1)}, u32[]{:S(2)}, u32[]{:S(2)}) %collective-permute-start.16) | collective-permute-done | bytes 155680 | tf_op jit(solution)/shard_map/ppermute | solution.py:309
  139.9 2.4 %collective-permute-start.31 = (f32[2,136,256]{2,1,0:T(8,128)S(1)}, f32[2,136,256]{2,1,0:T(8,128)S(1)}, u32[]{:S(2)}, u32[]{:S(2)}) collective-permute-start(f32[2,136,256]{2,1,0:T(8,128)S(1)} %add_up.42.refs_4_), channel_id=1, source_target_pairs={{0,8},{2,10},{4,12},{6,14},{8,0},{10,2},{12,4},{14,6},{16,24},{18,... | collective-permute-start | bytes 835592 | tf_op jit(solution)/shard_map/ppermute | solution.py:309
  142.3 2.7 %collective-permute-done.21.refs_3_ = f32[2,120,256]{2,1,0:T(8,128)S(1)} collective-permute-done((f32[2,120,256]{2,1,0:T(8,128)S(1)}, f32[2,120,256]{2,1,0:T(8,128)S(1)}, u32[]{:S(2)}, u32[]{:S(2)}) %collective-permute-start.21) | collective-permute-done | bytes 245792 | tf_op jit(solution)/shard_map/ppermute | solution.py:309
  145.7 3.9 %collective-permute-start.27 = (f32[2,144,256]{2,1,0:T(8,128)S(1)}, f32[2,144,256]{2,1,0:T(8,128)S(1)}, u32[]{:S(2)}, u32[]{:S(2)}) collective-permute-start(f32[2,144,256]{2,1,0:T(8,128)S(1)} %add_up.44.refs_4_), channel_id=1, source_target_pairs={{0,2},{2,0},{4,6},{6,4},{8,10},{10,8},{12,14},{14,12},{16,18},{18,... | collective-permute-start | bytes 884744 | tf_op jit(solution)/shard_map/ppermute | solution.py:309
  150.0 4.3 %collective-permute-done.27.refs_3_ = f32[2,144,256]{2,1,0:T(8,128)S(1)} collective-permute-done((f32[2,144,256]{2,1,0:T(8,128)S(1)}, f32[2,144,256]{2,1,0:T(8,128)S(1)}, u32[]{:S(2)}, u32[]{:S(2)}) %collective-permute-start.27) | collective-permute-done | bytes 294944 | tf_op jit(solution)/shard_map/ppermute | solution.py:309
  157.5 4.6 %collective-permute-done.29 = f32[1,144,256]{2,1,0:T(8,128)S(1)} collective-permute-done((f32[1,144,256]{2,1,0:T(8,128)S(1)}, f32[1,144,256]{2,1,0:T(8,128)S(1)}, u32[]{:S(2)}, u32[]{:S(2)}) %collective-permute-start.29) | collective-permute-done | bytes 147488 | tf_op jit(solution)/shard_map/ppermute | solution.py:309
  162.2 2.9 %collective-permute-done.32 = f32[1,136,256]{2,1,0:T(8,128)S(1)} collective-permute-done((f32[1,136,256]{2,1,0:T(8,128)S(1)}, f32[1,136,256]{2,1,0:T(8,128)S(1)}, u32[]{:S(2)}, u32[]{:S(2)}) %collective-permute-start.32) | collective-permute-done | bytes 139296 | tf_op jit(solution)/shard_map/ppermute | solution.py:309
  165.1 2.4 %place_columns.1 = (f32[256,512]{1,0:T(8,128)}, f32[256,512]{1,0:T(8,128)}) custom-call(s32[6]{0:T(128)S(1)} %pad_add_fusion.info, f32[4,256,256]{2,1,0:T(8,128)S(1)} %bitcast.71), custom_call_target="tpu_custom_call" | custom-call | tf_op jit(solution)/shard_map/place_columns/pallas_call | solution.py:293
  (71 shorter events, 26.0 us)
Async XLA Ops:
  13.5 5.8 %collective-permute-start.2 = (f32[3,2,1024,128]{3,2,1,0:T(8,128)S(1)}, f32[3,2,1024,128]{3,2,1,0:T(8,128)S(1)}, u32[]{:S(2)}, u32[]{:S(2)}) collective-permute-start(f32[3,2,1024,128]{3,2,1,0:T(8,128)S(1)} %get-tuple-element.23.refs_1_), channel_id=1, source_target_pairs={{0,1},{1,0},{2,3},{3,2},{4,5},{5,4},{6,7},{7,6},{8,9},{9,8},{10,11... | collective-permute-start | bytes 9437192 | tf_op jit(solution)/shard_map/ppermute | solution.py:313
  14.0 25.2 %collective-permute-start.1 = (f32[8,120,256]{2,1,0:T(8,128)S(1)}, f32[8,120,256]{2,1,0:T(8,128)S(1)}, u32[]{:S(2)}, u32[]{:S(2)}) collective-permute-start(f32[8,120,256]{2,1,0:T(8,128)S(1)} %bitcast.93), channel_id=1, source_target_pairs={{0,2},{2,0},{4,6},{6,4},{8,10},{10,8},{12,14},{14,12},{16,18},{18,... | collective-permute-start | bytes 2949128 | tf_op jit(solution)/shard_map/ppermute | solution.py:309
  16.6 27.4 %collective-permute-start = (f32[8,136,256]{2,1,0:T(8,128)S(1)}, f32[8,136,256]{2,1,0:T(8,128)S(1)}, u32[]{:S(2)}, u32[]{:S(2)}) collective-permute-start(f32[8,136,256]{2,1,0:T(8,128)S(1)} %bitcast.90), channel_id=1, source_target_pairs={{0,4},{2,6},{4,0},{6,2},{8,12},{10,14},{12,8},{14,10},{16,20},{18,... | collective-permute-start | bytes 3342344 | tf_op jit(solution)/shard_map/ppermute | solution.py:309
  33.7 32.4 %collective-permute-start.4 = (f32[8,152,256]{2,1,0:T(8,128)S(1)}, f32[8,152,256]{2,1,0:T(8,128)S(1)}, u32[]{:S(2)}, u32[]{:S(2)}) collective-permute-start(f32[8,152,256]{2,1,0:T(8,128)S(1)} %bitcast.88), channel_id=1, source_target_pairs={{0,2},{2,0},{4,6},{6,4},{8,10},{10,8},{12,14},{14,12},{16,18},{18,... | collective-permute-start | bytes 3735560 | tf_op jit(solution)/shard_map/ppermute | solution.py:309
  36.7 26.2 %collective-permute-start.5 = (f32[8,112,256]{2,1,0:T(8,128)S(1)}, f32[8,112,256]{2,1,0:T(8,128)S(1)}, u32[]{:S(2)}, u32[]{:S(2)}) collective-permute-start(f32[8,112,256]{2,1,0:T(8,128)S(1)} %bitcast.78), channel_id=1, source_target_pairs={{0,4},{2,6},{4,0},{6,2},{8,12},{10,14},{12,8},{14,10},{16,20},{18,... | collective-permute-start | bytes 2752520 | tf_op jit(solution)/shard_map/ppermute | solution.py:309
  39.3 21.2 %collective-permute-start.6 = (f32[4,120,256]{2,1,0:T(8,128)S(1)}, f32[4,120,256]{2,1,0:T(8,128)S(1)}, u32[]{:S(2)}, u32[]{:S(2)}) collective-permute-start(f32[4,120,256]{2,1,0:T(8,128)S(1)} %add_up.24.refs_2_), channel_id=1, source_target_pairs={{0,8},{2,10},{4,12},{6,14},{8,0},{10,2},{12,4},{14,6},{16,24},{18,... | collective-permute-start | bytes 1474568 | tf_op jit(solution)/shard_map/ppermute | solution.py:309
  44.1 23.5 %collective-permute-start.3 = (f32[4,136,256]{2,1,0:T(8,128)S(1)}, f32[4,136,256]{2,1,0:T(8,128)S(1)}, u32[]{:S(2)}, u32[]{:S(2)}) collective-permute-start(f32[4,136,256]{2,1,0:T(8,128)S(1)} %add_up.25.refs_3_), channel_id=1, source_target_pairs={{0,8},{2,10},{4,12},{6,14},{8,0},{10,2},{12,4},{14,6},{16,24},{18,... | collective-permute-start | bytes 1671176 | tf_op jit(solution)/shard_map/ppermute | solution.py:309
  63.0 14.2 %collective-permute-start.11 = (f32[4,112,256]{2,1,0:T(8,128)S(1)}, f32[4,112,256]{2,1,0:T(8,128)S(1)}, u32[]{:S(2)}, u32[]{:S(2)}) collective-permute-start(f32[4,112,256]{2,1,0:T(8,128)S(1)} %add_up.27.refs_2_), channel_id=1, source_target_pairs={{0,8},{2,10},{4,12},{6,14},{8,0},{10,2},{12,4},{14,6},{16,24},{18,... | collective-permute-start | bytes 1376264 | tf_op jit(solution)/shard_map/ppermute | solution.py:309
  64.6 8.9 %collective-permute-start.8 = (f32[2,120,256]{2,1,0:T(8,128)S(1)}, f32[2,120,256]{2,1,0:T(8,128)S(1)}, u32[]{:S(2)}, u32[]{:S(2)}) collective-permute-start(f32[2,120,256]{2,1,0:T(8,128)S(1)} %add_up.26.refs_2_), channel_id=1, source_target_pairs={{0,4},{2,6},{4,0},{6,2},{8,12},{10,14},{12,8},{14,10},{16,20},{18,... | collective-permute-start | bytes 737288 | tf_op jit(solution)/shard_map/ppermute | solution.py:309
  66.3 20.6 %collective-permute-start.13 = (f32[4,152,256]{2,1,0:T(8,128)S(1)}, f32[4,152,256]{2,1,0:T(8,128)S(1)}, u32[]{:S(2)}, u32[]{:S(2)}) collective-permute-start(f32[4,152,256]{2,1,0:T(8,128)S(1)} %add_up.28.refs_3_), channel_id=1, source_target_pairs={{0,4},{2,6},{4,0},{6,2},{8,12},{10,14},{12,8},{14,10},{16,20},{18,... | collective-permute-start | bytes 1867784 | tf_op jit(solution)/shard_map/ppermute | solution.py:309
  67.7 8.0 %collective-permute-start.7 = (f32[2,136,256]{2,1,0:T(8,128)S(1)}, f32[2,136,256]{2,1,0:T(8,128)S(1)}, u32[]{:S(2)}, u32[]{:S(2)}) collective-permute-start(f32[2,136,256]{2,1,0:T(8,128)S(1)} %add_up.29.refs_4_), channel_id=1, source_target_pairs={{0,2},{2,0},{4,6},{6,4},{8,10},{10,8},{12,14},{14,12},{16,18},{18,... | collective-permute-start | bytes 835592 | tf_op jit(solution)/shard_map/ppermute | solution.py:309
  69.2 45.7 %collective-permute-start.19 = (f32[8,144,256]{2,1,0:T(8,128)S(1)}, f32[8,144,256]{2,1,0:T(8,128)S(1)}, u32[]{:S(2)}, u32[]{:S(2)}) collective-permute-start(f32[8,144,256]{2,1,0:T(8,128)S(1)} %bitcast.77), channel_id=1, source_target_pairs={{0,4},{2,6},{4,0},{6,2},{8,12},{10,14},{12,8},{14,10},{16,20},{18,... | collective-permute-start | bytes 3538952 | tf_op jit(solution)/shard_map/ppermute | solution.py:309
  73.5 40.7 %collective-permute-start.20 = (f32[8,104,256]{2,1,0:T(8,128)S(1)}, f32[8,104,256]{2,1,0:T(8,128)S(1)}, u32[]{:S(2)}, u32[]{:S(2)}) collective-permute-start(f32[8,104,256]{2,1,0:T(8,128)S(1)} %bitcast.94), channel_id=1, source_target_pairs={{0,8},{2,10},{4,12},{6,14},{8,0},{10,2},{12,4},{14,6},{16,24},{18,... | collective-permute-start | bytes 2555912 | tf_op jit(solution)/shard_map/ppermute | solution.py:309
  75.7 31.3 %collective-permute-start.17 = (f32[8,120,256]{2,1,0:T(8,128)S(1)}, f32[8,120,256]{2,1,0:T(8,128)S(1)}, u32[]{:S(2)}, u32[]{:S(2)}) collective-permute-start(f32[8,120,256]{2,1,0:T(8,128)S(1)} %bitcast.92), channel_id=1, source_target_pairs={{0,2},{2,0},{4,6},{6,4},{8,10},{10,8},{12,14},{14,12},{16,18},{18,... | collective-permute-start | bytes 2949128 | tf_op jit(solution)/shard_map/ppermute | solution.py:309
  77.2 17.9 %collective-permute-start.9 = (f32[1,136,256]{2,1,0:T(8,128)S(1)}, f32[1,136,256]{2,1,0:T(8,128)S(1)}, u32[]{:S(2)}, u32[]{:S(2)}) collective-permute-start(f32[1,136,256]{2,1,0:T(8,128)S(1)} %add_up.31.refs_3_), channel_id=1, source_target_pairs={{0,16},{2,18},{4,20},{6,22},{8,24},{10,26},{12,28},{14,30},{16,0},... | collective-permute-start | bytes 417800 | tf_op jit(solution)/shard_map/ppermute | solution.py:309
  86.9 15.9 %collective-permute-start.12 = (f32[2,112,256]{2,1,0:T(8,128)S(1)}, f32[2,112,256]{2,1,0:T(8,128)S(1)}, u32[]{:S(2)}, u32[]{:S(2)}) collective-permute-start(f32[2,112,256]{2,1,0:T(8,128)S(1)} %add_up.32.refs_3_), channel_id=1, source_target_pairs={{0,2},{2,0},{4,6},{6,4},{8,10},{10,8},{12,14},{14,12},{16,18},{18,... | collective-permute-start | bytes 688136 | tf_op jit(solution)/shard_map/ppermute | solution.py:309
  95.2 9.1 %collective-permute-start.15 = (f32[2,152,256]{2,1,0:T(8,128)S(1)}, f32[2,152,256]{2,1,0:T(8,128)S(1)}, u32[]{:S(2)}, u32[]{:S(2)}) collective-permute-start(f32[2,152,256]{2,1,0:T(8,128)S(1)} %add_up.33.refs_4_), channel_id=1, source_target_pairs={{0,8},{2,10},{4,12},{6,14},{8,0},{10,2},{12,4},{14,6},{16,24},{18,... | collective-permute-start | bytes 933896 | tf_op jit(solution)/shard_map/ppermute | solution.py:309
  102.7 24.0 %collective-permute-start.22 = (f32[8,136,256]{2,1,0:T(8,128)S(1)}, f32[8,136,256]{2,1,0:T(8,128)S(1)}, u32[]{:S(2)}, u32[]{:S(2)}) collective-permute-start(f32[8,136,256]{2,1,0:T(8,128)S(1)} %bitcast.89), channel_id=1, source_target_pairs={{0,2},{2,0},{4,6},{6,4},{8,10},{10,8},{12,14},{14,12},{16,18},{18,... | collective-permute-start | bytes 3342344 | tf_op jit(solution)/shard_map/ppermute | solution.py:309
  104.2 6.4 %collective-permute-start.10 = (f32[1,120,256]{2,1,0:T(8,128)S(1)}, f32[1,120,256]{2,1,0:T(8,128)S(1)}, u32[]{:S(2)}, u32[]{:S(2)}) collective-permute-start(f32[1,120,256]{2,1,0:T(8,128)S(1)} %add_up.30.refs_4_), channel_id=1, source_target_pairs={{0,16},{2,18},{4,20},{6,22},{8,24},{10,26},{12,28},{14,30},{16,0},... | collective-permute-start | bytes 368648 | tf_op jit(solution)/shard_map/ppermute | solution.py:309
  107.1 16.7 %collective-permute-start.18 = (f32[4,120,256]{2,1,0:T(8,128)S(1)}, f32[4,120,256]{2,1,0:T(8,128)S(1)}, u32[]{:S(2)}, u32[]{:S(2)}) collective-permute-start(f32[4,120,256]{2,1,0:T(8,128)S(1)} %add_up.36.refs_2_), channel_id=1, source_target_pairs={{0,8},{2,10},{4,12},{6,14},{8,0},{10,2},{12,4},{14,6},{16,24},{18,... | collective-permute-start | bytes 1474568 | tf_op jit(solution)/shard_map/ppermute | solution.py:309
  110.7 16.4 %collective-permute-start.14 = (f32[1,112,256]{2,1,0:T(8,128)S(1)}, f32[1,112,256]{2,1,0:T(8,128)S(1)}, u32[]{:S(2)}, u32[]{:S(2)}) collective-permute-start(f32[1,112,256]{2,1,0:T(8,128)S(1)} %add_up.34.refs_4_), channel_id=1, source_target_pairs={{0,16},{2,18},{4,20},{6,22},{8,24},{10,26},{12,28},{14,30},{16,0},... | collective-permute-start | bytes 344072 | tf_op jit(solution)/shard_map/ppermute | solution.py:309
  114.3 15.9 %collective-permute-start.24 = (f32[4,104,256]{2,1,0:T(8,128)S(1)}, f32[4,104,256]{2,1,0:T(8,128)S(1)}, u32[]{:S(2)}, u32[]{:S(2)}) collective-permute-start(f32[4,104,256]{2,1,0:T(8,128)S(1)} %add_up.37.refs_2_), channel_id=1, source_target_pairs={{0,4},{2,6},{4,0},{6,2},{8,12},{10,14},{12,8},{14,10},{16,20},{18,... | collective-permute-start | bytes 1277960 | tf_op jit(solution)/shard_map/ppermute | solution.py:309
  115.0 30.6 %collective-permute-start.26 = (f32[4,144,256]{2,1,0:T(8,128)S(1)}, f32[4,144,256]{2,1,0:T(8,128)S(1)}, u32[]{:S(2)}, u32[]{:S(2)}) collective-permute-start(f32[4,144,256]{2,1,0:T(8,128)S(1)} %add_up.38.refs_3_), channel_id=1, source_target_pairs={{0,8},{2,10},{4,12},{6,14},{8,0},{10,2},{12,4},{14,6},{16,24},{18,... | collective-permute-start | bytes 1769480 | tf_op jit(solution)/shard_map/ppermute | solution.py:309
  126.9 12.9 %collective-permute-start.23 = (f32[4,136,256]{2,1,0:T(8,128)S(1)}, f32[4,136,256]{2,1,0:T(8,128)S(1)}, u32[]{:S(2)}, u32[]{:S(2)}) collective-permute-start(f32[4,136,256]{2,1,0:T(8,128)S(1)} %add_up.40.refs_3_), channel_id=1, source_target_pairs={{0,4},{2,6},{4,0},{6,2},{8,12},{10,14},{12,8},{14,10},{16,20},{18,... | collective-permute-start | bytes 1671176 | tf_op jit(solution)/shard_map/ppermute | solution.py:309
  127.2 12.5 %collective-permute-start.16 = (f32[1,152,256]{2,1,0:T(8,128)S(1)}, f32[1,152,256]{2,1,0:T(8,128)S(1)}, u32[]{:S(2)}, u32[]{:S(2)}) collective-permute-start(f32[1,152,256]{2,1,0:T(8,128)S(1)} %add_up.35.refs_2_), channel_id=1, source_target_pairs={{0,16},{2,18},{4,20},{6,22},{8,24},{10,26},{12,28},{14,30},{16,0},... | collective-permute-start | bytes 466952 | tf_op jit(solution)/shard_map/ppermute | solution.py:309
  129.9 15.1 %collective-permute-start.21 = (f32[2,120,256]{2,1,0:T(8,128)S(1)}, f32[2,120,256]{2,1,0:T(8,128)S(1)}, u32[]{:S(2)}, u32[]{:S(2)}) collective-permute-start(f32[2,120,256]{2,1,0:T(8,128)S(1)} %add_up.39.refs_2_), channel_id=1, source_target_pairs={{0,16},{2,18},{4,20},{6,22},{8,24},{10,26},{12,28},{14,30},{16,0},... | collective-permute-start | bytes 737288 | tf_op jit(solution)/shard_map/ppermute | solution.py:309
  130.3 19.4 %collective-permute-start.28 = (f32[2,104,256]{2,1,0:T(8,128)S(1)}, f32[2,104,256]{2,1,0:T(8,128)S(1)}, u32[]{:S(2)}, u32[]{:S(2)}) collective-permute-start(f32[2,104,256]{2,1,0:T(8,128)S(1)} %add_up.41.refs_3_), channel_id=1, source_target_pairs={{0,2},{2,0},{4,6},{6,4},{8,10},{10,8},{12,14},{14,12},{16,18},{18,... | collective-permute-start | bytes 638984 | tf_op jit(solution)/shard_map/ppermute | solution.py:309
  139.9 16.1 %collective-permute-start.31 = (f32[2,136,256]{2,1,0:T(8,128)S(1)}, f32[2,136,256]{2,1,0:T(8,128)S(1)}, u32[]{:S(2)}, u32[]{:S(2)}) collective-permute-start(f32[2,136,256]{2,1,0:T(8,128)S(1)} %add_up.42.refs_4_), channel_id=1, source_target_pairs={{0,8},{2,10},{4,12},{6,14},{8,0},{10,2},{12,4},{14,6},{16,24},{18,... | collective-permute-start | bytes 835592 | tf_op jit(solution)/shard_map/ppermute | solution.py:309
  145.7 8.6 %collective-permute-start.27 = (f32[2,144,256]{2,1,0:T(8,128)S(1)}, f32[2,144,256]{2,1,0:T(8,128)S(1)}, u32[]{:S(2)}, u32[]{:S(2)}) collective-permute-start(f32[2,144,256]{2,1,0:T(8,128)S(1)} %add_up.44.refs_4_), channel_id=1, source_target_pairs={{0,2},{2,0},{4,6},{6,4},{8,10},{10,8},{12,14},{14,12},{16,18},{18,... | collective-permute-start | bytes 884744 | tf_op jit(solution)/shard_map/ppermute | solution.py:309
  149.7 12.4 %collective-permute-start.30 = (f32[1,104,256]{2,1,0:T(8,128)S(1)}, f32[1,104,256]{2,1,0:T(8,128)S(1)}, u32[]{:S(2)}, u32[]{:S(2)}) collective-permute-start(f32[1,104,256]{2,1,0:T(8,128)S(1)} %add_up.45.refs_4_), channel_id=1, source_target_pairs={{0,16},{2,18},{4,20},{6,22},{8,24},{10,26},{12,28},{14,30},{16,0},... | collective-permute-start | bytes 319496 | tf_op jit(solution)/shard_map/ppermute | solution.py:309
  154.4 7.7 %collective-permute-start.29 = (f32[1,144,256]{2,1,0:T(8,128)S(1)}, f32[1,144,256]{2,1,0:T(8,128)S(1)}, u32[]{:S(2)}, u32[]{:S(2)}) collective-permute-start(f32[1,144,256]{2,1,0:T(8,128)S(1)} %add_up.46.refs_4_), channel_id=1, source_target_pairs={{0,16},{2,18},{4,20},{6,22},{8,24},{10,26},{12,28},{14,30},{16,0},... | collective-permute-start | bytes 442376 | tf_op jit(solution)/shard_map/ppermute | solution.py:309
  156.0 9.0 %collective-permute-start.32 = (f32[1,136,256]{2,1,0:T(8,128)S(1)}, f32[1,136,256]{2,1,0:T(8,128)S(1)}, u32[]{:S(2)}, u32[]{:S(2)}) collective-permute-start(f32[1,136,256]{2,1,0:T(8,128)S(1)} %add_up.47), channel_id=1, source_target_pairs={{0,16},{2,18},{4,20},{6,22},{8,24},{10,26},{12,28},{14,30},{16,0},... | collective-permute-start | bytes 417800 | tf_op jit(solution)/shard_map/ppermute | solution.py:309
  (1 other events, 4.9 us)
